TPU v7x, 128 devices: a whole 4x4x4 slice. The times are simulated.
128 devices in a mesh: dp: 2 (over core), row: 4 (over x), col: 16 (over z, y).
Axes of the slice: x: 4, y: 4, z: 4, core: 2. Of those that a mesh axis runs over, the one named last changes fastest.
Arguments:
- inputs: bfloat16 [768, 16384], P('col', ('dp', 'row')), may hold values from -6 to 6
- segments: int32 [2, 8192], P('dp'), may hold values from 0 to 4, as said below
- joint_weight: bfloat16 [768, 2304], P('col', 'row'), may hold values from -0.21875 to 0.21875
- joint_bias: float32 [1536], P('row'), may hold values from -1.8 to 1.8
- output_weight: bfloat16 [768, 768], P('row', 'col'), may hold values from -6 to 6
- output_bias: float32 [768], P('col'), may hold values from -1.8 to 1.8
- first_norm_gain: float32 [768], P('col'), may hold values from 0.5 to 1.5
- shift_first: float32 [768], P('col'), may hold values from -1.8 to 1.8
- up_weight: bfloat16 [768, 3072], P('col', 'row'), may hold values from -0.21875 to 0.21875
- up_bias: float32 [3072], P('row'), may hold values from -1.8 to 1.8
- down_weight: bfloat16 [768, 3072], P('col', 'row'), may hold values from -0.109375 to 0.109375
- down_bias: float32 [768], P('col'), may hold values from -1.8 to 1.8
- second_norm_gain: float32 [768], P('col'), may hold values from 0.5 to 1.5
- second_norm_shift: float32 [768], P('col'), may hold values from -1.8 to 1.8
- cotangent: bfloat16 [768, 16384], P('col', ('dp', 'row')), may hold values from -6 to 6
Outputs:
- layer_output: bfloat16 [768, 16384], P('col', ('dp', 'row'))
- grad_inputs: float32 [768, 16384], P('col', ('dp', 'row'))
- grad_joint_weight: float32 [768, 2304], P('col', 'row')
- grad_joint_bias: float32 [1536], P('row')
- grad_output_weight: float32 [768, 768], P('row', 'col')
- grad_output_bias: float32 [768], P('col')
- grad_gain_first: float32 [768], P('col')
- grad_shift_first: float32 [768], P('col')
- grad_up_weight: float32 [768, 3072], P('col', 'row')
- grad_up_bias: float32 [3072], P('row')
- grad_down_weight: float32 [768, 3072], P('col', 'row')
- grad_down_bias: float32 [768], P('col')
- grad_gain_second: float32 [768], P('col')
- grad_shift_second: float32 [768], P('col')
Inputs may be any that keep to these rules, and one draw needn't show every extreme that they name: `segments`: in every sequence the segment numbers start at 0, rise by 0 or 1 from one token to the next, and end at 4.
All inputs are finite; a program needn't handle non-finite values.
Results may differ from a plain program's by a relative error of at most 0.019.
Values may be sent and summed in bfloat16 or wider, within the bound.
No kernel may reach another device: no remote copies, remote signals or barrier semaphores. Data moves between devices by JAX's collectives and lax.ppermute only.
A program may use at most 128 MiB of HBM per device.

v0:
```python
import math

import jax
import jax.numpy as jnp
from jax import lax
from jax.sharding import PartitionSpec as P

HDIM = 64


epsilon = 1e-06
masked_score = -1e30


def joined_along(blocks, dim):
    dims = list(blocks.shape[1:])
    dims[dim] *= blocks.shape[0]
    return jnp.moveaxis(blocks, 0, dim).reshape(dims)


def from_everyone(shard, axis):
    peers = lax.axis_size(axis)
    return lax.all_to_all(
        jnp.broadcast_to(shard[None], (peers, *shard.shape)), axis, 0, 0, tiled=True
    )


def collect(shard, axis, dim):
    return joined_along(from_everyone(shard, axis), dim)


def over_copies(shard, axis):
    everything = from_everyone(shard, axis)
    return jnp.sum(everything, axis=0)


def in_one(arrays, axis):
    ends = [0]
    for a in arrays:
        ends.append(ends[-1] + a.size)
    subtotal = over_copies(jnp.concatenate([a.ravel() for a in arrays]), axis)
    return tuple((subtotal[b:e].reshape(a.shape) for a, b, e in zip(arrays, ends, ends[1:])))


def split_up(shard, dim, peers):
    before, after = (shard.shape[:dim], shard.shape[dim + 1 :])
    return jnp.moveaxis(shard.reshape(*before, peers, -1, *after), dim, 0)


def summed_on_arrival(shard, axis, dim):
    peers = lax.axis_size(axis)
    blocks = lax.all_to_all(split_up(shard, dim, peers), axis, 0, 0, tiled=True)
    return jnp.sum(blocks.astype(jnp.float32), axis=0)


def of_everyone(shard, axis):
    everything = from_everyone(shard, axis)
    return jnp.sum(everything.astype(jnp.float32), axis=0)


def gather_rows(operand):
    return collect(operand, "row", 0)


def gather_cols(operand):
    return lax.all_gather(operand, "col", axis=0, tiled=True)


def gather_keys(operand):
    return lax.all_gather(operand, "col", axis=0, tiled=True)


def feature_totals(former, latter):
    return in_one((former, latter), "col")


def product(operand, weight, flipped):
    if flipped:
        return lax.dot_general(
            operand, weight, (((1,), (1,)), ((), ())), preferred_element_type=jnp.float32
        )
    return jnp.dot(operand, weight, preferred_element_type=jnp.float32)


def across_cols(gathered, weight, flipped):
    full_rows = lax.all_to_all(gathered, "col", split_axis=0, concat_axis=1, tiled=True)
    upright = weight.T if flipped else weight
    return jnp.dot(full_rows, collect(upright, "col", 0), preferred_element_type=jnp.float32)


def across_rows(gathered, weight, flipped):
    return summed_on_arrival(product(gathered, weight, flipped).astype(jnp.bfloat16), "row", 0)


def weight_grad(operand, upstream):
    return lax.dot_general(
        operand, upstream, (((0,), (0,)), ((), ())), preferred_element_type=jnp.float32
    )


def layer_norm_apply(hidden, gain, shift):
    width = hidden.shape[1] * lax.axis_size("col")
    totals = feature_totals(jnp.sum(hidden, axis=1), jnp.sum(hidden * hidden, axis=1))
    centre = totals[0] / width
    spread = totals[1] / width - centre * centre
    inverse = lax.rsqrt(spread + epsilon)
    normed = (hidden - centre[:, None]) * inverse[:, None]
    return (normed * gain + shift, normed, inverse)


def norm_backward(upstream, normed, inverse, gain):
    width = upstream.shape[1] * lax.axis_size("col")
    scaled = upstream * gain
    totals = feature_totals(jnp.sum(scaled, axis=1), jnp.sum(scaled * normed, axis=1))
    result = inverse[:, None] * (
        scaled - totals[0][:, None] / width - normed * totals[1][:, None] / width
    )
    return (result, jnp.sum(upstream * normed, axis=0), jnp.sum(upstream, axis=0))


def block_scores(query_block, key_block, query_part, key_part, factor):
    scores = (
        jnp.einsum("qhd,khd->hqk", query_block, key_block, preferred_element_type=jnp.float32)
        * factor
    )
    allowed = query_part[:, None] == key_part[None, :]
    return (jnp.where(allowed[None], scores, masked_score), allowed)


def attend(queries, keys_values, query_segs, key_segs, factor):
    query_total, head_count, head_size = queries.shape
    seq_len = keys_values.shape[0]
    query_step = min(512, query_total)
    key_step = min(1024, seq_len)
    paired = keys_values.reshape(seq_len, head_count, 2, head_size)
    key_steps = jnp.arange(seq_len // key_step)

    def key_block_at(key_index):
        return (
            lax.dynamic_slice_in_dim(paired, key_index * key_step, key_step, 0),
            lax.dynamic_slice_in_dim(key_segs, key_index * key_step, key_step, 0),
        )

    def one_block(block_index):

        def first_pass(carry, key_index):
            highest, totals = carry
            key_block, key_part = key_block_at(key_index)
            scores, allowed = block_scores(
                queries, key_block[:, :, 0], query_segs, key_part, factor
            )
            raised = jnp.maximum(highest, jnp.max(scores, axis=2))
            weights = jnp.where(allowed[None], jnp.exp(scores - raised[:, :, None]), 0.0)
            return ((raised, totals * jnp.exp(highest - raised) + jnp.sum(weights, axis=2)), None)

        start_carry = (
            jnp.full((head_count, query_step), masked_score, jnp.float32),
            jnp.zeros((head_count, query_step), jnp.float32),
        )
        (highest, totals), unused = lax.scan(first_pass, start_carry, key_steps)
        log_total = highest + jnp.log(totals)

        def second_pass(summed, key_index):
            key_block, key_part = key_block_at(key_index)
            scores, allowed = block_scores(
                queries, key_block[:, :, 0], query_segs, key_part, factor
            )
            probs = jnp.where(allowed[None], jnp.exp(scores - log_total[:, :, None]), 0.0)
            update = jnp.einsum(
                "hqk,khd->qhd",
                probs.astype(jnp.bfloat16),
                key_block[:, :, 1],
                preferred_element_type=jnp.float32,
            )
            return (summed + update, None)

        summed, unused = lax.scan(
            second_pass, jnp.zeros((query_step, head_count, head_size), jnp.float32), key_steps
        )
        return (summed, log_total)

    results, log_totals = lax.map(one_block, jnp.arange(query_total // query_step))
    return (results.reshape(query_total, head_count * head_size), log_totals)


def attend_back(queries, keys_values, grad_out, log_totals, query_segs, key_segs, factor):
    query_total, head_count, head_size = queries.shape
    seq_len = keys_values.shape[0]
    query_step = min(512, query_total)
    key_step = min(1024, seq_len)
    paired = keys_values.reshape(seq_len, head_count, 2, head_size)
    key_steps = jnp.arange(seq_len // key_step)

    def key_block_at(key_index):
        return (
            lax.dynamic_slice_in_dim(paired, key_index * key_step, key_step, 0),
            lax.dynamic_slice_in_dim(key_segs, key_index * key_step, key_step, 0),
        )

    def one_block(block_index, carry):
        grad_queries, grad_keys = carry
        log_total = log_totals[block_index]

        def recompute(key_index):
            key_block, key_part = key_block_at(key_index)
            scores, allowed = block_scores(
                queries, key_block[:, :, 0], query_segs, key_part, factor
            )
            probs = jnp.where(allowed[None], jnp.exp(scores - log_total[:, :, None]), 0.0)
            grad_probs = jnp.einsum(
                "qhd,khd->hqk", grad_out, key_block[:, :, 1], preferred_element_type=jnp.float32
            )
            return (key_block, probs, grad_probs)

        def first_pass(delta_sum, key_index):
            key_block, probs, grad_probs = recompute(key_index)
            return (delta_sum + jnp.sum(probs * grad_probs, axis=2), None)

        delta, unused = lax.scan(
            first_pass, jnp.zeros((head_count, query_step), jnp.float32), key_steps
        )

        def second_pass(inner, key_index):
            grad_block_q, keys_grad = inner
            key_block, probs, grad_probs = recompute(key_index)
            grad_scores = (probs * (grad_probs - delta[:, :, None])).astype(jnp.bfloat16)
            grad_values = jnp.einsum(
                "hqk,qhd->khd",
                probs.astype(jnp.bfloat16),
                grad_out,
                preferred_element_type=jnp.float32,
            )
            grad_key_part = (
                jnp.einsum("hqk,qhd->khd", grad_scores, queries, preferred_element_type=jnp.float32)
                * factor
            )
            grad_block_q = (
                grad_block_q
                + jnp.einsum(
                    "hqk,khd->qhd",
                    grad_scores,
                    key_block[:, :, 0],
                    preferred_element_type=jnp.float32,
                )
                * factor
            )
            stacked = jnp.stack([grad_key_part, grad_values], axis=2)
            previous = lax.dynamic_slice_in_dim(keys_grad, key_index * key_step, key_step, 0)
            keys_grad = lax.dynamic_update_slice_in_dim(
                keys_grad, previous + stacked, key_index * key_step, 0
            )
            return ((grad_block_q, keys_grad), None)

        start_inner = (jnp.zeros((query_step, head_count, head_size), jnp.float32), grad_keys)
        (grad_block_q, grad_keys), unused = lax.scan(second_pass, start_inner, key_steps)
        grad_queries = grad_block_q
        return (grad_queries, grad_keys)

    start_carry = (
        jnp.zeros((query_total, head_count, head_size), jnp.float32),
        jnp.zeros((seq_len, head_count, 2, head_size), jnp.float32),
    )
    grad_queries, grad_keys = lax.fori_loop(0, query_total // query_step, one_block, start_carry)
    return (grad_queries, grad_keys.reshape(seq_len, head_count * 2 * head_size))


def per_device(
    inputs,
    segments,
    joint_weight,
    joint_bias,
    output_weight,
    output_bias,
    first_norm_gain,
    shift_first,
    up_weight,
    up_bias,
    down_weight,
    down_bias,
    second_norm_gain,
    second_norm_shift,
    cotangent,
):
    token_rows = inputs.T
    row_tokens = token_rows.shape[0]
    seq_len = row_tokens * lax.axis_size("row")
    query_total = seq_len // lax.axis_size("col")
    head_count = joint_bias.shape[0] // (2 * HDIM)
    factor = 1.0 / math.sqrt(HDIM)
    key_segs = segments[0]
    query_segs = lax.dynamic_slice_in_dim(
        key_segs, lax.axis_index("col") * query_total, query_total, 0
    )
    bias_pairs = joint_bias.reshape(head_count, 2, HDIM)
    bias_full = jnp.stack(
        [bias_pairs[:, 0], jnp.zeros_like(bias_pairs[:, 0]), bias_pairs[:, 1]], axis=1
    ).reshape(-1)
    gathered_inputs = gather_rows(token_rows)
    proj_low = (across_cols(gathered_inputs, joint_weight, False) + bias_full).astype(jnp.bfloat16)
    parts = proj_low.reshape(query_total, head_count, 3, HDIM)
    query_heads = parts[:, :, 0]
    local_keys = parts[:, :, 1:].reshape(query_total, head_count * 2 * HDIM)
    gathered_keys = gather_keys(local_keys)
    attended, log_totals = attend(query_heads, gathered_keys, query_segs, key_segs, factor)
    attended_low = attended.astype(jnp.bfloat16)
    gathered_attended = gather_cols(attended_low)
    attn = across_rows(gathered_attended, output_weight, False) + output_bias
    first_normalized, first_centered_scaled, first_inverse_deviation = layer_norm_apply(
        token_rows.astype(jnp.float32) + attn, first_norm_gain, shift_first
    )
    normed_low = first_normalized.astype(jnp.bfloat16)
    gathered_normed = gather_rows(normed_low)
    pre_act = across_cols(gathered_normed, up_weight, False) + up_bias
    activ_low = jax.nn.gelu(pre_act, approximate=False).astype(jnp.bfloat16)
    gathered_activ = gather_cols(activ_low)
    second_branch_output = across_rows(gathered_activ, down_weight, True) + down_bias
    encoder_result, second_centered_scaled, second_inverse_deviation = layer_norm_apply(
        first_normalized + second_branch_output, second_norm_gain, second_norm_shift
    )
    layer_output = encoder_result.T.astype(jnp.bfloat16)
    grad_second_hidden, grad_gain_second, grad_shift_second = norm_backward(
        cotangent.T.astype(jnp.float32),
        second_centered_scaled,
        second_inverse_deviation,
        second_norm_gain,
    )
    gathered_branch = gather_rows(grad_second_hidden.astype(jnp.bfloat16))
    d_activ = across_cols(gathered_branch, down_weight, False)
    activ_again = gather_cols(activ_low)
    grad_down_weight = weight_grad(gathered_branch, activ_again)
    grad_down_bias = jnp.sum(gathered_branch, axis=0, dtype=jnp.float32)
    unused_value, gelu_back = jax.vjp(
        lambda pre_value: jax.nn.gelu(pre_value, approximate=False), pre_act
    )
    d_pre_low = gelu_back(d_activ)[0].astype(jnp.bfloat16)
    gathered_pre = gather_cols(d_pre_low)
    grad_normalized_piece = across_rows(gathered_pre, up_weight, True)
    normed_again = gather_rows(normed_low)
    grad_up_weight = weight_grad(normed_again, gathered_pre)
    grad_up_bias = jnp.sum(gathered_pre, axis=0, dtype=jnp.float32)
    d_hidden_one, grad_gain_first, grad_shift_first = norm_backward(
        grad_second_hidden + grad_normalized_piece,
        first_centered_scaled,
        first_inverse_deviation,
        first_norm_gain,
    )
    gathered_attn = gather_rows(d_hidden_one.astype(jnp.bfloat16))
    d_attended = across_cols(gathered_attn, output_weight, True)
    attended_again = gather_cols(attended_low)
    grad_output_weight = weight_grad(attended_again, gathered_attn)
    grad_output_bias = jnp.sum(gathered_attn, axis=0, dtype=jnp.float32)
    d_attended_low = d_attended.astype(jnp.bfloat16).reshape(query_total, head_count, HDIM)
    keys_again = gather_keys(local_keys)
    grad_queries, grad_keys_all = attend_back(
        query_heads, keys_again, d_attended_low, log_totals, query_segs, key_segs, factor
    )
    grad_keys_local = lax.psum_scatter(
        grad_keys_all.astype(jnp.bfloat16), "col", scatter_dimension=0, tiled=True
    ).astype(jnp.float32)
    d_proj = (
        jnp.concatenate(
            [grad_queries[:, :, None], grad_keys_local.reshape(query_total, head_count, 2, HDIM)],
            axis=2,
        )
        .reshape(query_total, head_count * 3 * HDIM)
        .astype(jnp.bfloat16)
    )
    gathered_proj = gather_cols(d_proj)
    d_inputs_part = across_rows(gathered_proj, joint_weight, True)
    inputs_again = gather_rows(token_rows)
    grad_joint_weight = weight_grad(inputs_again, gathered_proj)
    column_sums = jnp.sum(gathered_proj, axis=0, dtype=jnp.float32).reshape(head_count, 3, HDIM)
    grad_joint_bias = jnp.stack([column_sums[:, 0], column_sums[:, 2]], axis=1).reshape(-1)
    grad_inputs = (d_hidden_one + d_inputs_part).T
    summed = (
        of_everyone(grad_joint_weight.astype(jnp.bfloat16), "dp").astype(jnp.float32),
        of_everyone(grad_joint_bias.astype(jnp.bfloat16), "dp").astype(jnp.float32),
        of_everyone(grad_output_weight.astype(jnp.bfloat16), "dp").astype(jnp.float32),
        of_everyone(grad_output_bias.astype(jnp.bfloat16), "dp").astype(jnp.float32),
        of_everyone(grad_up_weight.astype(jnp.bfloat16), "dp").astype(jnp.float32),
        of_everyone(grad_up_bias.astype(jnp.bfloat16), "dp").astype(jnp.float32),
        of_everyone(grad_down_weight.astype(jnp.bfloat16), "dp").astype(jnp.float32),
        of_everyone(grad_down_bias.astype(jnp.bfloat16), "dp").astype(jnp.float32),
    )
    norm_grads = in_one(
        (grad_gain_first, grad_shift_first, grad_gain_second, grad_shift_second), ("dp", "row")
    )
    return (
        layer_output,
        grad_inputs,
        summed[0],
        summed[1],
        summed[2],
        summed[3],
        norm_grads[0],
        norm_grads[1],
        summed[4],
        summed[5],
        summed[6],
        summed[7],
        norm_grads[2],
        norm_grads[3],
    )


def solution(mesh):
    return jax.shard_map(
        per_device,
        mesh=mesh,
        in_specs=(
            P("col", ("dp", "row")),
            P("dp", None),
            P("col", "row"),
            P("row"),
            P("row", "col"),
            P("col"),
            P("col"),
            P("col"),
            P("col", "row"),
            P("row"),
            P("col", "row"),
            P("col"),
            P("col"),
            P("col"),
            P("col", ("dp", "row")),
        ),
        out_specs=(
            P("col", ("dp", "row")),
            P("col", ("dp", "row")),
            P("col", "row"),
            P("row"),
            P("row", "col"),
            P("col"),
            P("col"),
            P("col"),
            P("col", "row"),
            P("row"),
            P("col", "row"),
            P("col"),
            P("col"),
            P("col"),
        ),
        check_vma=False,
    )
```

profile of v0, /device:TPU:1, one launch (start us, length us, event | category | flops | bytes accessed | tf_op | source)
XLA Modules:
  0.0 1182.1 jit_solution(9950273943247379723)
XLA Ops:
  8.2 16.0 %all_to_all.200 = bf16[4,2048,48]{1,2,0:T(8,128)(2,1)S(1)} all-to-all(bf16[4,2048,48]{1,2,0:T(8,128)(2,1)S(1)} %broadcast_in_dim.132), channel_id=1, replica_groups=mesh['dp'=2,'row'=4,'col'=16] {'row'}, dimensions={0} | all-to-all | bytes 1572864 | tf_op jit(solution)/shard_map/all_to_all | solution.py:23
  25.4 7.8 all-to-all-start.2
  35.6 11.9 %all-to-all-done.2 = bf16[16,48,576]{2,1,0:T(8,128)(2,1)S(1)} async-done(((bf16[16,48,576]{2,1,0:T(8,128)(2,1)}), bf16[16,48,576]{2,1,0:T(8,128)(2,1)S(1)}, u32[]{:S(2)}, u32[]{:S(2)}) %all-to-all-start.2) | async-done | bytes 884768 | tf_op jit(solution)/shard_map/all_to_all | solution.py:23
  52.0 11.4 all-to-all-done.1
  65.7 65.1 %all-gather.6.cloned.1.call-done = bf16[8192,384]{0,1:T(8,128)(2,1)} async-done(((bf16[512,384]{0,1:T(8,128)(2,1)}), bf16[8192,384]{0,1:T(8,128)(2,1)}) %all-gather.6.cloned.1.call-update) | async-done | bytes 6291472 | tf_op jit(solution)/shard_map/all_gather | solution.py:70
  136.9 50.6 %while.73 = (s32[]{:T(128)}, f32[3,512]{1,0:T(4,128)S(1)}, f32[3,512]{1,0:T(4,128)S(1)}, s32[512]{0:T(512)S(1)}, s32[8]{0:T(128)S(1)}, /*index=5*/s32[8192]{0:T(...) while((s32[]{:T(128)}, f32[3,512]{1,0:T(4,128)S(1)}, ...), condition=%wide.region_3.0_spmd.clone, body=%wide.region_0.3_spmd.clone.sunk | while | flops 214441472 | bytes 14840010 | solution.py:160
  187.6 48.6 %while.74 = (s32[]{:T(128)}, f32[512,3,64]{0,2,1:T(8,128)S(1)}, s32[8]{0:T(128)S(1)}, bf16[8192,3,2,64]{0,3,1,2:T(8,128)(2,1)}, s32[512]{0:T(512)S(1)}, /*index=...) while((s32[]{:T(128)}, f32[512,3,64]{0,2,1:T(8,128)S(1)}, ...), condition=%wide.region_5.6_spmd.clone, body=%wide.region_4.5_spmd.clone.sunk | while | flops 411238400 | bytes 2840792 | solution.py:177
  237.0 52.1 %all-gather.8.cloned.1.call-done = bf16[8192,192]{0,1:T(8,128)(2,1)} async-done(((bf16[512,192]{0,1:T(8,128)(2,1)}), bf16[8192,192]{0,1:T(8,128)(2,1)}) %all-gather.8.cloned.1.call-update) | async-done | bytes 3145744 | tf_op jit(solution)/shard_map/all_gather | solution.py:66
  291.8 14.4 %all_to_all.201 = bf16[4,2048,48]{1,2,0:T(8,128)(2,1)S(1)} all-to-all(bf16[4,2048,48]{1,2,0:T(8,128)(2,1)S(1)} %bitcast.365), channel_id=1, replica_groups=mesh['dp'=2,'row'=4,'col'=16] {'row'}, dimensions={0} | all-to-all | bytes 1572864 | tf_op jit(solution)/shard_map/all_to_all | solution.py:52
  307.5 12.0 %all_to_all.202 = f32[16,1,4096]{2,1,0:T(1,128)S(1)} all-to-all(f32[16,1,4096]{2,1,0:T(1,128)S(1)} %broadcast_in_dim.134), channel_id=1, replica_groups=mesh['dp'=2,'row'=4,'col'=16] {'col'}, dimensions={0} | all-to-all | bytes 524288 | tf_op jit(solution)/shard_map/all_to_all | solution.py:23
  320.4 10.7 all_to_all.203
  338.6 12.9 %all-to-all-done.7 = bf16[16,48,768]{2,1,0:T(8,128)(2,1)} async-done(((bf16[16,48,768]{2,1,0:T(8,128)(2,1)}), bf16[16,48,768]{2,1,0:T(8,128)(2,1)}, u32[]{:S(2)}, u32[]{:S(2)}) %all-to-all-start.7) | async-done | bytes 1179680 | tf_op jit(solution)/shard_map/all_to_all | solution.py:23
  351.5 13.7 %all_to_all.204 = bf16[16,512,48]{1,2,0:T(8,128)(2,1)S(1)} all-to-all(bf16[16,512,48]{1,2,0:T(8,128)(2,1)S(1)} %copy.176), channel_id=1, replica_groups=mesh['dp'=2,'row'=4,'col'=16] {'col'}, dimensions={0} | all-to-all | bytes 1572864 | tf_op jit(solution)/shard_map/all_to_all | solution.py:86
  372.0 91.8 %all-gather.10.cloned.1.call-done = bf16[8192,768]{1,0:T(8,128)(2,1)} async-done(((bf16[512,768]{1,0:T(8,128)(2,1)}), bf16[8192,768]{1,0:T(8,128)(2,1)}) %all-gather.10.cloned.1.call-update) | async-done | bytes 12582928 | tf_op jit(solution)/shard_map/all_gather | solution.py:66
  463.8 8.3 convolution_convert_fusion.3
  472.2 15.3 %all_to_all.205 = bf16[4,2048,48]{1,2,0:T(8,128)(2,1)S(1)} all-to-all(bf16[4,2048,48]{1,2,0:T(8,128)(2,1)S(1)} %bitcast.366), channel_id=1, replica_groups=mesh['dp'=2,'row'=4,'col'=16] {'row'}, dimensions={0} | all-to-all | bytes 1572864 | tf_op jit(solution)/shard_map/all_to_all | solution.py:52
  488.1 12.4 %all_to_all.206 = f32[16,1,4096]{2,1,0:T(1,128)S(1)} all-to-all(f32[16,1,4096]{2,1,0:T(1,128)S(1)} %broadcast_in_dim.137), channel_id=1, replica_groups=mesh['dp'=2,'row'=4,'col'=16] {'col'}, dimensions={0} | all-to-all | bytes 524288 | tf_op jit(solution)/shard_map/all_to_all | solution.py:23
  501.6 10.5 all_to_all.207
  512.5 10.7 all_to_all.208
  532.4 10.9 all-to-all-done.13
  543.4 14.3 %all_to_all.209 = bf16[16,512,48]{1,2,0:T(8,128)(2,1)S(1)} all-to-all(bf16[16,512,48]{1,2,0:T(8,128)(2,1)S(1)} %copy.181), channel_id=1, replica_groups=mesh['dp'=2,'row'=4,'col'=16] {'col'}, dimensions={0} | all-to-all | bytes 1572864 | tf_op jit(solution)/shard_map/all_to_all | solution.py:86
  561.6 91.8 %all-gather.12.cloned.1.call-done = bf16[8192,768]{1,0:T(8,128)(2,1)} async-done(((bf16[512,768]{1,0:T(8,128)(2,1)}), bf16[8192,768]{1,0:T(8,128)(2,1)}) %all-gather.12.cloned.1.call-update) | async-done | bytes 12582928 | tf_op jit(solution)/shard_map/all_gather | solution.py:66
  653.4 8.3 convolution_convert_fusion.2
  661.9 15.3 %all_to_all.210 = bf16[4,2048,48]{1,2,0:T(8,128)(2,1)S(1)} all-to-all(bf16[4,2048,48]{1,2,0:T(8,128)(2,1)S(1)} %bitcast.367), channel_id=1, replica_groups=mesh['dp'=2,'row'=4,'col'=16] {'row'}, dimensions={0} | all-to-all | bytes 1572864 | tf_op jit(solution)/shard_map/all_to_all | solution.py:52
  678.5 12.4 %all_to_all.211 = f32[16,1,4096]{2,1,0:T(1,128)S(1)} all-to-all(f32[16,1,4096]{2,1,0:T(1,128)S(1)} %broadcast_in_dim.141), channel_id=1, replica_groups=mesh['dp'=2,'row'=4,'col'=16] {'col'}, dimensions={0} | all-to-all | bytes 524288 | tf_op jit(solution)/shard_map/all_to_all | solution.py:23
  691.9 11.4 all_to_all.212
  719.8 10.3 all-to-all-done.17
  732.1 61.4 %while.75 = (s32[]{:T(128)}, f32[3,512]{1,0:T(4,128)S(1)}, s32[512]{0:T(512)S(1)}, s32[8]{0:T(128)S(1)}, s32[8192]{0:T(1024)}, /*index=5*/bf16[8192,3,2,64]{0,3,...) while((s32[]{:T(128)}, f32[3,512]{1,0:T(4,128)S(1)}, ...), condition=%wide.region_23.24_spmd.clone, body=%wide.region_21.23_spmd.clone.sunk | while | flops 412616192 | bytes 15642889 | solution.py:219
  799.6 128.5 %while.76 = (s32[]{:T(128)}, f32[512,3,64]{0,2,1:T(8,128)S(1)}, f32[8192,3,2,64]{0,3,2,1:T(8,128)}, s32[8]{0:T(128)S(1)}, bf16[8192,3,2,64]{0,3,1,2:T(8,128)(2,1...) while((s32[]{:T(128)}, f32[512,3,64]{0,2,1:T(8,128)S(1)}, ...), condition=%wide.region_25.26_spmd.clone, body=%wide.region_24.25_spmd.clone.sunk | while | flops 1027309568 | bytes 42107144 | solution.py:255
  928.1 8.1 convert_element_type.168
  936.6 81.8 %reduce-scatter.2.cloned.1.call-done = bf16[512,384]{0,1:T(8,128)(2,1)} async-done(((bf16[8192,384]{0,1:T(8,128)(2,1)}), bf16[512,384]{0,1:T(8,128)(2,1)}) %reduce-scatter.2.cloned.1.call-update) | async-done | bytes 393232 | tf_op jit(solution)/shard_map/reduce_scatter | solution.py:357
  1060.9 42.8 %all-gather.14.cloned.1.call-done = bf16[8192,576]{0,1:T(8,128)(2,1)} async-done(((bf16[512,576]{0,1:T(8,128)(2,1)}), bf16[8192,576]{0,1:T(8,128)(2,1)}) %all-gather.14.cloned.1.call-update) | async-done | bytes 9437200 | tf_op jit(solution)/shard_map/all_gather | solution.py:66
  (537 shorter events, 459.5 us)
Async XLA Ops:
  7.2 17.1 %copy-start.19 = (bf16[48,576]{1,0:T(8,128)(2,1)S(1)}, bf16[48,576]{1,0:T(8,128)(2,1)}, u32[]{:S(2)}) copy-start(bf16[48,576]{1,0:T(8,128)(2,1)} %param.25) | copy-start | bytes 165892
  25.4 22.1 %all-to-all-start.2 = ((bf16[16,48,576]{2,1,0:T(8,128)(2,1)}), bf16[16,48,576]{2,1,0:T(8,128)(2,1)S(1)}, u32[]{:S(2)}, u32[]{:S(2)}) async-start(bf16[16,48,576]{2,1,0:T(8,128)(2,1)} %broadcast_in_dim.133), calls=%async_computation.2 | async-start | bytes 1966080 | tf_op jit(solution)/shard_map/all_to_all | solution.py:23
  34.3 17.4 %copy-start.66 = (f32[384]{0:T(512)S(1)}, f32[384]{0:T(512)}, u32[]{:S(2)}) copy-start(f32[384]{0:T(512)} %param.26) | copy-start | bytes 4612
  47.5 15.9 %all-to-all-start.1 = ((bf16[16,512,48]{1,2,0:T(8,128)(2,1)}), bf16[16,512,48]{1,2,0:T(8,128)(2,1)S(1)}, u32[]{:S(2)}, u32[]{:S(2)}) async-start(bf16[16,512,48]{1,2,0:T(8,128)(2,1)} %copy.169), calls=%async_computation.1 | async-start | bytes 1572864 | tf_op jit(solution)/shard_map/all_to_all | solution.py:86
  51.7 79.2 %all-gather.6.cloned.1.call-start = ((), (), s32[]{:S(2)}) async-start(), calls=%async_computation.30 | async-start | bytes 6684672 | tf_op jit(solution)/shard_map/all_gather | solution.py:70
  64.9 224.3 %all-gather.8.cloned.1.call-start = ((), (), s32[]{:S(2)}) async-start(), calls=%async_computation.31 | async-start | bytes 3342336 | tf_op jit(solution)/shard_map/all_gather | solution.py:66
  187.6 101.5 %copy-start.41 = (bf16[192,48]{0,1:T(8,128)(2,1)S(1)}, bf16[192,48]{0,1:T(8,128)(2,1)}, u32[]{:S(2)}) copy-start(bf16[192,48]{0,1:T(8,128)(2,1)} %param.27) | copy-start | bytes 55300
  236.3 55.4 %copy-start.55 = (f32[3,512]{1,0:T(4,128)}, f32[3,512]{1,0:T(4,128)S(1)}, u32[]{:S(2)}) copy-start(f32[3,512]{1,0:T(4,128)S(1)} %get-tuple-element.1154) | copy-start | bytes 18436
  332.4 19.2 %all-to-all-start.7 = ((bf16[16,48,768]{2,1,0:T(8,128)(2,1)}), bf16[16,48,768]{2,1,0:T(8,128)(2,1)}, u32[]{:S(2)}, u32[]{:S(2)}) async-start(bf16[16,48,768]{2,1,0:T(8,128)(2,1)} %broadcast_in_dim.136), calls=%async_computation.7 | async-start | bytes 2359296 | tf_op jit(solution)/shard_map/all_to_all | solution.py:23
  337.0 126.8 %all-gather.10.cloned.1.call-start = ((), (), s32[]{:S(2)}) async-start(), calls=%async_computation.32 | async-start | bytes 13369344 | tf_op jit(solution)/shard_map/all_gather | solution.py:66
  338.1 27.1 %copy-start.69 = (f32[768]{0:T(1024)S(1)}, f32[768]{0:T(1024)}, u32[]{:S(2)}) copy-start(f32[768]{0:T(1024)} %param.32) | copy-start | bytes 9220
  365.2 98.6 %copy-start.29 = (bf16[48,768]{1,0:T(8,128)(2,1)S(1)}, bf16[48,768]{1,0:T(8,128)(2,1)}, u32[]{:S(2)}) copy-start(bf16[48,768]{1,0:T(8,128)(2,1)} %param.33) | copy-start | bytes 221188
  524.4 19.0 %all-to-all-start.13 = ((bf16[16,48,768]{2,1,0:T(8,128)(2,1)}), bf16[16,48,768]{2,1,0:T(8,128)(2,1)}, u32[]{:S(2)}, u32[]{:S(2)}) async-start(bf16[16,48,768]{2,1,0:T(8,128)(2,1)} %broadcast_in_dim.140), calls=%async_computation.13 | async-start | bytes 2359296 | tf_op jit(solution)/shard_map/all_to_all | solution.py:23
  528.8 124.6 %all-gather.12.cloned.1.call-start = ((), (), s32[]{:S(2)}) async-start(), calls=%async_computation.33 | async-start | bytes 13369344 | tf_op jit(solution)/shard_map/all_gather | solution.py:66
  557.6 95.8 %copy-start.31 = (bf16[48,768]{1,0:T(8,128)(2,1)S(1)}, bf16[48,768]{1,0:T(8,128)(2,1)}, u32[]{:S(2)}) copy-start(bf16[48,768]{1,0:T(8,128)(2,1)} %param.31) | copy-start | bytes 221188
  704.1 11.8 all-to-all-start.18
  712.5 19.6 %copy-start.56 = (f32[3,512]{1,0:T(4,128)S(1)}, f32[3,512]{1,0:T(4,128)}, u32[]{:S(2)}) copy-start(f32[3,512]{1,0:T(4,128)} %copy-done.55) | copy-start | bytes 18436
  715.9 14.1 %all-to-all-start.17 = ((bf16[16,512,48]{1,2,0:T(8,128)(2,1)}), bf16[16,512,48]{1,2,0:T(8,128)(2,1)S(1)}, u32[]{:S(2)}, u32[]{:S(2)}) async-start(bf16[16,512,48]{1,2,0:T(8,128)(2,1)} %copy.185), calls=%async_computation.17 | async-start | bytes 1572864 | tf_op jit(solution)/shard_map/all_to_all | solution.py:86
  719.5 298.8 %reduce-scatter.2.cloned.1.call-start = ((), (), s32[]{:S(2)}) async-start(), calls=%async_computation.34 | async-start | bytes 6684672 | tf_op jit(solution)/shard_map/reduce_scatter | solution.py:357
  936.2 84.0 %copy-start.1 = (bf16[4,2048,48]{1,2,0:T(8,128)(2,1)S(1)}, bf16[4,2048,48]{1,2,0:T(8,128)(2,1)}, u32[]{:S(2)}) copy-start(bf16[4,2048,48]{1,2,0:T(8,128)(2,1)} %copy-done) | copy-start | bytes 2359300
  936.3 167.4 %all-gather.14.cloned.1.call-start = ((), (), s32[]{:S(2)}) async-start(), calls=%async_computation.35 | async-start | bytes 10027008 | tf_op jit(solution)/shard_map/all_gather | solution.py:66
  1031.2 6.3 all-to-all-start.27
  1038.0 84.7 %all-to-all-start.28 = ((bf16[2,1,48]{2,1,0:T(2,128)(2,1)}), bf16[2,1,48]{2,1,0:T(2,128)(2,1)S(1)}, u32[]{:S(2)}, u32[]{:S(2)}) async-start(bf16[2,1,48]{2,1,0:T(2,128)(2,1)} %broadcast_in_dim.154), calls=%async_computation.29 | async-start | bytes 2048 | tf_op jit(solution)/shard_map/all_to_all | solution.py:23
  1057.7 46.0 %copy-start.20 = (bf16[48,576]{1,0:T(8,128)(2,1)S(1)}, bf16[48,576]{1,0:T(8,128)(2,1)}, u32[]{:S(2)}) copy-start(bf16[48,576]{1,0:T(8,128)(2,1)} %param.25) | copy-start | bytes 165892
  1122.7 23.6 %copy-start.67 = (bf16[2,1,48]{2,1,0:T(2,128)(2,1)}, bf16[2,1,48]{2,1,0:T(2,128)(2,1)S(1)}, u32[]{:S(2)}) copy-start(bf16[2,1,48]{2,1,0:T(2,128)(2,1)S(1)} %all-to-all-done.28) | copy-start | bytes 580
  1146.4 16.1 %copy-start.24 = (f32[2048]{0:T(1024)S(1)}, f32[2048]{0:T(1024)}, u32[]{:S(2)}) copy-start(f32[2048]{0:T(1024)} %copy-done.21) | copy-start | bytes 24580
  1146.4 16.1 %copy-start.28 = (f32[2048]{0:T(1024)S(1)}, f32[2048]{0:T(1024)}, u32[]{:S(2)}) copy-start(f32[2048]{0:T(1024)} %copy-done.25) | copy-start | bytes 24580
  1146.4 16.1 %copy-start.37 = (f32[2048]{0:T(1024)S(1)}, f32[2048]{0:T(1024)}, u32[]{:S(2)}) copy-start(f32[2048]{0:T(1024)} %copy-done.35) | copy-start | bytes 24580
  1146.4 16.1 %copy-start.40 = (f32[2048]{0:T(1024)S(1)}, f32[2048]{0:T(1024)}, u32[]{:S(2)}) copy-start(f32[2048]{0:T(1024)} %copy-done.38) | copy-start | bytes 24580
  1146.4 16.1 %copy-start.44 = (f32[2048]{0:T(1024)S(1)}, f32[2048]{0:T(1024)}, u32[]{:S(2)}) copy-start(f32[2048]{0:T(1024)} %copy-done.43) | copy-start | bytes 24580
  1146.5 15.8 %all-to-all-start.19 = ((bf16[4,2048,48]{1,2,0:T(8,128)(2,1)}), bf16[4,2048,48]{1,2,0:T(8,128)(2,1)S(1)}, u32[]{:S(2)}, u32[]{:S(2)}) async-start(bf16[4,2048,48]{1,2,0:T(8,128)(2,1)} %bitcast.277), calls=%async_computation.20 | async-start | bytes 1572864 | tf_op jit(solution)/shard_map/all_to_all | solution.py:52
  1164.7 9.6 all-to-all-start.24
  (62 other events, 559.3 us)
Sparse Core Ops, SparseCore 0:
  65.0 65.7 all-gather.5
  237.2 51.9 all-gather.7
  372.1 91.6 all-gather.9
  561.7 91.6 all-gather.11
  936.4 81.9 reduce-scatter.1
  1020.4 83.2 all-gather.13
where the time goes:
time: 1200 us; the launch traced here: 1180 us
  waiting for transfers between devices  499 us (42%)
  matrix products  239 us (20%)
  blocking collectives  193 us (16%)
  local copies, waits for them, and re-layouts  94.6 us (8%)
  other arithmetic  73 us (6%)
  starting transfers between devices  46.2 us (4%)
  loops' own time  22.4 us (2%)
  between operations  15.8 us (1%)
    all_gather x4, waiting for transfers between devices, gather_cols(): return lax.all_gather(operand, 'col', axis=0, tiled=True)  279 us
    all_to_all x14, blocking collectives, from_everyone(): lax.all_to_all(jnp.broadcast_to(shard[None], (peers, *shard.shape)), axis...  120 us
    reduce_scatter x1, waiting for transfers between devices, per_device(): lax.psum_scatter(grad_keys_all.astype(jnp.bfloat16), 'col', scatter_dimen...  81.8 us
    all_gather x1, waiting for transfers between devices, gather_keys(): return lax.all_gather(operand, 'col', axis=0, tiled=True)  65.1 us
    dot_general x16, matrix products, recompute(): jnp.einsum('qhd,khd->hqk', grad_out, key_block[:, :, 1], preferred_elemen...  55.4 us
    dot_general x24, matrix products, block_scores(): jnp.einsum('qhd,khd->hqk', query_block, key_block, preferred_element_type...  51.7 us
    all_to_all x3, blocking collectives, summed_on_arrival(): blocks = lax.all_to_all(split_up(shard, dim, peers), axis, 0, 0, tiled=True)  44.9 us
    all_to_all x7, waiting for transfers between devices, from_everyone(): lax.all_to_all(jnp.broadcast_to(shard[None], (peers, *shard.shape)), axis...  44.3 us
  transfers between devices with their start and end apart: 16, of which 15 were waited for; matrix products, arithmetic and copies ran while one was open for 5% of the time, Pallas kernels for 0%

commit v1 on v0

v1 whole, which is shorter than its diff:
```python
import functools
import math

import jax
import jax.numpy as jnp
from jax import lax
from jax.experimental import pallas as pl
from jax.experimental.pallas import tpu as pltpu
from jax.sharding import PartitionSpec as P

HDIM = 64
EPS = 1e-06
BLOCK_OUT = -1e30
LOG2E = 1.4426950408889634
LN2 = 0.6931471805599453
BF = jnp.bfloat16
F32 = jnp.float32

DIM = 768
NCOL = 16
NROW = 4
TOK = 128
PER_HEAD = 5
SHARE = 104
ROWS = NCOL * SHARE
KEYS = 8192
AUG = 144


def split3(v):
    hi = v.astype(BF)
    rest = v - hi.astype(F32)
    mid = rest.astype(BF)
    low = (rest - mid.astype(F32)).astype(BF)
    return hi, mid, low


def dot(a, b, ca, cb):
    return lax.dot_general(a, b, (((ca,), (cb,)), ((), ())), preferred_element_type=F32)


def gelu_parts(x):
    phi = 0.5 * (1.0 + lax.erf(x * (1.0 / math.sqrt(2.0))))
    return phi


def key_rows(seg_row):
    width = seg_row.shape[1]
    row = lax.broadcasted_iota(jnp.int32, (16, width), 0)
    hot = jnp.where(row < 5, jnp.where(row == seg_row, 1.0, 0.0), jnp.where(row < 8, 1.0, 0.0))
    return hot.astype(BF)


def forward_kernel(q_ref, kv_ref, segq_ref, segk_ref, o_ref, qa_ref, kt_ref, va_ref):
    nblk = KEYS // TOK

    def build(b, _):
        kv = kv_ref[b]
        off = pl.multiple_of(b * TOK, TOK)
        kt_ref[0:64, pl.ds(off, TOK)] = kv[0:64]
        kt_ref[64:128, pl.ds(off, TOK)] = kv[0:64]
        kt_ref[128:144, pl.ds(off, TOK)] = key_rows(segk_ref[pl.ds(b, 1), :])
        turned = kv.astype(F32).T
        lane = lax.broadcasted_iota(jnp.int32, (TOK, TOK), 1)
        va_ref[pl.ds(off, TOK), :] = jnp.where(
            lane >= 64, turned, jnp.where(lane == 0, 1.0, 0.0)
        ).astype(BF)
        return 0

    lax.fori_loop(0, nblk, build, 0)

    qblk = 416
    kblk = 1024

    def one(i, _):
        off = pl.multiple_of(i * qblk, 16)
        rows = pl.ds(off, qblk)
        scaled = q_ref[rows, :].astype(F32) * (LOG2E / 8.0)
        hi = scaled.astype(BF)
        lo = (scaled - hi.astype(F32)).astype(BF)
        seg = segq_ref[rows, :]
        lane = lax.broadcasted_iota(jnp.int32, (qblk, 16), 1)
        pen = jnp.where((lane < 5) & (lane != seg), BLOCK_OUT, 0.0)
        qa = jnp.concatenate([hi, lo, pen.astype(BF)], axis=1)

        def step(j, carry):
            top, acc = carry
            koff = pl.multiple_of(j * kblk, kblk)
            s = dot(qa, kt_ref[:, pl.ds(koff, kblk)], 1, 0)
            raised = jnp.maximum(top, jnp.max(s, axis=1, keepdims=True))
            p = jnp.exp2(s - raised).astype(BF)
            fade = jnp.exp2(top - raised)
            acc = acc * fade + dot(p, va_ref[pl.ds(koff, kblk), :], 1, 0)
            return raised, acc

        top, acc = lax.fori_loop(
            0,
            KEYS // kblk,
            step,
            (jnp.full((qblk, 1), -3e38, F32), jnp.zeros((qblk, 128), F32)),
        )
        total = acc[:, 0:1]
        o_ref[rows, :] = acc[:, 64:128] / total
        lse = top + jnp.log(total) * LOG2E
        h, m, l = split3(-lse)
        ls = jnp.where(
            lane == 5, h.astype(F32), jnp.where(lane == 6, m.astype(F32), jnp.where(lane == 7, l.astype(F32), pen))
        )
        qa_ref[rows, :] = jnp.concatenate([hi, lo, ls.astype(BF)], axis=1)
        return 0

    lax.fori_loop(0, ROWS // qblk, one, 0)


def attend(q, kv, segq, segk):
    return pl.pallas_call(
        forward_kernel,
        out_shape=(
            jax.ShapeDtypeStruct((ROWS, HDIM), F32),
            jax.ShapeDtypeStruct((ROWS, AUG), BF),
        ),
        in_specs=[pl.BlockSpec(memory_space=pltpu.VMEM)] * 4,
        out_specs=[pl.BlockSpec(memory_space=pltpu.VMEM)] * 2,
        scratch_shapes=[pltpu.VMEM((AUG, KEYS), BF), pltpu.VMEM((KEYS, 128), BF)],
        compiler_params=pltpu.CompilerParams(vmem_limit_bytes=56 * 2**20),
        cost_estimate=pl.CostEstimate(
            flops=2 * ROWS * KEYS * 512, bytes_accessed=4 * 2**20, transcendentals=ROWS * KEYS
        ),
        name="attend",
    )(q, kv, segq, segk)


def backward_kernel(qa_ref, q_ref, qt_ref, do_ref, dot_ref, o_ref, kv_ref, segk_ref, dkv_ref, dq_ref, doa_ref, acc_ref):
    step = pl.program_id(0)

    @pl.when(step == 0)
    def _():
        grad = do_ref[...].astype(F32)
        delta = jnp.sum(grad * o_ref[...], axis=1, keepdims=True)
        h, m, l = split3(-delta)
        lane = lax.broadcasted_iota(jnp.int32, (ROWS, 16), 1)
        ext = jnp.where(
            lane == 5, h.astype(F32), jnp.where(lane == 6, m.astype(F32), jnp.where(lane == 7, l.astype(F32), 0.0))
        )
        doa_ref[...] = jnp.concatenate([do_ref[...], ext.astype(BF)], axis=1)
        acc_ref[...] = jnp.zeros_like(acc_ref)

    kvt = jnp.concatenate([kv_ref[0, i] for i in range(4)], axis=1)
    extra = jnp.concatenate([key_rows(segk_ref[0, i : i + 1, :]) for i in range(4)], axis=1)
    kt = jnp.concatenate([kvt[0:64], kvt[0:64], extra], axis=0)
    vt = jnp.concatenate([kvt[64:128], extra], axis=0)
    turned = kvt.astype(F32).T.astype(BF)
    s = dot(qa_ref[...], kt, 1, 0)
    p = jnp.exp2(s)
    dp = dot(doa_ref[...], vt, 1, 0)
    ds = (p * dp).astype(BF)
    acc_ref[...] += dot(ds, turned, 1, 0)
    dk = dot(qt_ref[...], ds, 1, 0) * 0.125
    dv = dot(dot_ref[...], p.astype(BF), 1, 0)
    both = jnp.concatenate([dk, dv], axis=0).astype(BF)
    for i in range(4):
        dkv_ref[0, i] = both[:, i * TOK : (i + 1) * TOK]

    @pl.when(step == pl.num_programs(0) - 1)
    def _():
        dq_ref[...] = (acc_ref[:, 0:64] * 0.125).astype(BF)


def attend_back(qa, q, grad, o, kv, segk):
    whole = lambda shape: pl.BlockSpec(shape, lambda i: (0,) * len(shape))
    return pl.pallas_call(
        backward_kernel,
        grid=(NCOL,),
        out_shape=(
            jax.ShapeDtypeStruct((NCOL, 4, TOK, TOK), BF),
            jax.ShapeDtypeStruct((ROWS, HDIM), BF),
        ),
        in_specs=[
            whole((ROWS, AUG)),
            whole((ROWS, HDIM)),
            whole((HDIM, ROWS)),
            whole((ROWS, HDIM)),
            whole((HDIM, ROWS)),
            whole((ROWS, HDIM)),
            pl.BlockSpec((1, 4, TOK, TOK), lambda i: (i, 0, 0, 0)),
            pl.BlockSpec((1, 4, TOK), lambda i: (i, 0, 0)),
        ],
        out_specs=[
            pl.BlockSpec((1, 4, TOK, TOK), lambda i: (i, 0, 0, 0)),
            whole((ROWS, HDIM)),
        ],
        scratch_shapes=[pltpu.VMEM((ROWS, 80), BF), pltpu.VMEM((ROWS, 128), F32)],
        compiler_params=pltpu.CompilerParams(vmem_limit_bytes=56 * 2**20),
        cost_estimate=pl.CostEstimate(
            flops=2 * ROWS * KEYS * 5 * 256, bytes_accessed=8 * 2**20, transcendentals=ROWS * KEYS
        ),
        name="attend_back",
    )(qa, q, q.T, grad, grad.T, o, kv.reshape(NCOL, 4, TOK, TOK), segk.reshape(NCOL, 4, TOK))


def pack_rows(blocks):
    return jnp.concatenate([blocks[..., 0:64, :], blocks[..., 64:128, :]], axis=-1)


def unpack_rows(blocks):
    return jnp.concatenate([blocks[..., 0:64], blocks[..., 64:128]], axis=-2)


def to_workers(heads):
    padded = jnp.pad(heads, ((0, 0), (0, 32), (0, 0)))
    windows = jnp.stack([padded[:, SHARE * k : SHARE * k + 128] for k in range(PER_HEAD)], axis=1)
    keep = jnp.arange(128)[None, None, :, None] < SHARE
    windows = jnp.where(keep, windows, jnp.zeros_like(windows))
    windows = windows.reshape(15, 128, HDIM)
    return jnp.pad(pack_rows(windows), ((0, 1), (0, 0), (0, 0)))


def from_tokens(received):
    return unpack_rows(received)[:, :SHARE].reshape(ROWS, HDIM)


def to_tokens(rows):
    padded = jnp.pad(rows.reshape(NCOL, SHARE, HDIM), ((0, 0), (0, 128 - SHARE), (0, 0)))
    return pack_rows(padded)


def from_workers(received):
    rows = unpack_rows(received[:15])[:, :SHARE]
    return rows.reshape(3, PER_HEAD * SHARE, HDIM)[:, : NROW * TOK]


def exchange(blocks, axis):
    return lax.all_to_all(blocks, axis, 0, 0, tiled=True)


def swap_cores(v):
    return lax.ppermute(v, "dp", [(0, 1), (1, 0)])


def hi_lo(v):
    hi = v.astype(BF)
    return hi, (v - hi.astype(F32)).astype(BF)


def per_device(
    inputs,
    segments,
    joint_weight,
    joint_bias,
    output_weight,
    output_bias,
    first_norm_gain,
    shift_first,
    up_weight,
    up_bias,
    down_weight,
    down_bias,
    second_norm_gain,
    second_norm_shift,
    cotangent,
):
    core = lax.axis_index("dp")
    col = lax.axis_index("col")

    vectors = jnp.stack(
        [output_bias, first_norm_gain, shift_first, down_bias, second_norm_gain, second_norm_shift]
    )
    my_bias = lax.dynamic_slice_in_dim(up_bias, (core * NCOL + col) * 24, 24, 0)
    small = jnp.concatenate(
        [part.ravel() for part in split3(vectors)] + [part.ravel() for part in split3(my_bias)]
    )
    small = jnp.pad(small, (0, 4 * 384 - small.shape[0])).reshape(4, 384)
    shard = jnp.concatenate(
        [
            lax.dynamic_slice_in_dim(up_weight, core * 384, 384, 1),
            lax.dynamic_slice_in_dim(down_weight, core * 384, 384, 1),
            lax.dynamic_slice_in_dim(output_weight, core * 96, 96, 0).reshape(12, 384),
            small,
        ],
        axis=0,
    )
    everything = lax.all_gather(shard, ("dp", "row", "col"), axis=0, tiled=False)
    everything = everything.reshape(2, NROW, NCOL, 112, 384)
    up_full = jnp.transpose(everything[:, :, :, 0:48], (2, 3, 1, 0, 4)).reshape(DIM, 3072)
    down_full = jnp.transpose(everything[:, :, :, 48:96], (2, 3, 1, 0, 4)).reshape(DIM, 3072)
    out_full = jnp.transpose(
        everything[:, :, :, 96:108].reshape(2, NROW, NCOL, 96, 48), (1, 0, 3, 2, 4)
    ).reshape(DIM, DIM)
    little = everything[:, :, :, 108:112].reshape(2, NROW, NCOL, 1536).astype(F32)
    vecs = little[0, 0, :, :864].reshape(NCOL, 3, 6, 48).sum(1)
    vecs = jnp.transpose(vecs, (1, 0, 2)).reshape(6, DIM)
    out_b, gain_1, shift_1, down_b, gain_2, shift_2 = [vecs[i][None, :] for i in range(6)]
    up_b = little[:, :, :, 864:936].reshape(2, NROW, NCOL, 3, 24).sum(3)
    up_b = jnp.transpose(up_b, (1, 0, 2, 3)).reshape(1, 3072)

    def by_col(a):
        return jnp.transpose(a.reshape(48, NCOL, TOK), (1, 0, 2))

    first = jnp.concatenate(
        [by_col(inputs), by_col(cotangent), jnp.broadcast_to(joint_weight[None], (NCOL, 48, 576))],
        axis=2,
    )
    first = exchange(first, "col")
    x_t = first[:, :, 0:TOK].reshape(DIM, TOK)
    ct_t = first[:, :, TOK : 2 * TOK].reshape(DIM, TOK)
    wj = first[:, :, 2 * TOK :].reshape(DIM, 576)

    x4 = lax.all_gather(x_t, "row", axis=0, tiled=False)
    xc_t = jnp.transpose(x4, (1, 0, 2)).reshape(DIM, NROW * TOK)
    wj3 = wj.reshape(DIM, 3, 3, HDIM)
    wq = wj3[:, :, 0].reshape(DIM, 192)
    wkv = wj3[:, :, 1:].reshape(DIM, 384)
    bias3 = joint_bias.reshape(3, 2, HDIM)
    q_all = (dot(xc_t, wq, 0, 0) + bias3[:, 0].reshape(1, 192)).astype(BF)
    kv_bias = jnp.concatenate([jnp.zeros((3, HDIM), F32), bias3[:, 1]], axis=1).reshape(384, 1)
    kv_all = (dot(wkv, xc_t, 0, 0) + kv_bias).astype(BF)
    kv_heads = jnp.transpose(kv_all.reshape(3, 128, NROW, TOK), (0, 2, 1, 3)).reshape(3, 512, TOK)
    kv_out = jnp.broadcast_to(kv_heads[:, None], (3, PER_HEAD, 512, TOK)).reshape(15, 512, TOK)
    kv_out = jnp.concatenate([kv_out, kv_heads[2:3]], axis=0)
    q_out = to_workers(jnp.transpose(q_all.reshape(512, 3, HDIM), (1, 0, 2)))
    arrived = exchange(jnp.concatenate([kv_out, q_out], axis=1), "col")
    kv = arrived[:, :512].reshape(64, TOK, TOK)
    q = from_tokens(arrived[:, 512:])

    seg_k = jnp.transpose(segments.reshape(NROW, NCOL, TOK), (1, 0, 2))
    seg_rows = jnp.pad(seg_k.reshape(NCOL, 512), ((0, 0), (0, 8)))
    seg_q = lax.dynamic_slice_in_dim(seg_rows, lax.rem(col, PER_HEAD) * SHARE, SHARE, 1)
    seg_q = seg_q.reshape(ROWS, 1)
    seg_k = seg_k.reshape(64, TOK)

    o, qa = attend(q, kv, seg_q, seg_k)

    attended_r = from_workers(exchange(to_tokens(o.astype(BF)), "col"))
    attended_r = jnp.transpose(attended_r, (1, 0, 2)).reshape(NROW, TOK, 192)
    attended = exchange(attended_r, "row")
    attended = jnp.transpose(attended, (1, 0, 2)).reshape(TOK, DIM)

    tok = x_t.T.astype(F32)
    cot = ct_t.T.astype(F32)
    h1 = tok + (jnp.dot(attended, out_full, preferred_element_type=F32) + out_b)
    mean1 = jnp.mean(h1, axis=1, keepdims=True)
    off1 = h1 - mean1
    inv1 = lax.rsqrt(jnp.mean(off1 * off1, axis=1, keepdims=True) + EPS)
    xhat1 = off1 * inv1
    n1 = xhat1 * gain_1 + shift_1
    n1_low = n1.astype(BF)
    pre = jnp.dot(n1_low, up_full, preferred_element_type=F32) + up_b
    phi = gelu_parts(pre)
    activ = (pre * phi).astype(BF)
    slope = phi + pre * jnp.exp(-0.5 * pre * pre) * (1.0 / math.sqrt(2.0 * math.pi))
    h2 = n1 + (dot(activ, down_full, 1, 1) + down_b)
    mean2 = jnp.mean(h2, axis=1, keepdims=True)
    off2 = h2 - mean2
    inv2 = lax.rsqrt(jnp.mean(off2 * off2, axis=1, keepdims=True) + EPS)
    xhat2 = off2 * inv2
    final = (xhat2 * gain_2 + shift_2).astype(BF)
    dx2 = cot * gain_2
    dh2 = inv2 * (
        dx2 - jnp.mean(dx2, axis=1, keepdims=True) - xhat2 * jnp.mean(dx2 * xhat2, axis=1, keepdims=True)
    )
    d_branch = dh2.astype(BF)
    d_pre = (jnp.dot(d_branch, down_full, preferred_element_type=F32) * slope).astype(BF)
    up1 = dh2 + dot(d_pre, up_full, 1, 1)
    dx1 = up1 * gain_1
    dh1 = inv1 * (
        dx1 - jnp.mean(dx1, axis=1, keepdims=True) - xhat1 * jnp.mean(dx1 * xhat1, axis=1, keepdims=True)
    )
    d_attn = dh1.astype(BF)
    d_att = dot(d_attn, out_full, 1, 1).astype(BF)
    norm_vecs = jnp.stack(
        [
            jnp.sum(up1 * xhat1, axis=0),
            jnp.sum(up1, axis=0),
            jnp.sum(cot * xhat2, axis=0),
            jnp.sum(cot, axis=0),
        ]
    )

    d_att_r = jnp.transpose(d_att.reshape(TOK, NROW, 192), (1, 0, 2))
    d_att_r = exchange(d_att_r, "row").reshape(512, 3, HDIM)
    grad_o = from_tokens(exchange(to_workers(jnp.transpose(d_att_r, (1, 0, 2))), "col"))
    dkv, dq = attend_back(qa, q, grad_o, o, kv, seg_k)
    back = exchange(jnp.concatenate([dkv.reshape(NCOL, 512, TOK), to_tokens(dq)], axis=1), "col")
    dkv_sum = jnp.sum(back[:15, :512].reshape(3, PER_HEAD, NROW, TOK, TOK).astype(F32), axis=1)
    dkv_t = jnp.transpose(dkv_sum.astype(BF), (0, 2, 1, 3)).reshape(3, TOK, 512)
    dq_t = jnp.transpose(from_workers(back[:, 512:]), (0, 2, 1))
    dproj_t = jnp.concatenate([dq_t, dkv_t], axis=1).reshape(576, 512)

    din = jnp.dot(wj, dproj_t, preferred_element_type=F32).astype(BF)
    din = exchange(jnp.transpose(din.reshape(DIM, NROW, TOK), (1, 0, 2)), "row")
    grad_in = (jnp.sum(din.astype(F32), axis=0) + dh1.T).astype(BF)
    grad_wj = dot(xc_t, dproj_t, 1, 1)
    bias_j = jnp.sum(dproj_t.astype(F32), axis=1).reshape(3, 3, HDIM)
    bias_j = jnp.stack([bias_j[:, 0], bias_j[:, 2]], axis=1).reshape(-1)

    rows_v = jnp.concatenate([part.reshape(24, 128) for part in hi_lo(norm_vecs)], axis=0)
    share = jnp.concatenate([n1_low.T, d_branch.T, d_attn.T, rows_v], axis=0)
    share = jnp.broadcast_to(share[None], (NROW, 3 * DIM + 48, TOK))

    def by_row(a):
        return jnp.transpose(a.reshape(TOK, NROW, 6, 128), (1, 2, 0, 3)).reshape(NROW, DIM, TOK)

    sent = jnp.concatenate([share, by_row(d_pre), by_row(activ)], axis=1)
    got = exchange(sent, "row")

    def feats(a):
        return jnp.transpose(a, (1, 0, 2)).reshape(DIM, 512)

    n1_c = feats(got[:, 0:DIM])
    db_c = feats(got[:, DIM : 2 * DIM])
    da_c = feats(got[:, 2 * DIM : 3 * DIM])
    nv = got[:, 3 * DIM : 3 * DIM + 48].astype(F32).reshape(NROW, 2, 4, DIM).sum((0, 1))

    def hidden(a):
        return jnp.transpose(a.reshape(NROW, 6, TOK, 128), (0, 2, 1, 3)).reshape(512, DIM)

    dp_c = hidden(got[:, 3 * DIM + 48 : 4 * DIM + 48])
    ac_c = hidden(got[:, 4 * DIM + 48 :])
    g_up = jnp.dot(n1_c, dp_c, preferred_element_type=F32)
    g_down = jnp.dot(db_c, ac_c, preferred_element_type=F32)
    g_out = jnp.dot(da_c, attended_r.reshape(512, 192), preferred_element_type=F32)
    cols_v = jnp.stack(
        [jnp.sum(db_c.astype(F32), axis=1), jnp.sum(da_c.astype(F32), axis=1)] + [nv[i] for i in range(4)],
        axis=1,
    )
    up_sums = jnp.sum(dp_c.astype(F32), axis=0)

    def spread(v):
        return jnp.tile(v.reshape(48, -1), (NCOL, 1))

    def halves(v):
        blocks = v.reshape(NCOL, 2, 24, v.shape[1])
        mine = lax.dynamic_index_in_dim(blocks, core, 1, keepdims=False)
        other = lax.dynamic_index_in_dim(blocks, 1 - core, 1, keepdims=False)
        return (mine.astype(F32) + swap_cores(other).astype(F32)).astype(BF)

    def pair(v):
        theirs = swap_cores(v)
        return jnp.where(core == 0, jnp.concatenate([v, theirs]), jnp.concatenate([theirs, v]))

    wide = jnp.concatenate(
        [g_up.astype(BF), g_down.astype(BF), g_out.astype(BF)]
        + list(hi_lo(cols_v))
        + [spread(part) for part in hi_lo(up_sums)]
        + [jnp.zeros((DIM, 20), BF)],
        axis=1,
    )
    wide = jnp.sum(exchange(halves(wide), "col").astype(F32), axis=0)
    wide = pair(wide)
    grad_up = wide[:, 0:768]
    grad_down = wide[:, 768:1536]
    grad_out = wide[:, 1536:1728].T
    six = wide[:, 1728:1734] + wide[:, 1734:1740]
    grad_up_bias = (wide[:, 1740:1756] + wide[:, 1756:1772]).reshape(768)

    last = jnp.concatenate(
        [grad_wj.astype(BF)] + [spread(part) for part in hi_lo(bias_j)] + [jnp.zeros((DIM, 48), BF)], axis=1
    )
    last = halves(last)
    mixed = jnp.concatenate([last.reshape(NCOL, 120, 128), grad_in.reshape(NCOL, 48, TOK)], axis=1)
    mixed = exchange(mixed, "col")
    grad_inputs = jnp.transpose(mixed[:, 120:], (1, 0, 2)).reshape(48, 2048).astype(F32)
    last = jnp.sum(mixed[:, :120].astype(F32), axis=0).reshape(24, 640)
    last = pair(last)
    grad_joint = last[:, :576]
    grad_joint_bias = (last[:, 576:584] + last[:, 584:592]).reshape(384)

    out_blocks = exchange(final.T.reshape(NCOL, 48, TOK), "col")
    layer_output = jnp.transpose(out_blocks, (1, 0, 2)).reshape(48, 2048)

    return (
        layer_output,
        grad_inputs,
        grad_joint,
        grad_joint_bias,
        grad_out,
        six[:, 1],
        six[:, 2],
        six[:, 3],
        grad_up,
        grad_up_bias,
        grad_down,
        six[:, 0],
        six[:, 4],
        six[:, 5],
    )


def solution(mesh):
    grid = P("col", ("dp", "row"))
    block = P("col", "row")
    return jax.shard_map(
        per_device,
        mesh=mesh,
        in_specs=(
            grid, P("dp", None), block, P("row"), P("row", "col"), P("col"), P("col"), P("col"),
            block, P("row"), block, P("col"), P("col"), P("col"), grid,
        ),
        out_specs=(
            grid, grid, block, P("row"), P("row", "col"), P("col"), P("col"), P("col"),
            block, P("row"), block, P("col"), P("col"), P("col"),
        ),
        check_vma=False,
    )
```

time: 1200 us -> 540 us (0.45)
  waiting for transfers between devices: 499 us -> 129 us
  matrix products: 239 us -> 25.7 us
  blocking collectives: 193 us -> 21.7 us
  Pallas kernels: 0 us -> 72.7 us
  local copies, waits for them, and re-layouts: 94.6 us -> 147 us
  other arithmetic: 73 us -> 37.2 us
  starting transfers between devices: 46.2 us -> 80.3 us
  loops' own time: 22.4 us -> 0 us
    all_gather x5 -> x1, waiting for transfers between devices: 344 us -> 0.02 us  [per_device(): lax.all_gather(shard, ('dp', 'row', 'col'), axis=0, tiled=False)]
    dot_general x84 -> x13, matrix products: 239 us -> 25.7 us  [the longest x6 10.7 us: dot(): lax.dot_general(a, b, (((ca,), (cb,)), ((), ())), preferred_element_type=...]
    all_to_all x19 -> x1, blocking collectives: 193 us -> 9.19 us  [exchange(): return lax.all_to_all(blocks, axis, 0, 0, tiled=True)]
    reduce_scatter x1 -> x0, waiting for transfers between devices: 81.8 us -> none  [per_device(): lax.psum_scatter(grad_keys_all.astype(jnp.bfloat16), 'col', scatter_dimen...]
    pallas_call x0 -> x2, Pallas kernels: none -> 72.7 us  [the longest x1 36.5 us: attend_back(): pl.pallas_call(backward_kernel, grid=(NCOL,), out_shape=(jax.ShapeDtypeSt...]
    all_to_all x10 -> x11, waiting for transfers between devices: 73.3 us -> 129 us  [exchange(): return lax.all_to_all(blocks, axis, 0, 0, tiled=True)]
    dynamic_slice x73 -> x5, local copies, waits for them, and re-layouts: 53.7 us -> 1.85 us  [the longest x1 0.8 us: per_device(): lax.dynamic_slice_in_dim(down_weight, core * 384, 384, 1)]
    reshape x9 -> x24, local copies, waits for them, and re-layouts: 3.51 us -> 40.5 us  [the longest x1 11.4 us: per_device(): jnp.transpose(everything[:, :, :, 0:48], (2, 3, 1, 0, 4)).reshape(DIM, 3072)]
  transfers between devices with their start and end apart: 16 -> 16, of which waited for: 15 -> 12; matrix products, arithmetic and copies ran while one was open for 5% -> 29% of each run, Pallas kernels for 0% -> 7%
where the time goes in v1:
time: 540 us; the launch traced here: 530 us
  local copies, waits for them, and re-layouts  147 us (27%)
  waiting for transfers between devices  129 us (24%)
  starting transfers between devices  80.3 us (15%)
  Pallas kernels  72.7 us (13%)
  other arithmetic  37.2 us (7%)
  matrix products  25.7 us (5%)
  blocking collectives  21.7 us (4%)
  between operations  15.7 us (3%)
    all_to_all x11, waiting for transfers between devices, exchange(): return lax.all_to_all(blocks, axis, 0, 0, tiled=True)  129 us
    all_to_all x11, starting transfers between devices, exchange(): return lax.all_to_all(blocks, axis, 0, 0, tiled=True)  55.4 us
    pallas_call x1, Pallas kernels, attend_back(): pl.pallas_call(backward_kernel, grid=(NCOL,), out_shape=(jax.ShapeDtypeSt...  36.5 us
    pallas_call x1, Pallas kernels, attend(): pl.pallas_call(forward_kernel, out_shape=(jax.ShapeDtypeStruct((ROWS, HDI...  36.2 us
    unnamed x97, local copies, waits for them, and re-layouts  33.3 us
    ppermute x4, starting transfers between devices, swap_cores(): return lax.ppermute(v, 'dp', [(0, 1), (1, 0)])  24.8 us
    all_gather x1, blocking collectives, per_device(): x4 = lax.all_gather(x_t, 'row', axis=0, tiled=False)  12.5 us
    reshape x1, local copies, waits for them, and re-layouts, per_device(): jnp.transpose(everything[:, :, :, 0:48], (2, 3, 1, 0, 4)).reshape(DIM, 3072)  11.4 us
  transfers between devices with their start and end apart: 16, of which 12 were waited for; matrix products, arithmetic and copies ran while one was open for 29% of the time, Pallas kernels for 7%

profile of v1, /device:TPU:1, one launch (start us, length us, event | category | flops | bytes accessed | tf_op | source)
XLA Modules:
  0.0 529.8 jit_solution(8031523757663608475)
XLA Ops:
  14.9 8.7 %all-to-all-start = ((bf16[16,48,832]{2,1,0:T(8,128)(2,1)}), bf16[16,48,832]{2,1,0:T(8,128)(2,1)S(1)}, u32[]{:S(2)}, u32[]{:S(2)}) async-start(bf16[16,48,832]{2,1,0:T(8,128)(2,1)} %pad_maximum_fusion.1), calls=%async_computation | async-start | bytes 2752512 | tf_op jit(solution)/shard_map/all_to_all | solution.py:233
  23.9 20.3 %all-to-all-done = bf16[16,48,832]{2,1,0:T(8,128)(2,1)S(1)} async-done(((bf16[16,48,832]{2,1,0:T(8,128)(2,1)}), bf16[16,48,832]{2,1,0:T(8,128)(2,1)S(1)}, u32[]{:S(2)}, u32[]{:S(2)}) %all-to-all-start) | async-done | bytes 1277984 | tf_op jit(solution)/shard_map/all_to_all | solution.py:233
  52.9 12.5 %all_gather.9 = bf16[4,768,128]{2,1,0:T(8,128)(2,1)S(1)} all-gather(bf16[1,768,128]{2,1,0:T(8,128)(2,1)S(1)} %bitcast.321), channel_id=1, replica_groups=mesh['dp'=2,'row'=4,'col'=16] {'row'}, dimensions={0}, use_global_device_ids=true | all-gather | bytes 983040 | tf_op jit(solution)/shard_map/all_gather | solution.py:308
  75.6 6.6 %all-to-all-start.1 = ((bf16[16,576,128]{2,1,0:T(8,128)(2,1)}), bf16[16,576,128]{2,1,0:T(8,128)(2,1)S(1)}, u32[]{:S(2)}, u32[]{:S(2)}) async-start(bf16[16,576,128]{2,1,0:T(8,128)(2,1)} %fusion.3), calls=%async_computation.1 | async-start | bytes 4718592 | tf_op jit(solution)/shard_map/all_to_all | solution.py:233
  83.6 40.2 %all-to-all-done.1 = bf16[16,576,128]{2,1,0:T(8,128)(2,1)S(1)} async-done(((bf16[16,576,128]{2,1,0:T(8,128)(2,1)}), bf16[16,576,128]{2,1,0:T(8,128)(2,1)S(1)}, u32[]{:S(2)}, u32[]{:S(2)}) %all-to-all-start.1) | async-done | bytes 2359328 | tf_op jit(solution)/shard_map/all_to_all | solution.py:233
  126.3 36.2 %attend.1 = (f32[1664,64]{1,0:T(8,128)}, bf16[1664,144]{1,0:T(8,128)(2,1)}) custom-call(bf16[1664,64]{1,0:T(8,128)(2,1)} %bitcast.322, bf16[64,128,128]{2,1,0:T(8,128)(2,1)} %bitcast.312, s32[1664,1]{1,0:T(8,128)} %reshape.466.segq_ref, s32[64,128]{1,0:T(8,128)} %bitcast.366), custom_call_target="tpu_custom_call" | custom-call | flops 13958643712 | bytes 4194304 | tf_op jit(solution)/shard_map/attend/pallas_call | solution.py:116
  170.1 5.7 %all-to-all-done.2 = bf16[16,64,128]{2,1,0:T(8,128)(2,1)S(1)} async-done(((bf16[16,64,128]{2,1,0:T(8,128)(2,1)}), bf16[16,64,128]{2,1,0:T(8,128)(2,1)S(1)}, u32[]{:S(2)}, u32[]{:S(2)}) %all-to-all-start.2) | async-done | bytes 262176 | tf_op jit(solution)/shard_map/all_to_all | solution.py:233
  177.2 4.2 all-to-all-start.3
  181.4 8.7 %fusion.62 = (bf16[2,4,16,48,384]{4,3,2,1,0:T(8,128)(2,1)}, bf16[2,4,16,48,384]{4,3,2,1,0:T(8,128)(2,1)}) fusion(bf16[2,4,16,112,384]{4,3,2,1,0:T(8,128)(2,1)} %bitcast.291), kind=kLoop, calls=%fused_computation.201 | loop fusion | bytes 18874368 | tf_op jit(solution)/shard_map/slice | solution.py:285
  195.7 9.4 %copy.342 = bf16[2,4,16,48,384]{4,0,1,3,2:T(2,128)(2,1)} copy(bf16[2,4,16,48,384]{4,3,2,1,0:T(8,128)(2,1)} %get-tuple-element.62) | data formatting | bytes 9437184
  205.1 11.2 %reshape.424 = bf16[768,3072]{1,0:T(8,128)(2,1)} reshape(bf16[16,48,4,2,384]{4,3,2,1,0:T(2,128)(2,1)} %bitcast.288) | data formatting | bytes 9437184 | tf_op jit(solution)/shard_map/reshape | solution.py:285
  216.3 4.5 reshape.420
  224.6 5.3 %reshape.421 = bf16[768,768]{0,1:T(8,128)(2,1)S(1)} reshape(bf16[4,2,96,16,48]{2,1,0,4,3:T(2,128)(2,1)} %copy.261) | data formatting | bytes 2359296 | tf_op jit(solution)/shard_map/reshape | solution.py:288
  232.4 9.3 %copy.343 = bf16[2,4,16,48,384]{4,0,1,3,2:T(2,128)(2,1)} copy(bf16[2,4,16,48,384]{4,3,2,1,0:T(8,128)(2,1)} %get-tuple-element.63) | data formatting | bytes 9437184
  241.7 11.4 %reshape.422 = bf16[768,3072]{1,0:T(8,128)(2,1)} reshape(bf16[16,48,4,2,384]{4,3,2,1,0:T(2,128)(2,1)} %bitcast.289) | data formatting | bytes 9437184 | tf_op jit(solution)/shard_map/reshape | solution.py:284
  256.8 4.9 fusion.59
  267.4 9.2 %all_to_all.60 = bf16[4,128,192]{1,2,0:T(8,128)(2,1)S(1)} all-to-all(bf16[4,128,192]{1,2,0:T(8,128)(2,1)S(1)} %bitcast.344), channel_id=1, replica_groups=mesh['dp'=2,'row'=4,'col'=16] {'row'}, dimensions={0} | all-to-all | bytes 393216 | tf_op jit(solution)/shard_map/all_to_all | solution.py:233
  283.0 6.6 %all-to-all-done.6 = bf16[16,64,128]{2,1,0:T(8,128)(2,1)S(1)} async-done(((bf16[16,64,128]{2,1,0:T(8,128)(2,1)}), bf16[16,64,128]{2,1,0:T(8,128)(2,1)S(1)}, u32[]{:S(2)}, u32[]{:S(2)}) %all-to-all-start.6) | async-done | bytes 262176 | tf_op jit(solution)/shard_map/all_to_all | solution.py:233
  290.8 36.5 %attend_back.1 = (bf16[16,4,128,128]{3,2,1,0:T(8,128)(2,1)}, bf16[1664,64]{1,0:T(8,128)(2,1)}) custom-call(bf16[1664,144]{1,0:T(8,128)(2,1)} %get-tuple-element.19.qa_ref, bf16[1664,64]{1,0:T(8,128)(2,1)} %bitcast.323, bf16[64,1664]{1,0:T(8,128)(2,1)} %bitcast.360, bf16[1664,64]{1,0:T(8,128)(2,1)} %bitcast.326, bf16[64,1664]{1,0:T(8,128)(2,1)} %bitcast.361, ...), custom_call_target="tpu_custom_call" | custom-call | flops 34896609280 | bytes 8388608 | tf_op jit(solution)/shard_map/attend_back/pallas_call | solution.py:171
  356.3 6.4 %all-to-all-done.7 = bf16[16,576,128]{2,1,0:T(8,128)(2,1)S(1)} async-done(((bf16[16,576,128]{2,1,0:T(8,128)(2,1)}), bf16[16,576,128]{2,1,0:T(8,128)(2,1)S(1)}, u32[]{:S(2)}, u32[]{:S(2)}) %all-to-all-start.7) | async-done | bytes 2359328 | tf_op jit(solution)/shard_map/all_to_all | solution.py:233
  362.6 4.8 all-to-all-start.10
  378.4 7.9 %collective-permute-start = (bf16[16,24,640]{2,1,0:T(8,128)(2,1)}, bf16[16,24,640]{2,1,0:T(8,128)(2,1)}, u32[]{:S(2)}, u32[]{:S(2)}) collective-permute-start(bf16[16,24,640]{2,1,0:T(8,128)(2,1)} %dynamic-slice_bitcast_fusion.1), channel_id=1, source_target_pairs={{0,64},{64,0},{1,65},{65,1},{2,66},{66,2},{3,67},{67,3},{4,68},{68... | collective-permute-start | bytes 1474568 | tf_op jit(solution)/shard_map/ppermute | solution.py:237
  386.3 19.8 %all-to-all-done.10 = bf16[4,3888,128]{2,1,0:T(8,128)(2,1)} async-done(((bf16[4,3888,128]{2,1,0:T(8,128)(2,1)}), bf16[4,3888,128]{2,1,0:T(8,128)(2,1)}, u32[]{:S(2)}, u32[]{:S(2)}) %all-to-all-start.10) | async-done | bytes 3981344 | tf_op jit(solution)/shard_map/all_to_all | solution.py:233
  427.5 4.8 concatenate.113
  433.5 9.1 %collective-permute-start.2 = (bf16[16,24,1792]{2,1,0:T(8,128)(2,1)}, bf16[16,24,1792]{2,1,0:T(8,128)(2,1)}, u32[]{:S(2)}, u32[]{:S(2)}) collective-permute-start(bf16[16,24,1792]{2,1,0:T(8,128)(2,1)} %dynamic-slice_bitcast_fusion), channel_id=1, source_target_pairs={{0,64},{64,0},{1,65},{65,1},{2,66},{66,2},{3,67},{67,3},{4,68},{68... | collective-permute-start | bytes 4128776 | tf_op jit(solution)/shard_map/ppermute | solution.py:237
  444.3 4.2 all-to-all-start.8
  452.8 7.8 %all-to-all-done.8 = bf16[4,768,128]{1,2,0:T(8,128)(2,1)} async-done(((bf16[4,768,128]{1,2,0:T(8,128)(2,1)}), bf16[4,768,128]{1,2,0:T(8,128)(2,1)}, u32[]{:S(2)}, u32[]{:S(2)}) %all-to-all-start.8) | async-done | bytes 786464 | tf_op jit(solution)/shard_map/all_to_all | solution.py:233
  460.6 6.2 %all-to-all-start.4 = ((bf16[16,48,128]{2,1,0:T(8,128)(2,1)}), bf16[16,48,128]{2,1,0:T(8,128)(2,1)S(1)}, u32[]{:S(2)}, u32[]{:S(2)}) async-start(bf16[16,48,128]{2,1,0:T(8,128)(2,1)} %bitcast.343), calls=%async_computation.4 | async-start | bytes 393216 | tf_op jit(solution)/shard_map/all_to_all | solution.py:233
  474.7 6.0 %all-to-all-start.9 = ((bf16[16,168,128]{2,1,0:T(8,128)(2,1)}), bf16[16,168,128]{2,1,0:T(8,128)(2,1)S(1)}, u32[]{:S(2)}, u32[]{:S(2)}) async-start(bf16[16,168,128]{2,1,0:T(8,128)(2,1)} %pad_maximum_fusion.3), calls=%async_computation.9 | async-start | bytes 1376256 | tf_op jit(solution)/shard_map/all_to_all | solution.py:233
  483.5 8.6 %all-to-all-done.9 = bf16[16,168,128]{2,1,0:T(8,128)(2,1)S(1)} async-done(((bf16[16,168,128]{2,1,0:T(8,128)(2,1)}), bf16[16,168,128]{2,1,0:T(8,128)(2,1)S(1)}, u32[]{:S(2)}, u32[]{:S(2)}) %all-to-all-start.9) | async-done | bytes 688160 | tf_op jit(solution)/shard_map/all_to_all | solution.py:233
  500.5 13.0 %all-to-all-done.11 = bf16[16,24,1792]{2,1,0:T(8,128)(2,1)S(1)} async-done(((bf16[16,24,1792]{2,1,0:T(8,128)(2,1)}), bf16[16,24,1792]{2,1,0:T(8,128)(2,1)S(1)}, u32[]{:S(2)}, u32[]{:S(2)}) %all-to-all-start.11) | async-done | bytes 1376288 | tf_op jit(solution)/shard_map/all_to_all | solution.py:233
  513.7 4.8 collective-permute-start.3
  (315 shorter events, 159.4 us)
Async XLA Ops:
  7.2 6.4 %copy-start.28 = (bf16[48,576]{1,0:T(8,128)(2,1)S(1)}, bf16[48,576]{1,0:T(8,128)(2,1)}, u32[]{:S(2)}) copy-start(bf16[48,576]{1,0:T(8,128)(2,1)} %param.17) | copy-start | bytes 165892
  7.2 174.2 %all-gather.3.cloned.1.call-start = ((), (), s32[]{:S(2)}) async-start(), calls=%async_computation.12 | async-start | bytes 11096064 | tf_op jit(solution)/shard_map/all_gather | solution.py:282
  14.9 8.7 %copy-start.30 = (f32[384]{0:T(512)S(1)}, f32[384]{0:T(512)}, u32[]{:S(2)}) copy-start(f32[384]{0:T(512)} %param.18) | copy-start | bytes 4612
  14.9 29.3 %all-to-all-start = ((bf16[16,48,832]{2,1,0:T(8,128)(2,1)}), bf16[16,48,832]{2,1,0:T(8,128)(2,1)S(1)}, u32[]{:S(2)}, u32[]{:S(2)}) async-start(bf16[16,48,832]{2,1,0:T(8,128)(2,1)} %pad_maximum_fusion.1), calls=%async_computation | async-start | bytes 2752512 | tf_op jit(solution)/shard_map/all_to_all | solution.py:233
  51.0 15.6 %copy-start.6 = (bf16[768,3,1,64]{3,2,1,0:T(2,128)(2,1)S(1)}, bf16[768,3,1,64]{3,2,1,0:T(2,128)(2,1)}, u32[]{:S(2)}) copy-start(bf16[768,3,1,64]{3,2,1,0:T(2,128)(2,1)} %slice.372) | copy-start | bytes 884740
  52.9 16.5 %copy-start.5 = (bf16[768,3,2,64]{3,2,1,0:T(2,128)(2,1)S(1)}, bf16[768,3,2,64]{3,2,1,0:T(2,128)(2,1)}, u32[]{:S(2)}) copy-start(bf16[768,3,2,64]{3,2,1,0:T(2,128)(2,1)} %slice.369) | copy-start | bytes 1769476
  75.6 6.7 %copy-start.29 = (s32[1,8192]{1,0:T(1,128)S(1)}, s32[1,8192]{1,0:T(1,128)}, u32[]{:S(2)}) copy-start(s32[1,8192]{1,0:T(1,128)} %param.16) | copy-start | bytes 98308
  75.6 48.2 %all-to-all-start.1 = ((bf16[16,576,128]{2,1,0:T(8,128)(2,1)}), bf16[16,576,128]{2,1,0:T(8,128)(2,1)S(1)}, u32[]{:S(2)}, u32[]{:S(2)}) async-start(bf16[16,576,128]{2,1,0:T(8,128)(2,1)} %fusion.3), calls=%async_computation.1 | async-start | bytes 4718592 | tf_op jit(solution)/shard_map/all_to_all | solution.py:233
  82.3 43.0 %copy-start.27 = (s32[4,16,128]{2,0,1:T(4,128)}, s32[4,16,128]{2,0,1:T(4,128)S(1)}, u32[]{:S(2)}) copy-start(s32[4,16,128]{2,0,1:T(4,128)S(1)} %copy.346) | copy-start | bytes 98308
  162.5 5.7 %copy-start.18 = (f32[16,48,128]{2,1,0:T(8,128)S(1)}, f32[16,48,128]{2,1,0:T(8,128)}, u32[]{:S(2)}) copy-start(f32[16,48,128]{2,1,0:T(8,128)} %get-tuple-element.73) | copy-start | bytes 1179652
  164.6 11.2 %all-to-all-start.2 = ((bf16[16,64,128]{2,1,0:T(8,128)(2,1)}), bf16[16,64,128]{2,1,0:T(8,128)(2,1)S(1)}, u32[]{:S(2)}, u32[]{:S(2)}) async-start(bf16[16,64,128]{2,1,0:T(8,128)(2,1)} %pad_maximum_fusion.10), calls=%async_computation.2 | async-start | bytes 524288 | tf_op jit(solution)/shard_map/all_to_all | solution.py:233
  177.2 52.8 %all-to-all-start.3 = ((bf16[4,128,192]{1,2,0:T(8,128)(2,1)}), bf16[4,128,192]{1,2,0:T(8,128)(2,1)}, u32[]{:S(2)}, u32[]{:S(2)}) async-start(bf16[4,128,192]{1,2,0:T(8,128)(2,1)} %copy.259), calls=%async_computation.3 | async-start | bytes 393216 | tf_op jit(solution)/shard_map/all_to_all | solution.py:233
  224.6 5.4 %copy-start.11 = (f32[768,128]{0,1:T(8,128)S(1)}, f32[768,128]{0,1:T(8,128)}, u32[]{:S(2)}) copy-start(f32[768,128]{0,1:T(8,128)} %copy.262) | copy-start | bytes 1179652
  253.2 9.1 %slice-start.2 = ((s8[4718592]{0:T(1024)(128)(4,1)}), s8[4194304]{0:T(1024)(128)(4,1)S(1)}, s32[]{:S(2)}) async-start(s8[4718592]{0:T(1024)(128)(4,1)} %bitcast.286), calls=%async_computation.15 | async-start | bytes 8388608
  256.8 5.4 %slice-start.3 = ((s8[4718592]{0:T(1024)(128)(4,1)}), s8[524288]{0:T(1024)(128)(4,1)S(1)}, s32[]{:S(2)}) async-start(s8[4718592]{0:T(1024)(128)(4,1)} %bitcast.286), calls=%async_computation.16 | async-start | bytes 1048576
  278.6 11.0 %all-to-all-start.6 = ((bf16[16,64,128]{2,1,0:T(8,128)(2,1)}), bf16[16,64,128]{2,1,0:T(8,128)(2,1)S(1)}, u32[]{:S(2)}, u32[]{:S(2)}) async-start(bf16[16,64,128]{2,1,0:T(8,128)(2,1)} %pad.36.clone), calls=%async_computation.6 | async-start | bytes 524288 | tf_op jit(solution)/shard_map/all_to_all | solution.py:233
  331.7 30.9 %all-to-all-start.7 = ((bf16[16,576,128]{2,1,0:T(8,128)(2,1)}), bf16[16,576,128]{2,1,0:T(8,128)(2,1)S(1)}, u32[]{:S(2)}, u32[]{:S(2)}) async-start(bf16[16,576,128]{2,1,0:T(8,128)(2,1)} %maximum_maximum_fusion), calls=%async_computation.7 | async-start | bytes 4718592 | tf_op jit(solution)/shard_map/all_to_all | solution.py:233
  362.6 43.5 %all-to-all-start.10 = ((bf16[4,3888,128]{2,1,0:T(8,128)(2,1)}), bf16[4,3888,128]{2,1,0:T(8,128)(2,1)}, u32[]{:S(2)}, u32[]{:S(2)}) async-start(bf16[4,3888,128]{2,1,0:T(8,128)(2,1)} %pad_maximum_fusion), calls=%async_computation.10 | async-start | bytes 7962624 | tf_op jit(solution)/shard_map/all_to_all | solution.py:233
  378.4 70.9 %collective-permute-start = (bf16[16,24,640]{2,1,0:T(8,128)(2,1)}, bf16[16,24,640]{2,1,0:T(8,128)(2,1)}, u32[]{:S(2)}, u32[]{:S(2)}) collective-permute-start(bf16[16,24,640]{2,1,0:T(8,128)(2,1)} %dynamic-slice_bitcast_fusion.1), channel_id=1, source_target_pairs={{0,64},{64,0},{1,65},{65,1},{2,66},{66,2},{3,67},{67,3},{4,68},{68... | collective-permute-start | bytes 1474568 | tf_op jit(solution)/shard_map/ppermute | solution.py:237
  432.3 10.3 %copy-start.8 = (bf16[16,48,576]{2,1,0:T(8,128)(2,1)S(1)}, bf16[16,48,576]{2,1,0:T(8,128)(2,1)}, u32[]{:S(2)}) copy-start(bf16[16,48,576]{2,1,0:T(8,128)(2,1)} %copy-done.7) | copy-start | bytes 2654212
  432.3 10.3 %copy-start.24 = (bf16[3,192,512]{2,1,0:T(8,128)(2,1)S(1)}, bf16[3,192,512]{2,1,0:T(8,128)(2,1)}, u32[]{:S(2)}) copy-start(bf16[3,192,512]{2,1,0:T(8,128)(2,1)} %copy.278) | copy-start | bytes 1769476
  433.5 47.2 %collective-permute-start.2 = (bf16[16,24,1792]{2,1,0:T(8,128)(2,1)}, bf16[16,24,1792]{2,1,0:T(8,128)(2,1)}, u32[]{:S(2)}, u32[]{:S(2)}) collective-permute-start(bf16[16,24,1792]{2,1,0:T(8,128)(2,1)} %dynamic-slice_bitcast_fusion), channel_id=1, source_target_pairs={{0,64},{64,0},{1,65},{65,1},{2,66},{66,2},{3,67},{67,3},{4,68},{68... | collective-permute-start | bytes 4128776 | tf_op jit(solution)/shard_map/ppermute | solution.py:237
  442.6 5.9 %copy-start.23 = (bf16[768,128]{0,1:T(8,128)(2,1)S(1)}, bf16[768,128]{0,1:T(8,128)(2,1)}, u32[]{:S(2)}) copy-start(bf16[768,128]{0,1:T(8,128)(2,1)} %get-tuple-element.80) | copy-start | bytes 589828
  444.3 16.3 %all-to-all-start.8 = ((bf16[4,768,128]{1,2,0:T(8,128)(2,1)}), bf16[4,768,128]{1,2,0:T(8,128)(2,1)}, u32[]{:S(2)}, u32[]{:S(2)}) async-start(bf16[4,768,128]{1,2,0:T(8,128)(2,1)} %bitcast.340), calls=%async_computation.8 | async-start | bytes 1572864 | tf_op jit(solution)/shard_map/all_to_all | solution.py:233
  460.6 13.4 %all-to-all-start.4 = ((bf16[16,48,128]{2,1,0:T(8,128)(2,1)}), bf16[16,48,128]{2,1,0:T(8,128)(2,1)S(1)}, u32[]{:S(2)}, u32[]{:S(2)}) async-start(bf16[16,48,128]{2,1,0:T(8,128)(2,1)} %bitcast.343), calls=%async_computation.4 | async-start | bytes 393216 | tf_op jit(solution)/shard_map/all_to_all | solution.py:233
  474.7 17.4 %all-to-all-start.9 = ((bf16[16,168,128]{2,1,0:T(8,128)(2,1)}), bf16[16,168,128]{2,1,0:T(8,128)(2,1)S(1)}, u32[]{:S(2)}, u32[]{:S(2)}) async-start(bf16[16,168,128]{2,1,0:T(8,128)(2,1)} %pad_maximum_fusion.3), calls=%async_computation.9 | async-start | bytes 1376256 | tf_op jit(solution)/shard_map/all_to_all | solution.py:233
  483.5 12.3 %copy-start.22 = (bf16[16,48,128]{2,1,0:T(8,128)(2,1)S(1)}, bf16[16,48,128]{2,1,0:T(8,128)(2,1)}, u32[]{:S(2)}) copy-start(bf16[16,48,128]{2,1,0:T(8,128)(2,1)} %copy-done.21) | copy-start | bytes 589828
  492.1 21.4 %all-to-all-start.11 = ((bf16[16,24,1792]{2,1,0:T(8,128)(2,1)}), bf16[16,24,1792]{2,1,0:T(8,128)(2,1)S(1)}, u32[]{:S(2)}, u32[]{:S(2)}) async-start(bf16[16,24,1792]{2,1,0:T(8,128)(2,1)} %fusion.2), calls=%async_computation.11 | async-start | bytes 2752512 | tf_op jit(solution)/shard_map/all_to_all | solution.py:233
  496.6 25.9 %copy-start.1 = (bf16[192,48]{0,1:T(8,128)(2,1)S(1)}, bf16[192,48]{0,1:T(8,128)(2,1)}, u32[]{:S(2)}) copy-start(bf16[192,48]{0,1:T(8,128)(2,1)} %param.19) | copy-start | bytes 55300
  496.6 3.9 collective-permute-start.1
  500.5 22.0 %copy-start.26 = (f32[48,640]{1,0:T(8,128)}, f32[48,640]{1,0:T(8,128)S(1)}, u32[]{:S(2)}) copy-start(f32[48,640]{1,0:T(8,128)S(1)} %maximum_select_fusion.1) | copy-start | bytes 368644
  513.7 5.9 %collective-permute-start.3 = (f32[24,1792]{1,0:T(8,128)S(1)}, f32[24,1792]{1,0:T(8,128)S(1)}, u32[]{:S(2)}, u32[]{:S(2)}) collective-permute-start(f32[24,1792]{1,0:T(8,128)S(1)} %convert_reduce_fusion), channel_id=1, source_target_pairs={{0,64},{64,0},{1,65},{65,1},{2,66},{66,2},{3,67},{67,3},{4,68},{68... | collective-permute-start | bytes 516104 | tf_op jit(solution)/shard_map/ppermute | solution.py:237
  (19 other events, 54.7 us)
Sparse Core Ops, SparseCore 0:
  11.7 103.4 all-gather.2

commit v2 on v1

v2 whole, which is shorter than its diff:
```python
import math

import jax
import jax.numpy as jnp
from jax import lax
from jax.experimental import pallas as pl
from jax.experimental.pallas import tpu as pltpu
from jax.sharding import PartitionSpec as P

HDIM = 64
EPS = 1e-06
BLOCK_OUT = -1e30
LOG2E = 1.4426950408889634
BF = jnp.bfloat16
F32 = jnp.float32

DIM = 768
FF = 3072
NCOL = 16
NROW = 4
TOK = 128
PER_HEAD = 5
SHARE = 104
TAIL = SHARE - 64
ROWS = NCOL * SHARE
AUG = 144
JW = 640
HALF = 2
FWD_C = 4
BWD_C = 2
MIB = 2**20
VMEM = pl.BlockSpec(memory_space=pltpu.VMEM)
SENT = 3 * DIM + 48 + 2 * DIM
WROWS = 768


def split3(v):
    hi = v.astype(BF)
    rest = v - hi.astype(F32)
    mid = rest.astype(BF)
    low = (rest - mid.astype(F32)).astype(BF)
    return hi, mid, low


def dot(a, b, ca, cb):
    return lax.dot_general(a, b, (((ca,), (cb,)), ((), ())), preferred_element_type=F32)


def params(limit):
    return pltpu.CompilerParams(vmem_limit_bytes=limit * MIB)


def cost(us):
    return pl.CostEstimate(flops=int(us * 1e9), bytes_accessed=int(us * 2e6), transcendentals=0)


def whole(shape):
    return pl.BlockSpec(shape, lambda i: (0,) * len(shape))


def project_kernel(x_ref, w_ref, b_ref, extra_ref, first_ref, second_ref, q_ref):
    w = w_ref[...].reshape(DIM, JW)
    q_ref[...] = jnp.zeros_like(q_ref)
    for r in range(NROW):
        tokens = x_ref[r].astype(F32).T.astype(BF)
        y = dot(tokens, w, 1, 0) + b_ref[...]
        q_ref[r * TOK : (r + 1) * TOK, :] = y[:, 0:256]
        out, at = (first_ref, r) if r < HALF else (second_ref, r - HALF)
        for h in range(3):
            kv = y[:, 256 + 128 * h : 384 + 128 * h].T.astype(BF)
            for j in range(PER_HEAD * h, PER_HEAD * (h + 1) + (1 if h == 2 else 0)):
                out[j, at * TOK : (at + 1) * TOK, :] = kv
    for j in range(NCOL):
        h, k = min(j, 14) // PER_HEAD, min(j, 14) % PER_HEAD
        lanes = slice(HDIM * h, HDIM * (h + 1))
        a = q_ref[SHARE * k : SHARE * k + 64, lanes]
        b = q_ref[SHARE * k + 64 : SHARE * k + 128, lanes]
        first_ref[j, 256:320, :] = jnp.concatenate([a, b], axis=1).astype(BF)
    second_ref[:, 256:352, :] = extra_ref[...]


def project(x4, wj, bias, extra):
    return pl.pallas_call(
        project_kernel,
        out_shape=(
            jax.ShapeDtypeStruct((NCOL, 320, 128), BF),
            jax.ShapeDtypeStruct((NCOL, 352, 128), BF),
        ),
        in_specs=[VMEM] * 4,
        out_specs=[VMEM] * 2,
        scratch_shapes=[pltpu.VMEM((640, 256), F32)],
        compiler_params=params(40),
        cost_estimate=cost(3),
        name="project",
    )(x4, wj, bias, extra)


def key_rows(seg_row):
    row = lax.broadcasted_iota(jnp.int32, (16, seg_row.shape[1]), 0)
    hot = jnp.where(row < 5, jnp.where(row == seg_row, 1.0, 0.0), jnp.where(row < 8, 1.0, 0.0))
    return hot.astype(BF)


def offset_columns(value, base):
    h, m, l = split3(-value)
    lane = lax.broadcasted_iota(jnp.int32, base.shape, 1)
    return jnp.where(
        lane == 5,
        h.astype(F32),
        jnp.where(lane == 6, m.astype(F32), jnp.where(lane == 7, l.astype(F32), base)),
    )


def key_block(kv_ref, seg_ref, count):
    kvt = jnp.concatenate(
        [kv_ref[c, r * TOK : (r + 1) * TOK, :] for c in range(count) for r in range(HALF)], axis=1
    )
    extra = jnp.concatenate([key_rows(seg_ref[0, i : i + 1, :]) for i in range(count * HALF)], axis=1)
    return kvt, extra


def unpack(block_ref, store):
    for c in range(NCOL):
        block = block_ref[c].astype(F32)
        store(SHARE * c, block[:, 0:64])
        store(SHARE * c + 64, block[0:TAIL, 64:128])


def forward_step(qa_ref, kv_ref, seg_ref, acc_ref, top_ref):
    kvt, extra = key_block(kv_ref, seg_ref, FWD_C)
    kt = jnp.concatenate([kvt[0:64], kvt[0:64], extra], axis=0)
    turned = kvt.astype(F32).T
    lane = lax.broadcasted_iota(jnp.int32, turned.shape, 1)
    va = jnp.where(lane >= 64, turned, jnp.where(lane == 0, 1.0, 0.0)).astype(BF)
    s = dot(qa_ref[...], kt, 1, 0)
    parts = [s[:, i * 128 : (i + 1) * 128] for i in range(s.shape[1] // 128)]
    high = parts[0]
    for part in parts[1:]:
        high = jnp.maximum(high, part)
    top = top_ref[...]
    raised = jnp.maximum(top, jnp.broadcast_to(jnp.max(high, axis=1, keepdims=True), top.shape))
    p = jnp.concatenate([jnp.exp2(part - raised).astype(BF) for part in parts], axis=1)
    fade = jnp.exp2(top - raised)
    top_ref[...] = raised
    acc_ref[...] = acc_ref[...] * fade + dot(p, va, 1, 0)


def attend_first_kernel(q_ref, kv_ref, segq_ref, seg_ref, qa_ref, acc_ref, top_ref, q_scr):
    @pl.when(pl.program_id(0) == 0)
    def _():
        def store(at, rows):
            q_scr[at : at + rows.shape[0], :] = rows

        unpack(q_ref, store)
        scaled = q_scr[...] * (LOG2E / 8.0)
        hi = scaled.astype(BF)
        lo = (scaled - hi.astype(F32)).astype(BF)
        lane = lax.broadcasted_iota(jnp.int32, (ROWS, 16), 1)
        pen = jnp.where((lane < 5) & (lane != segq_ref[...]), BLOCK_OUT, 0.0)
        qa_ref[...] = jnp.concatenate([hi, lo, pen.astype(BF)], axis=1)
        acc_ref[...] = jnp.zeros_like(acc_ref)
        top_ref[...] = jnp.full_like(top_ref, -3e38)

    forward_step(qa_ref, kv_ref, seg_ref, acc_ref, top_ref)


def attend_second_kernel(
    qa_in, acc_in, top_in, kv_ref, seg_ref, qa_ref, o_ref, out_ref, acc_ref, top_ref
):
    @pl.when(pl.program_id(0) == 0)
    def _():
        acc_ref[...] = acc_in[...]
        top_ref[...] = top_in[...]

    forward_step(qa_in, kv_ref, seg_ref, acc_ref, top_ref)

    @pl.when(pl.program_id(0) == pl.num_programs(0) - 1)
    def _():
        acc = acc_ref[...]
        total = acc[:, 0:1]
        o = acc[:, 64:128] / total
        o_ref[...] = o
        qa_ref[:, 0:128] = qa_in[:, 0:128]
        lse = top_ref[:, 0:1] + jnp.log(total) * LOG2E
        qa_ref[:, 128:144] = offset_columns(lse, qa_in[:, 128:144].astype(F32)).astype(BF)
        for c in range(NCOL):
            out_ref[c] = pack(o_ref, SHARE * c)


def pack(ref, at, scale=None):
    a = ref[at : at + 64, 0:64]
    b = jnp.concatenate([ref[at + 64 : at + SHARE, 0:64], jnp.zeros((64 - TAIL, 64), F32)], axis=0)
    both = jnp.concatenate([a, b], axis=1)
    if scale is not None:
        both = both * scale
    return both.astype(BF)


def attend(first, second, segq, seg_first, seg_second):
    steps = NCOL // FWD_C
    kinds = (
        jax.ShapeDtypeStruct((ROWS, AUG), BF),
        jax.ShapeDtypeStruct((ROWS, 128), F32),
        jax.ShapeDtypeStruct((ROWS, 128), F32),
    )
    seg_spec = pl.BlockSpec((1, FWD_C * HALF, TOK), lambda i: (i, 0, 0))
    state = pl.pallas_call(
        attend_first_kernel,
        grid=(steps,),
        out_shape=kinds,
        in_specs=[
            pl.BlockSpec((NCOL, 64, 128), lambda i: (0, 4, 0)),
            pl.BlockSpec((FWD_C, 256, 128), lambda i: (i, 0, 0)),
            whole((ROWS, 1)),
            seg_spec,
        ],
        out_specs=[whole((ROWS, AUG)), whole((ROWS, 128)), whole((ROWS, 128))],
        scratch_shapes=[pltpu.VMEM((ROWS, HDIM), F32)],
        compiler_params=params(58),
        cost_estimate=cost(10),
        name="attend_first",
    )(first, first, segq, seg_first)
    return pl.pallas_call(
        attend_second_kernel,
        grid=(steps,),
        out_shape=(
            kinds[0],
            jax.ShapeDtypeStruct((ROWS, HDIM), F32),
            jax.ShapeDtypeStruct((NCOL, 64, 128), BF),
        ),
        in_specs=[
            whole((ROWS, AUG)),
            whole((ROWS, 128)),
            whole((ROWS, 128)),
            pl.BlockSpec((FWD_C, 256, 128), lambda i: (i, 0, 0)),
            seg_spec,
        ],
        out_specs=[whole((ROWS, AUG)), whole((ROWS, HDIM)), whole((NCOL, 64, 128))],
        scratch_shapes=[pltpu.VMEM((ROWS, 128), F32), pltpu.VMEM((ROWS, 128), F32)],
        compiler_params=params(58),
        cost_estimate=cost(10),
        name="attend_second",
    )(*state, second, seg_second)


def backward_step(qa_ref, doa_ref, turned_ref, kv_ref, seg_ref, acc_ref):
    kvt, extra = key_block(kv_ref, seg_ref, BWD_C)
    kt = jnp.concatenate([kvt[0:64], kvt[0:64], extra], axis=0)
    vt = jnp.concatenate([kvt[64:128], extra], axis=0)
    keys = kvt.astype(F32).T.astype(BF)
    p = jnp.exp2(dot(qa_ref[...], kt, 1, 0))
    dp = dot(doa_ref[...], vt, 1, 0)
    ds = (p * dp).astype(BF)
    acc_ref[...] += dot(ds, keys, 1, 0)
    dk = dot(turned_ref[0:64, :], ds, 1, 0) * 0.125
    dv = dot(turned_ref[64:128, :], p.astype(BF), 1, 0)
    return jnp.concatenate([dk, dv], axis=0).astype(BF)


def store_keys(out_ref, at, both):
    for c in range(BWD_C):
        for r in range(HALF):
            i = c * HALF + r
            out_ref[at + c, r * TOK : (r + 1) * TOK, :] = both[:, i * TOK : (i + 1) * TOK]


def back_first_kernel(
    q_ref, do_ref, qa_ref, o_ref, fin_ref, kv_ref, seg_ref, out_ref, doa_ref, turned_ref, acc_ref, pair_scr
):
    @pl.when(pl.program_id(0) == 0)
    def _():
        def store_q(at, rows):
            pair_scr[at : at + rows.shape[0], 0:64] = rows

        def store_do(at, rows):
            pair_scr[at : at + rows.shape[0], 64:128] = rows

        unpack(q_ref, store_q)
        unpack(do_ref, store_do)
        pairs = pair_scr[...]
        turned_ref[...] = pairs.T.astype(BF)
        grad = pairs[:, 64:128]
        delta = jnp.sum(grad * o_ref[...], axis=1, keepdims=True)
        ext = offset_columns(delta, jnp.zeros((ROWS, 16), F32))
        doa_ref[...] = jnp.concatenate([grad.astype(BF), ext.astype(BF)], axis=1)
        acc_ref[...] = jnp.zeros_like(acc_ref)

    both = backward_step(qa_ref, doa_ref, turned_ref, kv_ref, seg_ref, acc_ref)
    store_keys(out_ref, 0, both)
    out_ref[:, 256:304, :] = fin_ref[...]


def back_second_kernel(qa_ref, doa_ref, turned_ref, acc_in, kv_ref, seg_ref, out_ref, acc_ref):
    step = pl.program_id(0)

    @pl.when(step == 0)
    def _():
        acc_ref[...] = acc_in[...]

    both = backward_step(qa_ref, doa_ref, turned_ref, kv_ref, seg_ref, acc_ref)
    store_keys(out_ref, step * BWD_C, both)

    @pl.when(step == pl.num_programs(0) - 1)
    def _():
        for c in range(NCOL):
            out_ref[c, 256:320, :] = pack(acc_ref, SHARE * c, 0.125)


SEG_BACK = pl.BlockSpec((1, BWD_C * HALF, TOK), lambda i: (i, 0, 0))
KEYS_BACK = pl.BlockSpec((BWD_C, 256, 128), lambda i: (i, 0, 0))
BACK_STEPS = NCOL // BWD_C


def attend_back_first(first, grad, qa, o, fin, seg_first):
    return pl.pallas_call(
        back_first_kernel,
        grid=(BACK_STEPS,),
        out_shape=(
            jax.ShapeDtypeStruct((NCOL, 304, 128), BF),
            jax.ShapeDtypeStruct((ROWS, 80), BF),
            jax.ShapeDtypeStruct((128, ROWS), BF),
            jax.ShapeDtypeStruct((ROWS, 128), F32),
        ),
        in_specs=[
            pl.BlockSpec((NCOL, 64, 128), lambda i: (0, 4, 0)),
            whole((NCOL, 64, 128)),
            whole((ROWS, AUG)),
            whole((ROWS, HDIM)),
            pl.BlockSpec((BWD_C, 48, 128), lambda i: (i, 0, 0)),
            KEYS_BACK,
            SEG_BACK,
        ],
        out_specs=[
            pl.BlockSpec((BWD_C, 304, 128), lambda i: (i, 0, 0)),
            whole((ROWS, 80)),
            whole((128, ROWS)),
            whole((ROWS, 128)),
        ],
        scratch_shapes=[pltpu.VMEM((ROWS, 128), F32)],
        compiler_params=params(58),
        cost_estimate=cost(18),
        name="attend_back_first",
    )(first, grad, qa, o, fin, first, seg_first)


def attend_back_second(qa, doa, turned, acc, second, seg_second):
    return pl.pallas_call(
        back_second_kernel,
        grid=(BACK_STEPS,),
        out_shape=jax.ShapeDtypeStruct((NCOL, 320, 128), BF),
        in_specs=[
            whole((ROWS, AUG)),
            whole((ROWS, 80)),
            whole((128, ROWS)),
            whole((ROWS, 128)),
            KEYS_BACK,
            SEG_BACK,
        ],
        out_specs=whole((NCOL, 320, 128)),
        scratch_shapes=[pltpu.VMEM((ROWS, 128), F32)],
        compiler_params=params(58),
        cost_estimate=cost(18),
        name="attend_back_second",
    )(qa, doa, turned, acc, second, seg_second)


def gather_rows(block_ref, scr, rows=slice(0, 64)):
    for j in range(15):
        h, k = j // PER_HEAD, j % PER_HEAD
        block = block_ref[j, rows, :].astype(F32)
        lanes = slice(HDIM * h, HDIM * (h + 1))
        scr[SHARE * k : SHARE * k + 64, lanes] = block[:, 0:64]
        scr[SHARE * k + 64 : SHARE * (k + 1), lanes] = block[0:TAIL, 64:128]


def to_row_kernel(got_ref, bias_ref, out_ref, scr):
    gather_rows(got_ref, scr)
    for r in range(NROW):
        out_ref[r, 0:TOK, :] = scr[r * TOK : (r + 1) * TOK, :].astype(BF)
        out_ref[r, TOK : TOK + 16, :] = bias_ref[...]


def to_row(got, bias_rows):
    return pl.pallas_call(
        to_row_kernel,
        out_shape=jax.ShapeDtypeStruct((NROW, TOK + 16, 192), BF),
        in_specs=[VMEM] * 2,
        out_specs=VMEM,
        scratch_shapes=[pltpu.VMEM((528, 192), F32)],
        cost_estimate=cost(1),
        compiler_params=params(16),
        name="to_row",
    )(got, bias_rows)


def to_col_kernel(got_ref, out_ref, scr):
    scr[512:640, :] = jnp.zeros((128, 192), F32)
    for r in range(NROW):
        scr[r * TOK : (r + 1) * TOK, :] = got_ref[r].astype(F32)
    for j in range(15):
        h, k = j // PER_HEAD, j % PER_HEAD
        lanes = slice(HDIM * h, HDIM * (h + 1))
        a = scr[SHARE * k : SHARE * k + 64, lanes]
        b = scr[SHARE * k + 64 : SHARE * k + 128, lanes]
        out_ref[j] = jnp.concatenate([a, b], axis=1).astype(BF)
    out_ref[15] = jnp.zeros((64, 128), BF)


def to_col(got):
    return pl.pallas_call(
        to_col_kernel,
        out_shape=jax.ShapeDtypeStruct((NCOL, 64, 128), BF),
        in_specs=[VMEM],
        out_specs=VMEM,
        scratch_shapes=[pltpu.VMEM((640, 192), F32)],
        cost_estimate=cost(1),
        compiler_params=params(16),
        name="to_col",
    )(got)


def feature_mean(v):
    return jnp.sum(v, axis=1, keepdims=True) * (1.0 / DIM)


def tokenwise_kernel(
    att_ref, x_ref, extra_ref, all_ref,
    sent_ref, datt_ref, fin_ref, dh1_ref,
    up_ref, down_ref, out_ref, slope_ref, act_ref, sems,
):
    copies = []
    for g in range(3):
        for k in range(2):
            for r in range(NROW):
                copies.append(
                    pltpu.make_async_copy(
                        all_ref.at[k, r, :, 96:112, g * 128 : (g + 1) * 128],
                        out_ref.at[k * NROW + r, :, 16 * g : 16 * (g + 1), :],
                        sems.at[0],
                    )
                )
    n_out = len(copies)
    for r in range(NROW):
        for k in range(2):
            lanes = slice(r * DIM + k * 384, r * DIM + (k + 1) * 384)
            copies.append(
                pltpu.make_async_copy(all_ref.at[k, r, :, 0:48, :], up_ref.at[:, :, lanes], sems.at[1 + r])
            )
    for r in range(NROW):
        for k in range(2):
            lanes = slice(r * DIM + k * 384, r * DIM + (k + 1) * 384)
            copies.append(
                pltpu.make_async_copy(all_ref.at[k, r, :, 48:96, :], down_ref.at[:, :, lanes], sems.at[5 + r])
            )
    for copy in copies:
        copy.start()

    def wait(group):
        chosen = copies[:n_out] if group == 0 else copies[n_out + 2 * (group - 1) : n_out + 2 * group]
        for copy in chosen:
            copy.wait()

    tok = x_ref[...].reshape(DIM, TOK).astype(F32).T
    cot = extra_ref[:, 256:304, :].reshape(DIM, TOK).astype(F32).T
    vecs = extra_ref[:, 304:352, :].reshape(DIM, TOK).astype(F32).T
    out_b, gain_1, shift_1, down_b, gain_2, shift_2 = [
        vecs[i : i + 1] + vecs[6 + i : 7 + i] + vecs[12 + i : 13 + i] for i in range(6)
    ]
    gap = jnp.zeros((TOK, 32), BF)

    wait(0)
    attn = jnp.zeros((TOK, DIM), F32)
    for r in range(NROW):
        rows = att_ref[r, 0:TOK, :]
        for k in range(2):
            piece = jnp.concatenate([rows[:, 96 * k : 96 * (k + 1)], gap], axis=1)
            attn = attn + dot(piece, out_ref[k * NROW + r].reshape(DIM, 128), 1, 1)
    h1 = tok + (attn + out_b)
    off = h1 - feature_mean(h1)
    inv1 = lax.rsqrt(feature_mean(off * off) + EPS)
    xhat1 = off * inv1
    n1 = xhat1 * gain_1 + shift_1
    n1_low = n1.astype(BF)

    branch = jnp.zeros((TOK, DIM), F32)
    for r in range(NROW):
        wait(1 + r)
        cols = slice(r * DIM, (r + 1) * DIM)
        parts = att_ref[r, TOK : TOK + 12, :].astype(F32)
        parts = parts[0:4] + parts[4:8] + parts[8:12]
        up_b = jnp.concatenate([parts[i : i + 1] for i in range(4)], axis=1)
        pre = dot(n1_low, up_ref[:, :, cols].reshape(DIM, DIM), 1, 0) + up_b
        phi = 0.5 * (1.0 + lax.erf(pre * (1.0 / math.sqrt(2.0))))
        act = (pre * phi).astype(BF)
        slope_ref[:, cols] = phi + pre * jnp.exp(-0.5 * pre * pre) * (1.0 / math.sqrt(2.0 * math.pi))
        for i in range(6):
            at = 3 * DIM + 48 + DIM + i * TOK
            sent_ref[r, at : at + TOK, :] = act[:, i * TOK : (i + 1) * TOK]
        wait(5 + r)
        branch = branch + dot(act, down_ref[:, :, cols].reshape(DIM, DIM), 1, 1)
    h2 = n1 + (branch + down_b)
    off = h2 - feature_mean(h2)
    inv2 = lax.rsqrt(feature_mean(off * off) + EPS)
    xhat2 = off * inv2
    fin_ref[...] = (xhat2 * gain_2 + shift_2).T.astype(BF).reshape(NCOL, 48, TOK)
    dx = cot * gain_2
    dh2 = inv2 * (dx - feature_mean(dx) - xhat2 * feature_mean(dx * xhat2))
    d_branch = dh2.astype(BF)

    back = jnp.zeros((TOK, DIM), F32)
    for r in range(NROW):
        cols = slice(r * DIM, (r + 1) * DIM)
        d_act = dot(d_branch, down_ref[:, :, cols].reshape(DIM, DIM), 1, 0)
        d_pre = (d_act * slope_ref[:, cols]).astype(BF)
        for i in range(6):
            at = 3 * DIM + 48 + i * TOK
            sent_ref[r, at : at + TOK, :] = d_pre[:, i * TOK : (i + 1) * TOK]
        back = back + dot(d_pre, up_ref[:, :, cols].reshape(DIM, DIM), 1, 1)
    up1 = dh2 + back
    dx = up1 * gain_1
    dh1 = inv1 * (dx - feature_mean(dx) - xhat1 * feature_mean(dx * xhat1))
    d_attn = dh1.astype(BF)
    for r in range(NROW):
        pieces = [dot(d_attn, out_ref[k * NROW + r].reshape(DIM, 128), 1, 0)[:, 0:96] for k in range(2)]
        datt_ref[r] = jnp.concatenate(pieces, axis=1).astype(BF)
    turned = dh1.T
    dh1_ref[...] = turned
    shared = [n1.T.astype(BF), dh2.T.astype(BF), turned.astype(BF)]
    sums = [
        jnp.sum(v, axis=0, keepdims=True) for v in (up1 * xhat1, up1, cot * xhat2, cot)
    ]
    rows = []
    for part in range(2):
        for v in sums:
            hi = v.astype(BF).astype(F32)
            piece = hi if part == 0 else v - hi
            rows += [piece[:, i * 128 : (i + 1) * 128] for i in range(6)]
    shared.append(jnp.concatenate(rows, axis=0).astype(BF))
    at = 0
    for v in shared:
        for r in range(NROW):
            sent_ref[r, at : at + v.shape[0], :] = v
        at += v.shape[0]


def tokenwise(att, x_t, extra, everything):
    return pl.pallas_call(
        tokenwise_kernel,
        out_shape=(
            jax.ShapeDtypeStruct((NROW, SENT, TOK), BF),
            jax.ShapeDtypeStruct((NROW, TOK, 192), BF),
            jax.ShapeDtypeStruct((NCOL, 48, TOK), BF),
            jax.ShapeDtypeStruct((DIM, TOK), F32),
        ),
        in_specs=[VMEM] * 3 + [pl.BlockSpec(memory_space=pl.ANY)],
        out_specs=[VMEM] * 4,
        scratch_shapes=[
            pltpu.VMEM((NCOL, 48, FF), BF),
            pltpu.VMEM((NCOL, 48, FF), BF),
            pltpu.VMEM((2 * NROW, NCOL, 48, 128), BF),
            pltpu.VMEM((TOK, FF), F32),
            pltpu.VMEM((TOK, FF), BF),
            pltpu.SemaphoreType.DMA((9,)),
        ],
        compiler_params=params(48),
        cost_estimate=cost(15),
        name="tokenwise",
    )(att, x_t, extra, everything)


def place(core, mine_ref, other_ref, blocks, half_rows):
    for at, block in blocks:
        low = at < half_rows
        local = at if low else at - half_rows
        rows = slice(local, local + block.shape[1])
        keep = core == (0 if low else 1)

        @pl.when(keep)
        def _():
            mine_ref[:, rows, :] = block

        @pl.when(jnp.logical_not(keep))
        def _():
            other_ref[:, rows, :] = block


def weight_grads_kernel(core_ref, got_ref, att_ref, mine_ref, other_ref):
    core = core_ref[0]

    def feats(at):
        return jnp.concatenate([got_ref[r, at : at + DIM, :] for r in range(NROW)], axis=1)

    def hidden(at):
        return jnp.concatenate(
            [
                jnp.concatenate([got_ref[r, at + i * TOK : at + (i + 1) * TOK, :] for i in range(6)], axis=1)
                for r in range(NROW)
            ],
            axis=0,
        )

    def chunks(g, count):
        return [g[:, i * 128 : (i + 1) * 128].astype(BF).reshape(NCOL, 48, 128) for i in range(count)]

    ones = jnp.ones((16, NROW * TOK), BF)
    d_pre = hidden(3 * DIM + 48)
    d_branch = feats(DIM)
    d_attn = feats(2 * DIM)
    att = jnp.concatenate([att_ref[r, 0:TOK, :] for r in range(NROW)], axis=0)
    att = jnp.concatenate([att, jnp.zeros((NROW * TOK, 64), BF)], axis=1)
    pieces = chunks(dot(feats(0), d_pre, 1, 0), 6)
    pieces += chunks(dot(d_branch, hidden(4 * DIM + 48), 1, 0), 6)
    pieces += chunks(dot(d_attn, att, 1, 0), 2)
    sums = [dot(ones, d_branch, 1, 1)[0:1], dot(ones, d_attn, 1, 1)[0:1], dot(ones, d_pre, 1, 0)[0:1]]
    norm = got_ref[0, 3 * DIM : 3 * DIM + 48, :].astype(F32)
    for r in range(1, NROW):
        norm = norm + got_ref[r, 3 * DIM : 3 * DIM + 48, :].astype(F32)
    rows = [norm[0:24] + norm[24:48]]
    for v in sums:
        rows += [v[:, i * 128 : (i + 1) * 128] for i in range(6)]
    rows.append(jnp.zeros((6, 128), F32))
    rows = jnp.concatenate(rows, axis=0)
    hi = rows.astype(BF)
    lo = (rows - hi.astype(F32)).astype(BF)
    misc = jnp.concatenate([hi, lo], axis=0)
    blocks = [(48 * i, piece) for i, piece in enumerate(pieces)]
    blocks.append((672, jnp.broadcast_to(misc[None], (NCOL, 96, 128))))
    place(core, mine_ref, other_ref, blocks, WROWS // 2)


def weight_grads(core, got, att):
    kind = jax.ShapeDtypeStruct((NCOL, WROWS // 2, 128), BF)
    return pl.pallas_call(
        weight_grads_kernel,
        out_shape=(kind, kind),
        in_specs=[pl.BlockSpec(memory_space=pltpu.SMEM)] + [VMEM] * 2,
        out_specs=[VMEM] * 2,
        compiler_params=params(48),
        cost_estimate=cost(5),
        name="weight_grads",
    )(core, got, att)


def project_back_kernel(
    core_ref, first_ref, second_ref, w_ref, x_ref, din_ref, mine_ref, other_ref, scr
):
    core = core_ref[0]
    scr[...] = jnp.zeros_like(scr)
    gather_rows(second_ref, scr, slice(256, 320))
    dq = scr[0:512, :].T.astype(BF)
    w = w_ref[...].reshape(DIM, JW)
    grad = jnp.zeros((DIM, JW), F32)
    total = jnp.zeros((16, JW), F32)
    ones = jnp.ones((16, TOK), BF)
    for r in range(NROW):
        source, at = (first_ref, r) if r < HALF else (second_ref, r - HALF)
        parts = [dq[:, r * TOK : (r + 1) * TOK]]
        for h in range(3):
            acc = source[PER_HEAD * h, at * TOK : (at + 1) * TOK, :].astype(F32)
            for k in range(1, PER_HEAD):
                acc = acc + source[PER_HEAD * h + k, at * TOK : (at + 1) * TOK, :].astype(F32)
            parts.append(acc.astype(BF))
        d_proj = jnp.concatenate(parts, axis=0)
        din_ref[r] = dot(w, d_proj, 1, 0).astype(BF)
        grad = grad + dot(x_ref[r], d_proj, 1, 1)
        total = total + dot(ones, d_proj, 1, 1)
    rows = [total[0:1, i * 128 : (i + 1) * 128] for i in range(5)] + [jnp.zeros((3, 128), F32)]
    rows = jnp.concatenate(rows, axis=0)
    hi = rows.astype(BF)
    lo = (rows - hi.astype(F32)).astype(BF)
    misc = jnp.broadcast_to(jnp.concatenate([hi, lo], axis=0)[None], (NCOL, 16, 128))
    low = grad.astype(BF)
    pieces = [low[:, i * 128 : (i + 1) * 128].reshape(NCOL, 48, 128) for i in range(5)]
    blocks = [(0, pieces[0]), (48, pieces[1]), (96, pieces[2][:, 0:32]), (128, pieces[2][:, 32:48])]
    blocks += [(144, pieces[3]), (192, pieces[4]), (240, misc)]
    place(core, mine_ref, other_ref, blocks, 128)


def project_back(core, first, second, wj, x4):
    kind = jax.ShapeDtypeStruct((NCOL, 128, 128), BF)
    return pl.pallas_call(
        project_back_kernel,
        out_shape=(jax.ShapeDtypeStruct((NROW, DIM, TOK), BF), kind, kind),
        in_specs=[pl.BlockSpec(memory_space=pltpu.SMEM)] + [VMEM] * 4,
        out_specs=[VMEM] * 3,
        scratch_shapes=[pltpu.VMEM((528, 256), F32)],
        compiler_params=params(48),
        cost_estimate=cost(5),
        name="project_back",
    )(core, first, second, wj, x4)


def last_kernel(mine_ref, theirs_ref, din_ref, dh1_ref, out_ref):
    out_ref[:, 0:128, :] = (mine_ref[...].astype(F32) + theirs_ref[...].astype(F32)).astype(BF)
    total = dh1_ref[...]
    for r in range(NROW):
        total = total + din_ref[r].astype(F32)
    out_ref[:, 128:176, :] = total.astype(BF).reshape(NCOL, 48, TOK)


def last_payload(mine, theirs, din, dh1):
    return pl.pallas_call(
        last_kernel,
        out_shape=jax.ShapeDtypeStruct((NCOL, 176, 128), BF),
        in_specs=[VMEM] * 4,
        out_specs=VMEM,
        compiler_params=params(24),
        cost_estimate=cost(1),
        name="last_payload",
    )(mine, theirs, din, dh1)


def exchange(blocks, axis):
    return lax.all_to_all(blocks, axis, 0, 0, tiled=True)


def swap_cores(v):
    return lax.ppermute(v, "dp", [(0, 1), (1, 0)])


def pair(core, v):
    theirs = swap_cores(v)
    return jnp.where(core == 0, jnp.concatenate([v, theirs]), jnp.concatenate([theirs, v]))


def per_device(
    inputs,
    segments,
    joint_weight,
    joint_bias,
    output_weight,
    output_bias,
    first_norm_gain,
    shift_first,
    up_weight,
    up_bias,
    down_weight,
    down_bias,
    second_norm_gain,
    second_norm_shift,
    cotangent,
):
    core = lax.axis_index("dp")
    col = lax.axis_index("col")
    core_word = core.reshape(1).astype(jnp.int32)

    def by_col(a):
        return jnp.transpose(a.reshape(48, NCOL, TOK), (1, 0, 2))

    x_t = exchange(by_col(inputs), "col")
    jw = joint_weight.reshape(48, 3, 3, HDIM)
    jw = jnp.concatenate(
        [jw[:, :, 0].reshape(48, 192), jnp.zeros((48, 64), BF), jw[:, :, 1:].reshape(48, 384)], axis=1
    )
    x_t, jw = lax.optimization_barrier((x_t, jw))
    wj = exchange(jnp.broadcast_to(jw[None], (NCOL, 48, JW)), "col")
    x4 = lax.all_gather(x_t.reshape(DIM, TOK), "row", axis=0, tiled=False)

    turned = lax.dynamic_slice_in_dim(output_weight, core * 96, 96, 0).T
    turned = jnp.pad(turned, ((0, 0), (0, 32))).reshape(3, 16, 128)
    turned = jnp.transpose(turned, (1, 0, 2)).reshape(16, 384)
    shard = jnp.concatenate(
        [
            lax.dynamic_slice_in_dim(up_weight, core * 384, 384, 1),
            lax.dynamic_slice_in_dim(down_weight, core * 384, 384, 1),
            turned,
        ],
        axis=0,
    )
    everything = lax.all_gather(shard, ("dp", "row", "col"), axis=0, tiled=False)
    everything = everything.reshape(2, NROW, NCOL, 112, 384)

    vectors = jnp.stack(
        [output_bias, first_norm_gain, shift_first, down_bias, second_norm_gain, second_norm_shift], axis=1
    )
    vectors = jnp.pad(jnp.concatenate(split3(vectors), axis=1), ((0, 0), (0, 110)))
    extra = jnp.concatenate(
        [by_col(cotangent), jnp.broadcast_to(vectors[None], (NCOL, 48, 128))], axis=1
    )
    bias3 = joint_bias.reshape(3, 2, HDIM)
    bias = jnp.concatenate(
        [
            bias3[:, 0].reshape(192),
            jnp.zeros((64,), F32),
            jnp.concatenate([jnp.zeros((3, HDIM), F32), bias3[:, 1]], axis=1).reshape(384),
        ]
    ).reshape(1, JW)
    bias_rows = jnp.pad(jnp.concatenate([v.reshape(4, 192) for v in split3(up_bias)]), ((0, 4), (0, 0)))
    seg_k = jnp.transpose(segments.reshape(NROW, NCOL, TOK), (1, 0, 2))
    seg_rows = jnp.pad(seg_k.reshape(NCOL, 512), ((0, 0), (0, 8)))
    seg_q = lax.dynamic_slice_in_dim(seg_rows, lax.rem(col, PER_HEAD) * SHARE, SHARE, 1)
    seg_q = seg_q.reshape(ROWS, 1)
    seg_a = seg_k[:, :HALF]
    seg_b = seg_k[:, HALF:]

    first, second = project(x4, wj, bias, extra)
    first = exchange(first, "col")
    second = exchange(second, "col")
    by_step = lambda s, n: s.reshape(NCOL // n, n * HALF, TOK)
    qa, o, o_blocks = attend(first, second, seg_q, by_step(seg_a, FWD_C), by_step(seg_b, FWD_C))

    att_r = to_row(exchange(o_blocks, "col"), bias_rows)
    att = exchange(att_r, "row")
    sent, d_att, fin, dh1 = tokenwise(att, x_t, second, everything)

    grad_o = exchange(to_col(exchange(d_att, "row")), "col")
    got = exchange(sent, "row")
    back_a, doa, turned_qd, acc = attend_back_first(first, grad_o, qa, o, fin, by_step(seg_a, BWD_C))
    back_a = exchange(back_a, "col")
    mine, other = weight_grads(core_word, got, att_r)
    theirs = swap_cores(other)
    acc, mine = lax.optimization_barrier((acc, mine))
    back_b = attend_back_second(qa, doa, turned_qd, acc, second, by_step(seg_b, BWD_C))
    back_b, theirs = lax.optimization_barrier((back_b, theirs))
    back_b = exchange(back_b, "col")
    wide = (mine.astype(F32) + theirs.astype(F32)).astype(BF)
    wide = exchange(wide, "col")

    din, mine_j, other_j = project_back(core_word, back_a, back_b, wj, x4)
    theirs_j = swap_cores(other_j)
    din = exchange(din, "row")
    mixed = exchange(last_payload(mine_j, theirs_j, din, dh1), "col")

    layer_output = jnp.transpose(back_a[:, 256:304], (1, 0, 2)).reshape(48, 2048)
    wide = pair(core, jnp.sum(wide.astype(F32), axis=0))
    as_cols = lambda v, n: jnp.transpose(v.reshape(n, 48, 128), (1, 0, 2)).reshape(48, n * 128)
    grad_up = as_cols(wide[0:288], 6)
    grad_down = as_cols(wide[288:576], 6)
    grad_out = as_cols(wide[576:672], 2)[:, :192].T
    vecs = (wide[672:720] + wide[720:768])[:42].reshape(7, DIM)
    own = lax.dynamic_slice_in_dim(vecs[:6], col * 48, 48, 1)
    grad_up_bias = vecs[6]

    grad_inputs = jnp.transpose(mixed[:, 128:].astype(F32), (1, 0, 2)).reshape(48, 2048)
    last = pair(core, jnp.sum(mixed[:, :128].astype(F32), axis=0))
    gj = as_cols(last[0:240], 5)
    gj_q = gj[:, :192].reshape(48, 3, 1, HDIM)
    gj_kv = gj[:, 256:].reshape(48, 3, 2, HDIM)
    grad_joint = jnp.concatenate([gj_q, gj_kv], axis=2).reshape(48, 576)
    bj = (last[240:245] + last[248:253]).reshape(JW)
    bj = jnp.concatenate([bj[:192].reshape(3, 1, HDIM), bj[256:].reshape(3, 2, HDIM)[:, 1:]], axis=1)
    grad_joint_bias = bj.reshape(384)

    return (
        layer_output,
        grad_inputs,
        grad_joint,
        grad_joint_bias,
        grad_out,
        own[5],
        own[0],
        own[1],
        grad_up,
        grad_up_bias,
        grad_down,
        own[4],
        own[2],
        own[3],
    )


def solution(mesh):
    grid = P("col", ("dp", "row"))
    block = P("col", "row")
    return jax.shard_map(
        per_device,
        mesh=mesh,
        in_specs=(
            grid, P("dp", None), block, P("row"), P("row", "col"), P("col"), P("col"), P("col"),
            block, P("row"), block, P("col"), P("col"), P("col"), grid,
        ),
        out_specs=(
            grid, grid, block, P("row"), P("row", "col"), P("col"), P("col"), P("col"),
            block, P("row"), block, P("col"), P("col"), P("col"),
        ),
        check_vma=False,
    )
```

time: 540 us -> 355 us (0.66); the launches traced: 530 us -> 354 us
  local copies, waits for them, and re-layouts: 147 us -> 18.3 us
  blocking collectives: 21.7 us -> 67.8 us
  waiting for transfers between devices: 129 us -> 84.8 us
  other arithmetic: 37.2 us -> 6.53 us
  matrix products: 25.7 us -> 0 us
  Pallas kernels: 72.7 us -> 89.7 us
  starting transfers between devices: 80.3 us -> 71.8 us
    all_to_all x1 -> x4, blocking collectives: 9.19 us -> 55.6 us  [exchange(): return lax.all_to_all(blocks, axis, 0, 0, tiled=True)]
    all_to_all x11 -> x10, waiting for transfers between devices: 129 us -> 83.6 us  [exchange(): return lax.all_to_all(blocks, axis, 0, 0, tiled=True)]
    reshape x21 -> x18, local copies, waits for them, and re-layouts: 39.2 us -> 5.28 us  [the longest x4 1.36 us: per_device(): jnp.transpose(v.reshape(n, 48, 128), (1, 0, 2)).reshape(48, n * 128)]
    unnamed x97 -> x57, local copies, waits for them, and re-layouts: 33.3 us -> 3.88 us
    dot_general x13 -> x0, matrix products: 25.7 us -> none  [the longest x6 10.7 us: dot(): lax.dot_general(a, b, (((ca,), (cb,)), ((), ())), preferred_element_type=...]
    slice x26 -> x16, local copies, waits for them, and re-layouts: 25.7 us -> 1.8 us  [the longest x1 0.74 us: per_device(): grad_down = as_cols(wide[288:576], 6)]
    pallas_call x2 -> x11, Pallas kernels: 72.7 us -> 89.7 us  [the longest x1 20.6 us: attend_back_first(): pl.pallas_call(back_first_kernel, grid=(BACK_STEPS,), out_shape=(jax.Shap...]
    convert_element_type x16 -> x3, other arithmetic: 16 us -> 2.97 us  [the longest x1 2.96 us: per_device(): wide = (mine.astype(F32) + theirs.astype(F32)).astype(BF)]
  transfers between devices with their start and end apart: 16 -> 15, of which waited for: 12 -> 12; matrix products, arithmetic and copies ran while one was open for 29% -> 5% of each run, Pallas kernels for 7% -> 22%
where the time goes in v2:
time: 355 us; the launch traced here: 354 us
  Pallas kernels  89.7 us (25%)
  waiting for transfers between devices  84.8 us (24%)
  starting transfers between devices  71.8 us (20%)
  blocking collectives  67.8 us (19%)
  local copies, waits for them, and re-layouts  18.3 us (5%)
  between operations  14.6 us (4%)
  other arithmetic  6.53 us (2%)
    all_to_all x10, waiting for transfers between devices, exchange(): return lax.all_to_all(blocks, axis, 0, 0, tiled=True)  83.6 us
    all_to_all x4, blocking collectives, exchange(): return lax.all_to_all(blocks, axis, 0, 0, tiled=True)  55.6 us
    all_to_all x10, starting transfers between devices, exchange(): return lax.all_to_all(blocks, axis, 0, 0, tiled=True)  51.4 us
    pallas_call x1, Pallas kernels, attend_back_first(): pl.pallas_call(back_first_kernel, grid=(BACK_STEPS,), out_shape=(jax.Shap...  20.6 us
    ppermute x4, starting transfers between devices, swap_cores(): return lax.ppermute(v, 'dp', [(0, 1), (1, 0)])  20.4 us
    pallas_call x1, Pallas kernels, attend_back_second(): pl.pallas_call(back_second_kernel, grid=(BACK_STEPS,), out_shape=jax.Shap...  19.5 us
    pallas_call x1, Pallas kernels, attend(): pl.pallas_call(attend_second_kernel, grid=(steps,), out_shape=(kinds[0],...  12.7 us
    all_gather x1, blocking collectives, per_device(): x4 = lax.all_gather(x_t.reshape(DIM, TOK), 'row', axis=0, tiled=False)  12.2 us
  transfers between devices with their start and end apart: 15, of which 12 were waited for; matrix products, arithmetic and copies ran while one was open for 5% of the time, Pallas kernels for 22%

profile of v2, /device:TPU:1, one launch (start us, length us, event | category | flops | bytes accessed | tf_op | source)
XLA Modules:
  0.0 353.6 jit_solution(15163940700744274705)
XLA Ops:
  10.4 8.6 %all-to-all-start = ((bf16[16,48,128]{2,1,0:T(8,128)(2,1)}), bf16[16,48,128]{2,1,0:T(8,128)(2,1)S(1)}, u32[]{:S(2)}, u32[]{:S(2)}) async-start(bf16[16,48,128]{2,1,0:T(8,128)(2,1)} %bitcast_bitcast_fusion.1), calls=%async_computation | async-start | bytes 393216 | tf_op jit(solution)/shard_map/all_to_all | solution.py:714
  20.8 5.4 %all-to-all-done.x_ref = bf16[16,48,128]{2,1,0:T(8,128)(2,1)S(1)} async-done(((bf16[16,48,128]{2,1,0:T(8,128)(2,1)}), bf16[16,48,128]{2,1,0:T(8,128)(2,1)S(1)}, u32[]{:S(2)}, u32[]{:S(2)}) %all-to-all-start) | async-done | bytes 196640 | tf_op jit(solution)/shard_map/all_to_all | solution.py:714
  27.3 3.6 %all-to-all-start.1 = ((bf16[16,48,640]{2,1,0:T(8,128)(2,1)}), bf16[16,48,640]{2,1,0:T(8,128)(2,1)S(1)}, u32[]{:S(2)}, u32[]{:S(2)}) async-start(bf16[16,48,640]{2,1,0:T(8,128)(2,1)} %broadcast_in_dim.9), calls=%async_computation.1 | async-start | bytes 1966080 | tf_op jit(solution)/shard_map/all_to_all | solution.py:714
  31.4 12.2 %all_gather.9.x_ref = bf16[4,768,128]{2,1,0:T(8,128)(2,1)S(1)} all-gather(bf16[1,768,128]{2,1,0:T(8,128)(2,1)S(1)} %bitcast.104), channel_id=1, replica_groups=mesh['dp'=2,'row'=4,'col'=16] {'row'}, dimensions={0}, use_global_device_ids=true | all-gather | bytes 983040 | tf_op jit(solution)/shard_map/all_gather | solution.py:757
  47.8 24.5 %all_to_all.70.q_ref.kv_ref = bf16[16,320,128]{2,1,0:T(8,128)(2,1)} all-to-all(bf16[16,320,128]{2,1,0:T(8,128)(2,1)S(1)} %get-tuple-element.43), channel_id=1, replica_groups=mesh['dp'=2,'row'=4,'col'=16] {'col'}, dimensions={0} | all-to-all | bytes 2621440 | tf_op jit(solution)/shard_map/all_to_all | solution.py:714
  72.3 3.8 %all-to-all-start.3 = ((bf16[16,352,128]{2,1,0:T(8,128)(2,1)}), bf16[16,352,128]{2,1,0:T(8,128)(2,1)S(1)}, u32[]{:S(2)}, u32[]{:S(2)}) async-start(bf16[16,352,128]{2,1,0:T(8,128)(2,1)} %get-tuple-element.47), calls=%async_computation.3 | async-start | bytes 2883584 | tf_op jit(solution)/shard_map/all_to_all | solution.py:714
  78.1 11.4 %attend_first.1 = (bf16[1664,144]{1,0:T(8,128)(2,1)}, f32[1664,128]{1,0:T(8,128)}, f32[1664,128]{1,0:T(8,128)}) custom-call(bf16[16,320,128]{2,1,0:T(8,128)(2,1)} %all_to_all.70.q_ref.kv_ref, bf16[16,320,128]{2,1,0:T(8,128)(2,1)} %all_to_all.70.q_ref.kv_ref, s32[1664,1]{1,0:T(8,128)} %reshape.193.segq_ref, s32[4,8,128]{2,1,0:T(8,128)} %bitcast.123), custom_call_target="tpu_custom_call" | custom-call | flops 10000000000 | bytes 20000000 | tf_op jit(solution)/shard_map/attend_first/pallas_call | solution.py:207
  89.6 11.8 %all-to-all-done.3.kv_ref.extra_ref = bf16[16,352,128]{2,1,0:T(8,128)(2,1)S(1)} async-done(((bf16[16,352,128]{2,1,0:T(8,128)(2,1)}), bf16[16,352,128]{2,1,0:T(8,128)(2,1)S(1)}, u32[]{:S(2)}, u32[]{:S(2)}) %all-to-all-start.3) | async-done | bytes 1441824 | tf_op jit(solution)/shard_map/all_to_all | solution.py:714
  102.5 12.7 %attend_second.1 = (bf16[1664,144]{1,0:T(8,128)(2,1)}, f32[1664,64]{1,0:T(8,128)}, bf16[16,64,128]{2,1,0:T(8,128)(2,1)}) custom-call(bf16[1664,144]{1,0:T(8,128)(2,1)} %get-tuple-element.44.qa_in, f32[1664,128]{1,0:T(8,128)} %get-tuple-element.45.acc_in, f32[1664,128]{1,0:T(8,128)} %get-tuple-element.46.top_in, bf16[16,352,128]{2,1,0:T(8,128)(2,1)} %copy-done.1, ...), custom_call_target="tpu_custom_call" | custom-call | flops 10000000000 | bytes 20000000 | tf_op jit(solution)/shard_map/attend_second/pallas_call | solution.py:223
  115.3 3.5 all-to-all-start.4
  119.1 7.2 %all-to-all-done.4.got_ref = bf16[16,64,128]{2,1,0:T(8,128)(2,1)S(1)} async-done(((bf16[16,64,128]{2,1,0:T(8,128)(2,1)}), bf16[16,64,128]{2,1,0:T(8,128)(2,1)S(1)}, u32[]{:S(2)}, u32[]{:S(2)}) %all-to-all-start.4) | async-done | bytes 262176 | tf_op jit(solution)/shard_map/all_to_all | solution.py:714
  126.4 12.7 %all_to_all.71.att_ref = bf16[4,144,192]{2,1,0:T(8,128)(2,1)S(1)} all-to-all(bf16[4,144,192]{2,1,0:T(8,128)(2,1)S(1)} %to_row.1.att_ref), channel_id=1, replica_groups=mesh['dp'=2,'row'=4,'col'=16] {'row'}, dimensions={0} | all-to-all | bytes 442368 | tf_op jit(solution)/shard_map/all_to_all | solution.py:714
  139.2 12.1 %tokenwise.1 = (bf16[4,3888,128]{2,1,0:T(8,128)(2,1)}, bf16[4,128,192]{2,1,0:T(8,128)(2,1)S(1)}, bf16[16,48,128]{2,1,0:T(8,128)(2,1)S(1)}, f32[768,128]{1,0:T(8,128)S(1)}) custom-call(bf16[4,144,192]{2,1,0:T(8,128)(2,1)S(1)} %all_to_all.71.att_ref, bf16[16,48,128]{2,1,0:T(8,128)(2,1)S(1)} %all-to-all-done.x_ref, bf16[16,352,128]{2,1,0:T(8,128)(2,1)S(1)} %copy-done.2, ...), custom_call_target="tpu_custom_call" | custom-call | flops 15000000512 | bytes 30000000 | tf_op jit(solution)/shard_map/tokenwise/pallas_call | solution.py:547
  151.5 7.5 %all_to_all.72 = bf16[4,128,192]{1,2,0:T(8,128)(2,1)S(1)} all-to-all(bf16[4,128,192]{1,2,0:T(8,128)(2,1)S(1)} %copy.67), channel_id=1, replica_groups=mesh['dp'=2,'row'=4,'col'=16] {'row'}, dimensions={0} | all-to-all | bytes 393216 | tf_op jit(solution)/shard_map/all_to_all | solution.py:714
  159.4 10.8 %all_to_all.73.do_ref = bf16[16,64,128]{2,1,0:T(8,128)(2,1)} all-to-all(bf16[16,64,128]{2,1,0:T(8,128)(2,1)S(1)} %to_col.1), channel_id=1, replica_groups=mesh['dp'=2,'row'=4,'col'=16] {'col'}, dimensions={0} | all-to-all | bytes 524288 | tf_op jit(solution)/shard_map/all_to_all | solution.py:714
  170.2 4.9 %all-to-all-start.9 = ((bf16[4,3888,128]{2,1,0:T(8,128)(2,1)}), bf16[4,3888,128]{2,1,0:T(8,128)(2,1)}, u32[]{:S(2)}, u32[]{:S(2)}) async-start(bf16[4,3888,128]{2,1,0:T(8,128)(2,1)} %get-tuple-element.57), calls=%async_computation.9 | async-start | bytes 7962624 | tf_op jit(solution)/shard_map/all_to_all | solution.py:714
  175.1 20.6 %attend_back_first.1 = (bf16[16,304,128]{2,1,0:T(8,128)(2,1)}, bf16[1664,80]{1,0:T(8,128)(2,1)}, bf16[128,1664]{1,0:T(8,128)(2,1)}, f32[1664,128]{1,0:T(8,128)}) custom-call(bf16[16,320,128]{2,1,0:T(8,128)(2,1)} %all_to_all.70.q_ref.kv_ref, bf16[16,64,128]{2,1,0:T(8,128)(2,1)} %all_to_all.73.do_ref, bf16[1664,144]{1,0:T(8,128)(2,1)} %get-tuple-element.50.qa_ref, ...), custom_call_target="tpu_custom_call" | custom-call | flops 17999998976 | bytes 36000000 | tf_op jit(solution)/shard_map/attend_back_first/pallas_call | solution.py:315
  195.7 12.3 %all-to-all-done.9.got_ref = bf16[4,3888,128]{2,1,0:T(8,128)(2,1)} async-done(((bf16[4,3888,128]{2,1,0:T(8,128)(2,1)}), bf16[4,3888,128]{2,1,0:T(8,128)(2,1)}, u32[]{:S(2)}, u32[]{:S(2)}) %all-to-all-start.9) | async-done | bytes 3981344 | tf_op jit(solution)/shard_map/all_to_all | solution.py:714
  208.0 3.9 %all-to-all-start.8 = ((bf16[16,304,128]{2,1,0:T(8,128)(2,1)}), bf16[16,304,128]{2,1,0:T(8,128)(2,1)S(1)}, u32[]{:S(2)}, u32[]{:S(2)}) async-start(bf16[16,304,128]{2,1,0:T(8,128)(2,1)} %get-tuple-element.53), calls=%async_computation.8 | async-start | bytes 2490368 | tf_op jit(solution)/shard_map/all_to_all | solution.py:714
  211.9 4.8 %weight_grads.1 = (bf16[16,384,128]{2,1,0:T(8,128)(2,1)S(1)}, bf16[16,384,128]{2,1,0:T(8,128)(2,1)S(1)}) custom-call(s32[1]{0:T(128)} %bitcast.20.core_ref, bf16[4,3888,128]{2,1,0:T(8,128)(2,1)} %all-to-all-done.9.got_ref, bf16[4,144,192]{2,1,0:T(8,128)(2,1)S(1)} %to_row.1.att_ref), custom_call_target="tpu_custom_call" | custom-call | flops 5000000000 | bytes 10000000 | tf_op jit(solution)/shard_map/weight_grads/pallas_call | solution.py:633
  216.7 14.7 %collective-permute-start = (bf16[16,384,128]{2,1,0:T(8,128)(2,1)S(1)}, bf16[16,384,128]{2,1,0:T(8,128)(2,1)}, u32[]{:S(2)}, u32[]{:S(2)}) collective-permute-start(bf16[16,384,128]{2,1,0:T(8,128)(2,1)S(1)} %get-tuple-element.60), channel_id=1, source_target_pairs={{0,64},{64,0},{1,65},{65,1},{2,66},{66,2},{3,67},{67,3},{4,68},{68... | collective-permute-start | bytes 4718600 | tf_op jit(solution)/shard_map/ppermute | solution.py:718
  231.4 19.5 %attend_back_second.1 = bf16[16,320,128]{2,1,0:T(8,128)(2,1)} custom-call(bf16[1664,144]{1,0:T(8,128)(2,1)} %get-tuple-element.50.qa_ref, bf16[1664,80]{1,0:T(8,128)(2,1)} %get-tuple-element.54.doa_ref, bf16[128,1664]{1,0:T(8,128)(2,1)} %get-tuple-element.55.turned_ref, f32[1664,128]{1,0:T(8,128)} %get-tuple-element.59.acc_in, ...), custom_call_target="tpu_custom_call" | custom-call | flops 17999998976 | bytes 36000000 | tf_op jit(solution)/shard_map/attend_back_second/pallas_call | solution.py:347
  250.9 6.7 %all-to-all-start.10 = ((bf16[16,320,128]{2,1,0:T(8,128)(2,1)}), bf16[16,320,128]{2,1,0:T(8,128)(2,1)}, u32[]{:S(2)}, u32[]{:S(2)}) async-start(bf16[16,320,128]{2,1,0:T(8,128)(2,1)} %attend_back_second.1), calls=%async_computation.10 | async-start | bytes 2621440 | tf_op jit(solution)/shard_map/all_to_all | solution.py:714
  257.7 3.0 add_convert_fusion
  260.6 18.7 %all-to-all-done.10.second_ref = bf16[16,320,128]{2,1,0:T(8,128)(2,1)} async-done(((bf16[16,320,128]{2,1,0:T(8,128)(2,1)}), bf16[16,320,128]{2,1,0:T(8,128)(2,1)}, u32[]{:S(2)}, u32[]{:S(2)}) %all-to-all-start.10) | async-done | bytes 1310752 | tf_op jit(solution)/shard_map/all_to_all | solution.py:714
  279.3 4.4 %all-to-all-start.13 = ((bf16[16,384,128]{2,1,0:T(8,128)(2,1)}), bf16[16,384,128]{2,1,0:T(8,128)(2,1)}, u32[]{:S(2)}, u32[]{:S(2)}) async-start(bf16[16,384,128]{2,1,0:T(8,128)(2,1)} %add_convert_fusion), calls=%async_computation.13 | async-start | bytes 3145728 | tf_op jit(solution)/shard_map/all_to_all | solution.py:714
  283.7 5.0 %project_back.1 = (bf16[4,768,128]{2,1,0:T(8,128)(2,1)}, bf16[16,128,128]{2,1,0:T(8,128)(2,1)S(1)}, bf16[16,128,128]{2,1,0:T(8,128)(2,1)S(1)}) custom-call(s32[1]{0:T(128)} %bitcast.20.core_ref, bf16[16,304,128]{2,1,0:T(8,128)(2,1)S(1)} %all-to-all-done.8.first_ref, bf16[16,320,128]{2,1,0:T(8,128)(2,1)} %all-to-all-done.10.second_ref, ...), custom_call_target="tpu_custom_call" | custom-call | flops 5000000000 | bytes 10000000 | tf_op jit(solution)/shard_map/project_back/pallas_call | solution.py:681
  290.3 15.7 %all-to-all-done.13 = bf16[16,384,128]{2,1,0:T(8,128)(2,1)} async-done(((bf16[16,384,128]{2,1,0:T(8,128)(2,1)}), bf16[16,384,128]{2,1,0:T(8,128)(2,1)}, u32[]{:S(2)}, u32[]{:S(2)}) %all-to-all-start.13) | async-done | bytes 1572896 | tf_op jit(solution)/shard_map/all_to_all | solution.py:714
  306.0 3.6 %all-to-all-start.11 = ((bf16[4,768,128]{2,1,0:T(8,128)(2,1)}), bf16[4,768,128]{2,1,0:T(8,128)(2,1)S(1)}, u32[]{:S(2)}, u32[]{:S(2)}) async-start(bf16[4,768,128]{2,1,0:T(8,128)(2,1)} %get-tuple-element.64), calls=%async_computation.11 | async-start | bytes 1572864 | tf_op jit(solution)/shard_map/all_to_all | solution.py:714
  311.3 3.1 collective-permute-start.3
  320.7 8.2 %all-to-all-start.12 = ((bf16[16,176,128]{2,1,0:T(8,128)(2,1)}), bf16[16,176,128]{2,1,0:T(8,128)(2,1)S(1)}, u32[]{:S(2)}, u32[]{:S(2)}) async-start(bf16[16,176,128]{2,1,0:T(8,128)(2,1)} %last_payload.1), calls=%async_computation.12 | async-start | bytes 1441792 | tf_op jit(solution)/shard_map/all_to_all | solution.py:714
  332.1 8.9 %all-to-all-done.12 = bf16[16,176,128]{2,1,0:T(8,128)(2,1)S(1)} async-done(((bf16[16,176,128]{2,1,0:T(8,128)(2,1)}), bf16[16,176,128]{2,1,0:T(8,128)(2,1)S(1)}, u32[]{:S(2)}, u32[]{:S(2)}) %all-to-all-start.12) | async-done | bytes 720928 | tf_op jit(solution)/shard_map/all_to_all | solution.py:714
  (149 shorter events, 32.7 us)
Async XLA Ops:
  7.2 13.4 %copy-start.19 = (f32[384]{0:T(512)S(1)}, f32[384]{0:T(512)}, u32[]{:S(2)}) copy-start(f32[384]{0:T(512)} %param.18) | copy-start | bytes 4612
  7.2 13.5 %copy-start.20 = (f32[48]{0:T(128)S(1)}, f32[48]{0:T(128)}, u32[]{:S(2)}) copy-start(f32[48]{0:T(128)} %param.20) | copy-start | bytes 580
  7.2 13.5 %copy-start.21 = (f32[48]{0:T(128)S(1)}, f32[48]{0:T(128)}, u32[]{:S(2)}) copy-start(f32[48]{0:T(128)} %param.21) | copy-start | bytes 580
  7.2 13.5 %copy-start.22 = (f32[48]{0:T(128)S(1)}, f32[48]{0:T(128)}, u32[]{:S(2)}) copy-start(f32[48]{0:T(128)} %param.22) | copy-start | bytes 580
  7.2 13.5 %copy-start.23 = (f32[48]{0:T(128)S(1)}, f32[48]{0:T(128)}, u32[]{:S(2)}) copy-start(f32[48]{0:T(128)} %param.26) | copy-start | bytes 580
  7.2 13.5 %copy-start.24 = (f32[48]{0:T(128)S(1)}, f32[48]{0:T(128)}, u32[]{:S(2)}) copy-start(f32[48]{0:T(128)} %param.27) | copy-start | bytes 580
  7.3 13.5 %copy-start.25 = (f32[48]{0:T(128)S(1)}, f32[48]{0:T(128)}, u32[]{:S(2)}) copy-start(f32[48]{0:T(128)} %param.28) | copy-start | bytes 580
  7.3 131.9 %all-gather.3.cloned.1.call-start = ((), (), s32[]{:S(2)}) async-start(), calls=%async_computation.14 | async-start | bytes 11096064 | tf_op jit(solution)/shard_map/all_gather | solution.py:770
  10.4 15.8 %all-to-all-start = ((bf16[16,48,128]{2,1,0:T(8,128)(2,1)}), bf16[16,48,128]{2,1,0:T(8,128)(2,1)S(1)}, u32[]{:S(2)}, u32[]{:S(2)}) async-start(bf16[16,48,128]{2,1,0:T(8,128)(2,1)} %bitcast_bitcast_fusion.1), calls=%async_computation | async-start | bytes 393216 | tf_op jit(solution)/shard_map/all_to_all | solution.py:714
  20.8 10.5 %copy-start.16 = (bf16[48,2048]{1,0:T(8,128)(2,1)S(1)}, bf16[48,2048]{1,0:T(8,128)(2,1)}, u32[]{:S(2)}) copy-start(bf16[48,2048]{1,0:T(8,128)(2,1)} %param.29) | copy-start | bytes 589828
  27.3 18.4 %all-to-all-start.1 = ((bf16[16,48,640]{2,1,0:T(8,128)(2,1)}), bf16[16,48,640]{2,1,0:T(8,128)(2,1)S(1)}, u32[]{:S(2)}, u32[]{:S(2)}) async-start(bf16[16,48,640]{2,1,0:T(8,128)(2,1)} %broadcast_in_dim.9), calls=%async_computation.1 | async-start | bytes 1966080 | tf_op jit(solution)/shard_map/all_to_all | solution.py:714
  72.3 29.1 %all-to-all-start.3 = ((bf16[16,352,128]{2,1,0:T(8,128)(2,1)}), bf16[16,352,128]{2,1,0:T(8,128)(2,1)S(1)}, u32[]{:S(2)}, u32[]{:S(2)}) async-start(bf16[16,352,128]{2,1,0:T(8,128)(2,1)} %get-tuple-element.47), calls=%async_computation.3 | async-start | bytes 2883584 | tf_op jit(solution)/shard_map/all_to_all | solution.py:714
  102.5 16.3 %copy-start.18 = (f32[768]{0:T(1024)S(1)}, f32[768]{0:T(1024)}, u32[]{:S(2)}) copy-start(f32[768]{0:T(1024)} %param.24) | copy-start | bytes 9220
  115.3 11.0 %all-to-all-start.4 = ((bf16[16,64,128]{2,1,0:T(8,128)(2,1)}), bf16[16,64,128]{2,1,0:T(8,128)(2,1)S(1)}, u32[]{:S(2)}, u32[]{:S(2)}) async-start(bf16[16,64,128]{2,1,0:T(8,128)(2,1)} %get-tuple-element.48), calls=%async_computation.4 | async-start | bytes 524288 | tf_op jit(solution)/shard_map/all_to_all | solution.py:714
  119.1 20.1 %copy-start.2 = (bf16[16,352,128]{2,1,0:T(8,128)(2,1)S(1)}, bf16[16,352,128]{2,1,0:T(8,128)(2,1)}, u32[]{:S(2)}) copy-start(bf16[16,352,128]{2,1,0:T(8,128)(2,1)} %copy-done.1) | copy-start | bytes 4325380
  151.3 8.0 %copy-start.11 = (f32[768,128]{1,0:T(8,128)}, f32[768,128]{1,0:T(8,128)S(1)}, u32[]{:S(2)}) copy-start(f32[768,128]{1,0:T(8,128)S(1)} %get-tuple-element.65.dh1_ref) | copy-start | bytes 1179652
  170.2 37.8 %all-to-all-start.9 = ((bf16[4,3888,128]{2,1,0:T(8,128)(2,1)}), bf16[4,3888,128]{2,1,0:T(8,128)(2,1)}, u32[]{:S(2)}, u32[]{:S(2)}) async-start(bf16[4,3888,128]{2,1,0:T(8,128)(2,1)} %get-tuple-element.57), calls=%async_computation.9 | async-start | bytes 7962624 | tf_op jit(solution)/shard_map/all_to_all | solution.py:714
  208.0 42.9 %all-to-all-start.8 = ((bf16[16,304,128]{2,1,0:T(8,128)(2,1)}), bf16[16,304,128]{2,1,0:T(8,128)(2,1)S(1)}, u32[]{:S(2)}, u32[]{:S(2)}) async-start(bf16[16,304,128]{2,1,0:T(8,128)(2,1)} %get-tuple-element.53), calls=%async_computation.8 | async-start | bytes 2490368 | tf_op jit(solution)/shard_map/all_to_all | solution.py:714
  216.7 34.2 %collective-permute-start = (bf16[16,384,128]{2,1,0:T(8,128)(2,1)S(1)}, bf16[16,384,128]{2,1,0:T(8,128)(2,1)}, u32[]{:S(2)}, u32[]{:S(2)}) collective-permute-start(bf16[16,384,128]{2,1,0:T(8,128)(2,1)S(1)} %get-tuple-element.60), channel_id=1, source_target_pairs={{0,64},{64,0},{1,65},{65,1},{2,66},{66,2},{3,67},{67,3},{4,68},{68... | collective-permute-start | bytes 4718600 | tf_op jit(solution)/shard_map/ppermute | solution.py:718
  250.9 28.4 %all-to-all-start.10 = ((bf16[16,320,128]{2,1,0:T(8,128)(2,1)}), bf16[16,320,128]{2,1,0:T(8,128)(2,1)}, u32[]{:S(2)}, u32[]{:S(2)}) async-start(bf16[16,320,128]{2,1,0:T(8,128)(2,1)} %attend_back_second.1), calls=%async_computation.10 | async-start | bytes 2621440 | tf_op jit(solution)/shard_map/all_to_all | solution.py:714
  260.6 23.1 %copy-start.4 = (bf16[16,48,640]{2,1,0:T(8,128)(2,1)S(1)}, bf16[16,48,640]{2,1,0:T(8,128)(2,1)}, u32[]{:S(2)}) copy-start(bf16[16,48,640]{2,1,0:T(8,128)(2,1)} %copy-done.3) | copy-start | bytes 2949124
  260.6 23.1 %copy-start.6 = (bf16[4,768,128]{2,1,0:T(8,128)(2,1)S(1)}, bf16[4,768,128]{2,1,0:T(8,128)(2,1)}, u32[]{:S(2)}) copy-start(bf16[4,768,128]{2,1,0:T(8,128)(2,1)} %copy-done.5) | copy-start | bytes 2359300
  279.3 26.7 %all-to-all-start.13 = ((bf16[16,384,128]{2,1,0:T(8,128)(2,1)}), bf16[16,384,128]{2,1,0:T(8,128)(2,1)}, u32[]{:S(2)}, u32[]{:S(2)}) async-start(bf16[16,384,128]{2,1,0:T(8,128)(2,1)} %add_convert_fusion), calls=%async_computation.13 | async-start | bytes 3145728 | tf_op jit(solution)/shard_map/all_to_all | solution.py:714
  306.0 9.2 %copy-start.8 = (bf16[16,128,128]{2,1,0:T(8,128)(2,1)S(1)}, bf16[16,128,128]{2,1,0:T(8,128)(2,1)}, u32[]{:S(2)}) copy-start(bf16[16,128,128]{2,1,0:T(8,128)(2,1)} %copy-done.7) | copy-start | bytes 1572868
  306.0 12.6 %all-to-all-start.11 = ((bf16[4,768,128]{2,1,0:T(8,128)(2,1)}), bf16[4,768,128]{2,1,0:T(8,128)(2,1)S(1)}, u32[]{:S(2)}, u32[]{:S(2)}) async-start(bf16[4,768,128]{2,1,0:T(8,128)(2,1)} %get-tuple-element.64), calls=%async_computation.11 | async-start | bytes 1572864 | tf_op jit(solution)/shard_map/all_to_all | solution.py:714
  309.6 8.9 %copy-start.10 = (bf16[16,128,128]{2,1,0:T(8,128)(2,1)S(1)}, bf16[16,128,128]{2,1,0:T(8,128)(2,1)}, u32[]{:S(2)}) copy-start(bf16[16,128,128]{2,1,0:T(8,128)(2,1)} %copy-done.9) | copy-start | bytes 1572868
  311.3 4.2 %collective-permute-start.3 = (f32[384,128]{1,0:T(8,128)S(1)}, f32[384,128]{1,0:T(8,128)S(1)}, u32[]{:S(2)}, u32[]{:S(2)}) collective-permute-start(f32[384,128]{1,0:T(8,128)S(1)} %convert_reduce_fusion), channel_id=1, source_target_pairs={{0,64},{64,0},{1,65},{65,1},{2,66},{66,2},{3,67},{67,3},{4,68},{68... | collective-permute-start | bytes 589832 | tf_op jit(solution)/shard_map/ppermute | solution.py:718
  315.1 1.9 collective-permute-start.1
  320.7 8.3 %copy-start.15 = (f32[288,128]{1,0:T(8,128)S(1)}, f32[288,128]{1,0:T(8,128)}, u32[]{:S(2)}) copy-start(f32[288,128]{1,0:T(8,128)} %get-tuple-element.68) | copy-start | bytes 442372
  320.7 9.6 %slice-start = ((f32[768,128]{1,0:T(8,128)}), f32[96,128]{1,0:T(8,128)S(1)}, s32[]{:S(2)}) async-start(f32[768,128]{1,0:T(8,128)} %copy-done.14), calls=%async_computation.15 | async-start | bytes 98304 | tf_op jit(solution)/shard_map/slice | solution.py:829
  320.7 20.3 %all-to-all-start.12 = ((bf16[16,176,128]{2,1,0:T(8,128)(2,1)}), bf16[16,176,128]{2,1,0:T(8,128)(2,1)S(1)}, u32[]{:S(2)}, u32[]{:S(2)}) async-start(bf16[16,176,128]{2,1,0:T(8,128)(2,1)} %last_payload.1), calls=%async_computation.12 | async-start | bytes 1441792 | tf_op jit(solution)/shard_map/all_to_all | solution.py:714
  341.0 3.5 collective-permute-start.2
  (10 other events, 27.4 us)
Sparse Core Ops, SparseCore 0:
  11.5 101.4 all-gather.2

commit v3 on v2

--- a/solution.py
+++ b/solution.py
@@ -26,10 +26,15 @@
 AUG = 144
 JW = 640
 HALF = 2
-FWD_C = 4
+FWD_C = 2
 BWD_C = 2
+Q_AT = NROW * TOK
+C_AT = Q_AT + 64
+BLOCK = C_AT + 48
 MIB = 2**20
+COL = ("z", "y")
 VMEM = pl.BlockSpec(memory_space=pltpu.VMEM)
+SMEM = pl.BlockSpec(memory_space=pltpu.SMEM)
 SENT = 3 * DIM + 48 + 2 * DIM
 WROWS = 768
 
@@ -54,45 +59,44 @@
     return pl.CostEstimate(flops=int(us * 1e9), bytes_accessed=int(us * 2e6), transcendentals=0)
 
 
+Q_BLOCK = pl.BlockSpec((NCOL, 64, 128), lambda i: (0, Q_AT // 64, 0))
+
+
 def whole(shape):
     return pl.BlockSpec(shape, lambda i: (0,) * len(shape))
 
 
-def project_kernel(x_ref, w_ref, b_ref, extra_ref, first_ref, second_ref, q_ref):
+def project_kernel(x_ref, w_ref, b_ref, cot_ref, out_ref, q_ref):
     w = w_ref[...].reshape(DIM, JW)
     q_ref[...] = jnp.zeros_like(q_ref)
     for r in range(NROW):
         tokens = x_ref[r].astype(F32).T.astype(BF)
         y = dot(tokens, w, 1, 0) + b_ref[...]
         q_ref[r * TOK : (r + 1) * TOK, :] = y[:, 0:256]
-        out, at = (first_ref, r) if r < HALF else (second_ref, r - HALF)
         for h in range(3):
             kv = y[:, 256 + 128 * h : 384 + 128 * h].T.astype(BF)
             for j in range(PER_HEAD * h, PER_HEAD * (h + 1) + (1 if h == 2 else 0)):
-                out[j, at * TOK : (at + 1) * TOK, :] = kv
+                out_ref[j, r * TOK : (r + 1) * TOK, :] = kv
     for j in range(NCOL):
         h, k = min(j, 14) // PER_HEAD, min(j, 14) % PER_HEAD
         lanes = slice(HDIM * h, HDIM * (h + 1))
         a = q_ref[SHARE * k : SHARE * k + 64, lanes]
         b = q_ref[SHARE * k + 64 : SHARE * k + 128, lanes]
-        first_ref[j, 256:320, :] = jnp.concatenate([a, b], axis=1).astype(BF)
-    second_ref[:, 256:352, :] = extra_ref[...]
-
-
-def project(x4, wj, bias, extra):
+        out_ref[j, Q_AT:C_AT, :] = jnp.concatenate([a, b], axis=1).astype(BF)
+    out_ref[:, C_AT:BLOCK, :] = cot_ref[...]
+
+
+def project(x4, wj, bias, cot):
     return pl.pallas_call(
         project_kernel,
-        out_shape=(
-            jax.ShapeDtypeStruct((NCOL, 320, 128), BF),
-            jax.ShapeDtypeStruct((NCOL, 352, 128), BF),
-        ),
+        out_shape=jax.ShapeDtypeStruct((NCOL, BLOCK, 128), BF),
         in_specs=[VMEM] * 4,
-        out_specs=[VMEM] * 2,
+        out_specs=VMEM,
         scratch_shapes=[pltpu.VMEM((640, 256), F32)],
         compiler_params=params(40),
         cost_estimate=cost(3),
         name="project",
-    )(x4, wj, bias, extra)
+    )(x4, wj, bias, cot)
 
 
 def key_rows(seg_row):
@@ -111,12 +115,15 @@
     )
 
 
-def key_block(kv_ref, seg_ref, count):
-    kvt = jnp.concatenate(
-        [kv_ref[c, r * TOK : (r + 1) * TOK, :] for c in range(count) for r in range(HALF)], axis=1
-    )
-    extra = jnp.concatenate([key_rows(seg_ref[0, i : i + 1, :]) for i in range(count * HALF)], axis=1)
-    return kvt, extra
+def key_block(kv_refs, seg_ref):
+    tiles = [
+        ref[c, at : at + TOK, :]
+        for c in range(kv_refs[0].shape[0])
+        for ref in kv_refs
+        for at in range(0, ref.shape[1], TOK)
+    ]
+    extra = [key_rows(seg_ref[0, i : i + 1, :]) for i in range(len(tiles))]
+    return jnp.concatenate(tiles, axis=1), jnp.concatenate(extra, axis=1)
 
 
 def unpack(block_ref, store):
@@ -127,7 +134,7 @@
 
 
 def forward_step(qa_ref, kv_ref, seg_ref, acc_ref, top_ref):
-    kvt, extra = key_block(kv_ref, seg_ref, FWD_C)
+    kvt, extra = key_block([kv_ref], seg_ref)
     kt = jnp.concatenate([kvt[0:64], kvt[0:64], extra], axis=0)
     turned = kvt.astype(F32).T
     lane = lax.broadcasted_iota(jnp.int32, turned.shape, 1)
@@ -145,7 +152,9 @@
     acc_ref[...] = acc_ref[...] * fade + dot(p, va, 1, 0)
 
 
-def attend_first_kernel(q_ref, kv_ref, segq_ref, seg_ref, qa_ref, acc_ref, top_ref, q_scr):
+def attend_kernel(
+    q_ref, kv_ref, segq_ref, seg_ref, qa_ref, o_ref, out_ref, q_scr, acc_ref, top_ref
+):
     @pl.when(pl.program_id(0) == 0)
     def _():
         def store(at, rows):
@@ -163,26 +172,13 @@
 
     forward_step(qa_ref, kv_ref, seg_ref, acc_ref, top_ref)
 
-
-def attend_second_kernel(
-    qa_in, acc_in, top_in, kv_ref, seg_ref, qa_ref, o_ref, out_ref, acc_ref, top_ref
-):
-    @pl.when(pl.program_id(0) == 0)
-    def _():
-        acc_ref[...] = acc_in[...]
-        top_ref[...] = top_in[...]
-
-    forward_step(qa_in, kv_ref, seg_ref, acc_ref, top_ref)
-
     @pl.when(pl.program_id(0) == pl.num_programs(0) - 1)
     def _():
         acc = acc_ref[...]
         total = acc[:, 0:1]
-        o = acc[:, 64:128] / total
-        o_ref[...] = o
-        qa_ref[:, 0:128] = qa_in[:, 0:128]
+        o_ref[...] = acc[:, 64:128] / total
         lse = top_ref[:, 0:1] + jnp.log(total) * LOG2E
-        qa_ref[:, 128:144] = offset_columns(lse, qa_in[:, 128:144].astype(F32)).astype(BF)
+        qa_ref[:, 128:144] = offset_columns(lse, qa_ref[:, 128:144].astype(F32)).astype(BF)
         for c in range(NCOL):
             out_ref[c] = pack(o_ref, SHARE * c)
 
@@ -196,55 +192,36 @@
     return both.astype(BF)
 
 
-def attend(first, second, segq, seg_first, seg_second):
-    steps = NCOL // FWD_C
-    kinds = (
-        jax.ShapeDtypeStruct((ROWS, AUG), BF),
-        jax.ShapeDtypeStruct((ROWS, 128), F32),
-        jax.ShapeDtypeStruct((ROWS, 128), F32),
-    )
-    seg_spec = pl.BlockSpec((1, FWD_C * HALF, TOK), lambda i: (i, 0, 0))
-    state = pl.pallas_call(
-        attend_first_kernel,
-        grid=(steps,),
-        out_shape=kinds,
-        in_specs=[
-            pl.BlockSpec((NCOL, 64, 128), lambda i: (0, 4, 0)),
-            pl.BlockSpec((FWD_C, 256, 128), lambda i: (i, 0, 0)),
-            whole((ROWS, 1)),
-            seg_spec,
-        ],
-        out_specs=[whole((ROWS, AUG)), whole((ROWS, 128)), whole((ROWS, 128))],
-        scratch_shapes=[pltpu.VMEM((ROWS, HDIM), F32)],
-        compiler_params=params(58),
-        cost_estimate=cost(10),
-        name="attend_first",
-    )(first, first, segq, seg_first)
-    return pl.pallas_call(
-        attend_second_kernel,
-        grid=(steps,),
+def attend(arrived, segq, seg_k):
+    seg = seg_k.reshape(NCOL // FWD_C, FWD_C * NROW, TOK)
+    return pl.pallas_call(
+        attend_kernel,
+        grid=(NCOL // FWD_C,),
         out_shape=(
-            kinds[0],
+            jax.ShapeDtypeStruct((ROWS, AUG), BF),
             jax.ShapeDtypeStruct((ROWS, HDIM), F32),
             jax.ShapeDtypeStruct((NCOL, 64, 128), BF),
         ),
         in_specs=[
-            whole((ROWS, AUG)),
-            whole((ROWS, 128)),
-            whole((ROWS, 128)),
-            pl.BlockSpec((FWD_C, 256, 128), lambda i: (i, 0, 0)),
-            seg_spec,
+            Q_BLOCK,
+            pl.BlockSpec((FWD_C, Q_AT, 128), lambda i: (i, 0, 0)),
+            whole((ROWS, 1)),
+            pl.BlockSpec((1, FWD_C * NROW, TOK), lambda i: (i, 0, 0)),
         ],
         out_specs=[whole((ROWS, AUG)), whole((ROWS, HDIM)), whole((NCOL, 64, 128))],
-        scratch_shapes=[pltpu.VMEM((ROWS, 128), F32), pltpu.VMEM((ROWS, 128), F32)],
-        compiler_params=params(58),
-        cost_estimate=cost(10),
-        name="attend_second",
-    )(*state, second, seg_second)
-
-
-def backward_step(qa_ref, doa_ref, turned_ref, kv_ref, seg_ref, acc_ref):
-    kvt, extra = key_block(kv_ref, seg_ref, BWD_C)
+        scratch_shapes=[
+            pltpu.VMEM((ROWS, HDIM), F32),
+            pltpu.VMEM((ROWS, 128), F32),
+            pltpu.VMEM((ROWS, 128), F32),
+        ],
+        compiler_params=params(60),
+        cost_estimate=cost(20),
+        name="attend",
+    )(arrived, arrived, segq, seg)
+
+
+def backward_step(qa_ref, doa_ref, turned_ref, kv_refs, seg_ref, acc_ref):
+    kvt, extra = key_block(kv_refs, seg_ref)
     kt = jnp.concatenate([kvt[0:64], kvt[0:64], extra], axis=0)
     vt = jnp.concatenate([kvt[64:128], extra], axis=0)
     keys = kvt.astype(F32).T.astype(BF)
@@ -285,19 +262,21 @@
         doa_ref[...] = jnp.concatenate([grad.astype(BF), ext.astype(BF)], axis=1)
         acc_ref[...] = jnp.zeros_like(acc_ref)
 
-    both = backward_step(qa_ref, doa_ref, turned_ref, kv_ref, seg_ref, acc_ref)
+    both = backward_step(qa_ref, doa_ref, turned_ref, [kv_ref], seg_ref, acc_ref)
     store_keys(out_ref, 0, both)
     out_ref[:, 256:304, :] = fin_ref[...]
 
 
-def back_second_kernel(qa_ref, doa_ref, turned_ref, acc_in, kv_ref, seg_ref, out_ref, acc_ref):
+def back_second_kernel(
+    qa_ref, doa_ref, turned_ref, acc_in, kv_ref, seg_ref, out_ref, acc_ref
+):
     step = pl.program_id(0)
 
     @pl.when(step == 0)
     def _():
         acc_ref[...] = acc_in[...]
 
-    both = backward_step(qa_ref, doa_ref, turned_ref, kv_ref, seg_ref, acc_ref)
+    both = backward_step(qa_ref, doa_ref, turned_ref, [kv_ref], seg_ref, acc_ref)
     store_keys(out_ref, step * BWD_C, both)
 
     @pl.when(step == pl.num_programs(0) - 1)
@@ -307,11 +286,11 @@
 
 
 SEG_BACK = pl.BlockSpec((1, BWD_C * HALF, TOK), lambda i: (i, 0, 0))
-KEYS_BACK = pl.BlockSpec((BWD_C, 256, 128), lambda i: (i, 0, 0))
 BACK_STEPS = NCOL // BWD_C
 
 
-def attend_back_first(first, grad, qa, o, fin, seg_first):
+def attend_back_first(arrived, grad, qa, o, fin, seg_k):
+    seg = seg_k[:, :HALF].reshape(BACK_STEPS, BWD_C * HALF, TOK)
     return pl.pallas_call(
         back_first_kernel,
         grid=(BACK_STEPS,),
@@ -322,12 +301,12 @@
             jax.ShapeDtypeStruct((ROWS, 128), F32),
         ),
         in_specs=[
-            pl.BlockSpec((NCOL, 64, 128), lambda i: (0, 4, 0)),
+            Q_BLOCK,
             whole((NCOL, 64, 128)),
             whole((ROWS, AUG)),
             whole((ROWS, HDIM)),
             pl.BlockSpec((BWD_C, 48, 128), lambda i: (i, 0, 0)),
-            KEYS_BACK,
+            pl.BlockSpec((BWD_C, HALF * TOK, 128), lambda i: (i, 0, 0)),
             SEG_BACK,
         ],
         out_specs=[
@@ -340,10 +319,11 @@
         compiler_params=params(58),
         cost_estimate=cost(18),
         name="attend_back_first",
-    )(first, grad, qa, o, fin, first, seg_first)
-
-
-def attend_back_second(qa, doa, turned, acc, second, seg_second):
+    )(arrived, grad, qa, o, fin, arrived, seg)
+
+
+def attend_back_second(qa, doa, turned, acc, arrived, seg_k):
+    seg = seg_k[:, HALF:].reshape(BACK_STEPS, BWD_C * HALF, TOK)
     return pl.pallas_call(
         back_second_kernel,
         grid=(BACK_STEPS,),
@@ -353,7 +333,7 @@
             whole((ROWS, 80)),
             whole((128, ROWS)),
             whole((ROWS, 128)),
-            KEYS_BACK,
+            pl.BlockSpec((BWD_C, HALF * TOK, 128), lambda i: (i, 1, 0)),
             SEG_BACK,
         ],
         out_specs=whole((NCOL, 320, 128)),
@@ -361,7 +341,7 @@
         compiler_params=params(58),
         cost_estimate=cost(18),
         name="attend_back_second",
-    )(qa, doa, turned, acc, second, seg_second)
+    )(qa, doa, turned, acc, arrived, seg)
 
 
 def gather_rows(block_ref, scr, rows=slice(0, 64)):
@@ -424,10 +404,11 @@
 
 
 def tokenwise_kernel(
-    att_ref, x_ref, extra_ref, all_ref,
+    row_ref, att_ref, x_ref, cot_ref, vec_ref, all_ref,
     sent_ref, datt_ref, fin_ref, dh1_ref,
-    up_ref, down_ref, out_ref, slope_ref, act_ref, sems,
+    up_ref, down_ref, out_ref, slope_ref, sems,
 ):
+    row = row_ref[0]
     copies = []
     for g in range(3):
         for k in range(2):
@@ -461,8 +442,8 @@
             copy.wait()
 
     tok = x_ref[...].reshape(DIM, TOK).astype(F32).T
-    cot = extra_ref[:, 256:304, :].reshape(DIM, TOK).astype(F32).T
-    vecs = extra_ref[:, 304:352, :].reshape(DIM, TOK).astype(F32).T
+    cot = cot_ref[...].reshape(DIM, TOK).astype(F32).T
+    vecs = vec_ref[...].reshape(DIM, TOK).astype(F32).T[64:128]
     out_b, gain_1, shift_1, down_b, gain_2, shift_2 = [
         vecs[i : i + 1] + vecs[6 + i : 7 + i] + vecs[12 + i : 13 + i] for i in range(6)
     ]
@@ -495,7 +476,7 @@
         slope_ref[:, cols] = phi + pre * jnp.exp(-0.5 * pre * pre) * (1.0 / math.sqrt(2.0 * math.pi))
         for i in range(6):
             at = 3 * DIM + 48 + DIM + i * TOK
-            sent_ref[r, at : at + TOK, :] = act[:, i * TOK : (i + 1) * TOK]
+            sent_ref[lax.rem(r + NROW - row, NROW), at : at + TOK, :] = act[:, i * TOK : (i + 1) * TOK]
         wait(5 + r)
         branch = branch + dot(act, down_ref[:, :, cols].reshape(DIM, DIM), 1, 1)
     h2 = n1 + (branch + down_b)
@@ -514,7 +495,7 @@
         d_pre = (d_act * slope_ref[:, cols]).astype(BF)
         for i in range(6):
             at = 3 * DIM + 48 + i * TOK
-            sent_ref[r, at : at + TOK, :] = d_pre[:, i * TOK : (i + 1) * TOK]
+            sent_ref[lax.rem(r + NROW - row, NROW), at : at + TOK, :] = d_pre[:, i * TOK : (i + 1) * TOK]
         back = back + dot(d_pre, up_ref[:, :, cols].reshape(DIM, DIM), 1, 1)
     up1 = dh2 + back
     dx = up1 * gain_1
@@ -543,7 +524,7 @@
         at += v.shape[0]
 
 
-def tokenwise(att, x_t, extra, everything):
+def tokenwise(row, att, x_t, arrived, wj, everything):
     return pl.pallas_call(
         tokenwise_kernel,
         out_shape=(
@@ -552,20 +533,32 @@
             jax.ShapeDtypeStruct((NCOL, 48, TOK), BF),
             jax.ShapeDtypeStruct((DIM, TOK), F32),
         ),
-        in_specs=[VMEM] * 3 + [pl.BlockSpec(memory_space=pl.ANY)],
-        out_specs=[VMEM] * 4,
+        grid=(1,),
+        in_specs=[
+            SMEM,
+            whole((NROW, TOK + 16, 192)),
+            whole((NCOL, 48, TOK)),
+            pl.BlockSpec((NCOL, 48, TOK), lambda i: (0, C_AT // 48, 0)),
+            pl.BlockSpec((NCOL, 48, TOK), lambda i: (0, 0, 1)),
+            pl.BlockSpec(memory_space=pl.ANY),
+        ],
+        out_specs=[
+            whole((NROW, SENT, TOK)),
+            whole((NROW, TOK, 192)),
+            whole((NCOL, 48, TOK)),
+            whole((DIM, TOK)),
+        ],
         scratch_shapes=[
             pltpu.VMEM((NCOL, 48, FF), BF),
             pltpu.VMEM((NCOL, 48, FF), BF),
             pltpu.VMEM((2 * NROW, NCOL, 48, 128), BF),
             pltpu.VMEM((TOK, FF), F32),
-            pltpu.VMEM((TOK, FF), BF),
             pltpu.SemaphoreType.DMA((9,)),
         ],
         compiler_params=params(48),
         cost_estimate=cost(15),
         name="tokenwise",
-    )(att, x_t, extra, everything)
+    )(row, att, x_t, arrived, wj, everything)
 
 
 def place(core, mine_ref, other_ref, blocks, half_rows):
@@ -584,16 +577,20 @@
             other_ref[:, rows, :] = block
 
 
-def weight_grads_kernel(core_ref, got_ref, att_ref, mine_ref, other_ref):
-    core = core_ref[0]
+def weight_grads_kernel(
+    core_ref, row_ref, own_ref, got_1, got_2, got_3, att_ref, mine_ref, other_ref
+):
+    core, row = core_ref[0], row_ref[0]
+    got_ref = [own_ref.at[0], got_1, got_2, got_3]
+    source = [lax.rem(row + NROW - d, NROW) for d in range(NROW)]
 
     def feats(at):
-        return jnp.concatenate([got_ref[r, at : at + DIM, :] for r in range(NROW)], axis=1)
+        return jnp.concatenate([got_ref[r][at : at + DIM, :] for r in range(NROW)], axis=1)
 
     def hidden(at):
         return jnp.concatenate(
             [
-                jnp.concatenate([got_ref[r, at + i * TOK : at + (i + 1) * TOK, :] for i in range(6)], axis=1)
+                jnp.concatenate([got_ref[r][at + i * TOK : at + (i + 1) * TOK, :] for i in range(6)], axis=1)
                 for r in range(NROW)
             ],
             axis=0,
@@ -606,15 +603,15 @@
     d_pre = hidden(3 * DIM + 48)
     d_branch = feats(DIM)
     d_attn = feats(2 * DIM)
-    att = jnp.concatenate([att_ref[r, 0:TOK, :] for r in range(NROW)], axis=0)
+    att = jnp.concatenate([att_ref[source[r], 0:TOK, :] for r in range(NROW)], axis=0)
     att = jnp.concatenate([att, jnp.zeros((NROW * TOK, 64), BF)], axis=1)
     pieces = chunks(dot(feats(0), d_pre, 1, 0), 6)
     pieces += chunks(dot(d_branch, hidden(4 * DIM + 48), 1, 0), 6)
     pieces += chunks(dot(d_attn, att, 1, 0), 2)
     sums = [dot(ones, d_branch, 1, 1)[0:1], dot(ones, d_attn, 1, 1)[0:1], dot(ones, d_pre, 1, 0)[0:1]]
-    norm = got_ref[0, 3 * DIM : 3 * DIM + 48, :].astype(F32)
+    norm = got_ref[0][3 * DIM : 3 * DIM + 48, :].astype(F32)
     for r in range(1, NROW):
-        norm = norm + got_ref[r, 3 * DIM : 3 * DIM + 48, :].astype(F32)
+        norm = norm + got_ref[r][3 * DIM : 3 * DIM + 48, :].astype(F32)
     rows = [norm[0:24] + norm[24:48]]
     for v in sums:
         rows += [v[:, i * 128 : (i + 1) * 128] for i in range(6)]
@@ -628,17 +625,20 @@
     place(core, mine_ref, other_ref, blocks, WROWS // 2)
 
 
-def weight_grads(core, got, att):
+def weight_grads(core, row, sent, got, att):
     kind = jax.ShapeDtypeStruct((NCOL, WROWS // 2, 128), BF)
     return pl.pallas_call(
         weight_grads_kernel,
         out_shape=(kind, kind),
-        in_specs=[pl.BlockSpec(memory_space=pltpu.SMEM)] + [VMEM] * 2,
-        out_specs=[VMEM] * 2,
-        compiler_params=params(48),
-        cost_estimate=cost(5),
+        grid=(1,),
+        in_specs=[SMEM, SMEM, pl.BlockSpec((1, SENT, TOK), lambda i: (0, 0, 0))]
+        + [whole((SENT, TOK))] * 3
+        + [whole((NROW, TOK + 16, 192))],
+        out_specs=[whole(kind.shape)] * 2,
+        compiler_params=params(56),
+        cost_estimate=cost(1),
         name="weight_grads",
-    )(core, got, att)
+    )(core, row, sent, *got, att)
 
 
 def project_back_kernel(
@@ -681,7 +681,7 @@
     return pl.pallas_call(
         project_back_kernel,
         out_shape=(jax.ShapeDtypeStruct((NROW, DIM, TOK), BF), kind, kind),
-        in_specs=[pl.BlockSpec(memory_space=pltpu.SMEM)] + [VMEM] * 4,
+        in_specs=[SMEM] + [VMEM] * 4,
         out_specs=[VMEM] * 3,
         scratch_shapes=[pltpu.VMEM((528, 256), F32)],
         compiler_params=params(48),
@@ -714,13 +714,12 @@
     return lax.all_to_all(blocks, axis, 0, 0, tiled=True)
 
 
+def around(v, axis, shift):
+    return lax.ppermute(v, axis, [(i, (i + shift) % 4) for i in range(4)])
+
+
 def swap_cores(v):
     return lax.ppermute(v, "dp", [(0, 1), (1, 0)])
-
-
-def pair(core, v):
-    theirs = swap_cores(v)
-    return jnp.where(core == 0, jnp.concatenate([v, theirs]), jnp.concatenate([theirs, v]))
 
 
 def per_device(
@@ -741,19 +740,29 @@
     cotangent,
 ):
     core = lax.axis_index("dp")
-    col = lax.axis_index("col")
+    col = lax.axis_index(COL)
+    row = lax.axis_index("row")
+    my_y = lax.axis_index("y")
     core_word = core.reshape(1).astype(jnp.int32)
+    row_word = row.reshape(1).astype(jnp.int32)
 
     def by_col(a):
         return jnp.transpose(a.reshape(48, NCOL, TOK), (1, 0, 2))
 
-    x_t = exchange(by_col(inputs), "col")
+    blocks = by_col(inputs)
+    blocks, up_weight, down_weight, output_weight = lax.optimization_barrier(
+        (blocks, up_weight, down_weight, output_weight)
+    )
+    x_t = exchange(blocks, COL)
+    vectors = jnp.stack(
+        [output_bias, first_norm_gain, shift_first, down_bias, second_norm_gain, second_norm_shift], axis=1
+    )
+    vectors = jnp.pad(jnp.concatenate(split3(vectors), axis=1), ((0, 0), (0, 46)))
     jw = joint_weight.reshape(48, 3, 3, HDIM)
-    jw = jnp.concatenate(
-        [jw[:, :, 0].reshape(48, 192), jnp.zeros((48, 64), BF), jw[:, :, 1:].reshape(48, 384)], axis=1
-    )
+    jw = jnp.concatenate([jw[:, :, 0].reshape(48, 192), vectors, jw[:, :, 1:].reshape(48, 384)], axis=1)
+    jw = jnp.broadcast_to(jw[None], (NCOL, 48, JW))
     x_t, jw = lax.optimization_barrier((x_t, jw))
-    wj = exchange(jnp.broadcast_to(jw[None], (NCOL, 48, JW)), "col")
+    wj = exchange(jw, COL)
     x4 = lax.all_gather(x_t.reshape(DIM, TOK), "row", axis=0, tiled=False)
 
     turned = lax.dynamic_slice_in_dim(output_weight, core * 96, 96, 0).T
@@ -767,16 +776,9 @@
         ],
         axis=0,
     )
-    everything = lax.all_gather(shard, ("dp", "row", "col"), axis=0, tiled=False)
+    everything = lax.all_gather(shard, ("dp", "row", "z", "y"), axis=0, tiled=False)
     everything = everything.reshape(2, NROW, NCOL, 112, 384)
 
-    vectors = jnp.stack(
-        [output_bias, first_norm_gain, shift_first, down_bias, second_norm_gain, second_norm_shift], axis=1
-    )
-    vectors = jnp.pad(jnp.concatenate(split3(vectors), axis=1), ((0, 0), (0, 110)))
-    extra = jnp.concatenate(
-        [by_col(cotangent), jnp.broadcast_to(vectors[None], (NCOL, 48, 128))], axis=1
-    )
     bias3 = joint_bias.reshape(3, 2, HDIM)
     bias = jnp.concatenate(
         [
@@ -790,39 +792,50 @@
     seg_rows = jnp.pad(seg_k.reshape(NCOL, 512), ((0, 0), (0, 8)))
     seg_q = lax.dynamic_slice_in_dim(seg_rows, lax.rem(col, PER_HEAD) * SHARE, SHARE, 1)
     seg_q = seg_q.reshape(ROWS, 1)
-    seg_a = seg_k[:, :HALF]
-    seg_b = seg_k[:, HALF:]
-
-    first, second = project(x4, wj, bias, extra)
-    first = exchange(first, "col")
-    second = exchange(second, "col")
-    by_step = lambda s, n: s.reshape(NCOL // n, n * HALF, TOK)
-    qa, o, o_blocks = attend(first, second, seg_q, by_step(seg_a, FWD_C), by_step(seg_b, FWD_C))
-
-    att_r = to_row(exchange(o_blocks, "col"), bias_rows)
+
+    arrived = exchange(project(x4, wj, bias, by_col(cotangent)), COL)
+    qa, o, o_blocks = attend(arrived, seg_q, seg_k)
+
+    att_r = to_row(exchange(o_blocks, COL), bias_rows)
     att = exchange(att_r, "row")
-    sent, d_att, fin, dh1 = tokenwise(att, x_t, second, everything)
-
-    grad_o = exchange(to_col(exchange(d_att, "row")), "col")
-    got = exchange(sent, "row")
-    back_a, doa, turned_qd, acc = attend_back_first(first, grad_o, qa, o, fin, by_step(seg_a, BWD_C))
-    back_a = exchange(back_a, "col")
-    mine, other = weight_grads(core_word, got, att_r)
+    sent, d_att, fin, dh1 = tokenwise(row_word, att, x_t, arrived, wj, everything)
+
+    d_blocks = to_col(exchange(d_att, "row"))
+    d_blocks, sent = lax.optimization_barrier((d_blocks, sent))
+    grad_o = exchange(d_blocks, COL)
+    got = [around(sent[d], "row", d) for d in range(1, NROW)]
+    back_a, doa, turned_qd, acc = attend_back_first(arrived, grad_o, qa, o, fin, seg_k)
+    back_b = attend_back_second(qa, doa, turned_qd, acc, arrived, seg_k)
+    back_a = exchange(back_a, COL)
+    late = lax.optimization_barrier((back_b, got, sent))
+    got, sent = late[1:]
+    mine, other = weight_grads(core_word, row_word, sent, got, att_r)
     theirs = swap_cores(other)
-    acc, mine = lax.optimization_barrier((acc, mine))
-    back_b = attend_back_second(qa, doa, turned_qd, acc, second, by_step(seg_b, BWD_C))
-    back_b, theirs = lax.optimization_barrier((back_b, theirs))
-    back_b = exchange(back_b, "col")
-    wide = (mine.astype(F32) + theirs.astype(F32)).astype(BF)
-    wide = exchange(wide, "col")
+    back_b, back_a = lax.optimization_barrier((back_b, back_a))
+    back_b = exchange(back_b, COL)
+    wide = (mine.astype(F32) + theirs.astype(F32)).astype(BF).reshape(4, 4, WROWS // 2, 128)
+    wide, back_b = lax.optimization_barrier((wide, back_b))
+    wide = lax.psum_scatter(wide, "z", scatter_dimension=0, tiled=False)
 
     din, mine_j, other_j = project_back(core_word, back_a, back_b, wj, x4)
     theirs_j = swap_cores(other_j)
     din = exchange(din, "row")
-    mixed = exchange(last_payload(mine_j, theirs_j, din, dh1), "col")
+    mixed = last_payload(mine_j, theirs_j, din, dh1)
+    mixed, wide = lax.optimization_barrier((mixed, wide))
+    mixed = exchange(mixed, COL)
+    wide = lax.dynamic_index_in_dim(wide, my_y, 0, keepdims=False).astype(F32) + sum(
+        around(lax.dynamic_index_in_dim(wide, lax.rem(my_y + d, 4), 0, keepdims=False), "y", d).astype(F32)
+        for d in range(1, 4)
+    )
 
     layer_output = jnp.transpose(back_a[:, 256:304], (1, 0, 2)).reshape(48, 2048)
-    wide = pair(core, jnp.sum(wide.astype(F32), axis=0))
+    mixed, wide = lax.optimization_barrier((mixed, wide))
+    mine = jnp.concatenate([wide, jnp.sum(mixed[:, :128].astype(F32), axis=0)], axis=0)
+    theirs = swap_cores(mine)
+    low = jnp.where(core == 0, mine, theirs)
+    high = jnp.where(core == 0, theirs, mine)
+    wide = jnp.concatenate([low[:384], high[:384]], axis=0)
+    last = jnp.concatenate([low[384:], high[384:]], axis=0)
     as_cols = lambda v, n: jnp.transpose(v.reshape(n, 48, 128), (1, 0, 2)).reshape(48, n * 128)
     grad_up = as_cols(wide[0:288], 6)
     grad_down = as_cols(wide[288:576], 6)
@@ -830,9 +843,7 @@
     vecs = (wide[672:720] + wide[720:768])[:42].reshape(7, DIM)
     own = lax.dynamic_slice_in_dim(vecs[:6], col * 48, 48, 1)
     grad_up_bias = vecs[6]
-
     grad_inputs = jnp.transpose(mixed[:, 128:].astype(F32), (1, 0, 2)).reshape(48, 2048)
-    last = pair(core, jnp.sum(mixed[:, :128].astype(F32), axis=0))
     gj = as_cols(last[0:240], 5)
     gj_q = gj[:, :192].reshape(48, 3, 1, HDIM)
     gj_kv = gj[:, 256:].reshape(48, 3, 2, HDIM)
@@ -860,18 +871,20 @@
 
 
 def solution(mesh):
-    grid = P("col", ("dp", "row"))
-    block = P("col", "row")
+    sizes = (mesh.shape["dp"], mesh.shape["row"], 4, 4)
+    fine = jax.sharding.Mesh(mesh.devices.reshape(sizes), ("dp", "row", "z", "y"))
+    grid = P(COL, ("dp", "row"))
+    block = P(COL, "row")
     return jax.shard_map(
         per_device,
-        mesh=mesh,
+        mesh=fine,
         in_specs=(
-            grid, P("dp", None), block, P("row"), P("row", "col"), P("col"), P("col"), P("col"),
-            block, P("row"), block, P("col"), P("col"), P("col"), grid,
+            grid, P("dp", None), block, P("row"), P("row", COL), P(COL), P(COL), P(COL),
+            block, P("row"), block, P(COL), P(COL), P(COL), grid,
         ),
         out_specs=(
-            grid, grid, block, P("row"), P("row", "col"), P("col"), P("col"), P("col"),
-            block, P("row"), block, P("col"), P("col"), P("col"),
+            grid, grid, block, P("row"), P("row", COL), P(COL), P(COL), P(COL),
+            block, P("row"), block, P(COL), P(COL), P(COL),
         ),
         check_vma=False,
     )

time: 355 us -> 328 us (0.924)
  blocking collectives: 67.8 us -> 12.3 us
  local copies, waits for them, and re-layouts: 18.3 us -> 38.7 us
  waiting for transfers between devices: 84.8 us -> 90.3 us
    all_to_all x4 -> x0, blocking collectives: 55.6 us -> none  [exchange(): return lax.all_to_all(blocks, axis, 0, 0, tiled=True)]
    unnamed x57 -> x52, local copies, waits for them, and re-layouts: 3.88 us -> 16 us
    ppermute x4 -> x3, starting transfers between devices: 20.4 us -> 13.3 us  [swap_cores(): return lax.ppermute(v, 'dp', [(0, 1), (1, 0)])]
    ppermute x0 -> x6, starting transfers between devices: none -> 6.02 us  [around(): return lax.ppermute(v, axis, [(i, (i + shift) % 4) for i in range(4)])]
    all_to_all x10 -> x11, waiting for transfers between devices: 83.6 us -> 88.3 us  [exchange(): return lax.all_to_all(blocks, axis, 0, 0, tiled=True)]
    all_to_all x10 -> x11, starting transfers between devices: 51.4 us -> 56 us  [exchange(): return lax.all_to_all(blocks, axis, 0, 0, tiled=True)]
    squeeze x0 -> x2, local copies, waits for them, and re-layouts: none -> 4.48 us  [the longest x1 3.47 us: per_device(): got = [around(sent[d], 'row', d) for d in range(1, NROW)]]
    pallas_call x4 -> x3, Pallas kernels: 31.1 us -> 28.3 us  [the longest x1 20.9 us: attend(): pl.pallas_call(attend_kernel, grid=(NCOL // FWD_C,), out_shape=(jax.Shape...]
  transfers between devices with their start and end apart: 15 -> 22, of which waited for: 12 -> 12; matrix products, arithmetic and copies ran while one was open for 5% -> 6% of each run, Pallas kernels for 22% -> 23%
where the time goes in v3:
time: 328 us; the launch traced here: 326 us
  waiting for transfers between devices  90.3 us (28%)
  Pallas kernels  89 us (27%)
  starting transfers between devices  75.3 us (23%)
  local copies, waits for them, and re-layouts  38.7 us (12%)
  between operations  14.5 us (4%)
  blocking collectives  12.3 us (4%)
  other arithmetic  6.4 us (2%)
    all_to_all x11, waiting for transfers between devices, exchange(): return lax.all_to_all(blocks, axis, 0, 0, tiled=True)  88.3 us
    all_to_all x11, starting transfers between devices, exchange(): return lax.all_to_all(blocks, axis, 0, 0, tiled=True)  56 us
    pallas_call x1, Pallas kernels, attend(): pl.pallas_call(attend_kernel, grid=(NCOL // FWD_C,), out_shape=(jax.Shape...  20.9 us
    pallas_call x1, Pallas kernels, attend_back_first(): pl.pallas_call(back_first_kernel, grid=(BACK_STEPS,), out_shape=(jax.Shap...  20.6 us
    pallas_call x1, Pallas kernels, attend_back_second(): pl.pallas_call(back_second_kernel, grid=(BACK_STEPS,), out_shape=jax.Shap...  19.6 us
    unnamed x52, local copies, waits for them, and re-layouts  16 us
    ppermute x3, starting transfers between devices, swap_cores(): return lax.ppermute(v, 'dp', [(0, 1), (1, 0)])  13.3 us
    pallas_call x1, Pallas kernels, tokenwise(): pl.pallas_call(tokenwise_kernel, out_shape=(jax.ShapeDtypeStruct((NROW, S...  13.1 us
  transfers between devices with their start and end apart: 22, of which 12 were waited for; matrix products, arithmetic and copies ran while one was open for 6% of the time, Pallas kernels for 23%

profile of v3, /device:TPU:1, one launch (start us, length us, event | category | flops | bytes accessed | tf_op | source)
XLA Modules:
  0.0 326.5 jit_solution(2746426313935775812)
XLA Ops:
  11.1 8.6 %all-to-all-start = ((bf16[16,48,128]{2,1,0:T(8,128)(2,1)}), bf16[16,48,128]{2,1,0:T(8,128)(2,1)S(1)}, u32[]{:S(2)}, u32[]{:S(2)}) async-start(bf16[16,48,128]{2,1,0:T(8,128)(2,1)} %bitcast_bitcast_fusion.1), calls=%async_computation | async-start | bytes 393216 | tf_op jit(solution)/shard_map/all_to_all | solution.py:714
  22.3 4.6 %all-to-all-done.x_ref = bf16[16,48,128]{2,1,0:T(8,128)(2,1)S(1)} async-done(((bf16[16,48,128]{2,1,0:T(8,128)(2,1)}), bf16[16,48,128]{2,1,0:T(8,128)(2,1)S(1)}, u32[]{:S(2)}, u32[]{:S(2)}) %all-to-all-start) | async-done | bytes 196640 | tf_op jit(solution)/shard_map/all_to_all | solution.py:714
  28.0 3.6 %all-to-all-start.1 = ((bf16[16,48,640]{2,1,0:T(8,128)(2,1)}), bf16[16,48,640]{2,1,0:T(8,128)(2,1)S(1)}, u32[]{:S(2)}, u32[]{:S(2)}) async-start(bf16[16,48,640]{2,1,0:T(8,128)(2,1)} %broadcast_in_dim.4), calls=%async_computation.1 | async-start | bytes 1966080 | tf_op jit(solution)/shard_map/all_to_all | solution.py:714
  32.0 12.3 %all_gather.9.x_ref = bf16[4,768,128]{2,1,0:T(8,128)(2,1)S(1)} all-gather(bf16[1,768,128]{2,1,0:T(8,128)(2,1)S(1)} %bitcast.121), channel_id=1, replica_groups=mesh['dp'=2,'row'=4,'z'=4,'y'=4] {'row'}, dimensions={0}, use_global_device_ids=true | all-gather | bytes 983040 | tf_op jit(solution)/shard_map/all_gather | solution.py:766
  44.3 2.1 all-to-all-done.1.w_ref.vec_ref
  48.9 4.7 %all-to-all-start.2 = ((bf16[16,624,128]{2,1,0:T(8,128)(2,1)}), bf16[16,624,128]{2,1,0:T(8,128)(2,1)S(1)}, u32[]{:S(2)}, u32[]{:S(2)}) async-start(bf16[16,624,128]{2,1,0:T(8,128)(2,1)} %copy-done.3), calls=%async_computation.2 | async-start | bytes 5111808 | tf_op jit(solution)/shard_map/all_to_all | solution.py:714
  57.6 28.9 %all-to-all-done.2.q_ref.kv_ref.cot_ref = bf16[16,624,128]{2,1,0:T(8,128)(2,1)S(1)} async-done(((bf16[16,624,128]{2,1,0:T(8,128)(2,1)}), bf16[16,624,128]{2,1,0:T(8,128)(2,1)S(1)}, u32[]{:S(2)}, u32[]{:S(2)}) %all-to-all-start.2) | async-done | bytes 2555936 | tf_op jit(solution)/shard_map/all_to_all | solution.py:714
  88.0 20.9 %attend.1 = (bf16[1664,144]{1,0:T(8,128)(2,1)}, f32[1664,64]{1,0:T(8,128)}, bf16[16,64,128]{2,1,0:T(8,128)(2,1)}) custom-call(bf16[16,624,128]{2,1,0:T(8,128)(2,1)} %copy-done.1, bf16[16,624,128]{2,1,0:T(8,128)(2,1)} %copy-done.1, s32[1664,1]{1,0:T(8,128)} %reshape.199.segq_ref, s32[8,8,128]{2,1,0:T(8,128)} %bitcast.132), custom_call_target="tpu_custom_call" | custom-call | flops 20000000000 | bytes 40000000 | tf_op jit(solution)/shard_map/attend/pallas_call | solution.py:197
  108.8 7.0 %all-to-all-start.3 = ((bf16[16,64,128]{2,1,0:T(8,128)(2,1)}), bf16[16,64,128]{2,1,0:T(8,128)(2,1)}, u32[]{:S(2)}, u32[]{:S(2)}) async-start(bf16[16,64,128]{2,1,0:T(8,128)(2,1)} %get-tuple-element.54), calls=%async_computation.3 | async-start | bytes 524288 | tf_op jit(solution)/shard_map/all_to_all | solution.py:714
  116.2 7.3 %all-to-all-done.3.got_ref = bf16[16,64,128]{2,1,0:T(8,128)(2,1)} async-done(((bf16[16,64,128]{2,1,0:T(8,128)(2,1)}), bf16[16,64,128]{2,1,0:T(8,128)(2,1)}, u32[]{:S(2)}, u32[]{:S(2)}) %all-to-all-start.3) | async-done | bytes 262176 | tf_op jit(solution)/shard_map/all_to_all | solution.py:714
  125.3 4.6 %all-to-all-start.4 = ((bf16[4,144,192]{2,1,0:T(8,128)(2,1)}), bf16[4,144,192]{2,1,0:T(8,128)(2,1)}, u32[]{:S(2)}, u32[]{:S(2)}) async-start(bf16[4,144,192]{2,1,0:T(8,128)(2,1)} %to_row.1.att_ref), calls=%async_computation.4 | async-start | bytes 589824 | tf_op jit(solution)/shard_map/all_to_all | solution.py:714
  129.9 5.8 %all-to-all-done.4.att_ref = bf16[4,144,192]{2,1,0:T(8,128)(2,1)} async-done(((bf16[4,144,192]{2,1,0:T(8,128)(2,1)}), bf16[4,144,192]{2,1,0:T(8,128)(2,1)}, u32[]{:S(2)}, u32[]{:S(2)}) %all-to-all-start.4) | async-done | bytes 221216 | tf_op jit(solution)/shard_map/all_to_all | solution.py:714
  137.8 13.1 %tokenwise.1 = (bf16[4,3888,128]{2,1,0:T(8,128)(2,1)}, bf16[4,128,192]{2,1,0:T(8,128)(2,1)S(1)}, bf16[16,48,128]{2,1,0:T(8,128)(2,1)S(1)}, f32[768,128]{1,0:T(8,128)S(1)}) custom-call(s32[1]{0:T(128)} %bitcast.13.row_ref, bf16[4,144,192]{2,1,0:T(8,128)(2,1)} %all-to-all-done.4.att_ref, bf16[16,48,128]{2,1,0:T(8,128)(2,1)S(1)} %copy-done.8, ...), custom_call_target="tpu_custom_call" | custom-call | flops 15000000512 | bytes 30000000 | tf_op jit(solution)/shard_map/tokenwise/pallas_call | solution.py:528
  154.9 3.4 %all-to-all-start.5 = ((bf16[4,128,192]{1,2,0:T(8,128)(2,1)}), bf16[4,128,192]{1,2,0:T(8,128)(2,1)S(1)}, u32[]{:S(2)}, u32[]{:S(2)}) async-start(bf16[4,128,192]{1,2,0:T(8,128)(2,1)} %copy.68), calls=%async_computation.5 | async-start | bytes 393216 | tf_op jit(solution)/shard_map/all_to_all | solution.py:714
  159.7 3.7 %all-to-all-done.5 = bf16[4,128,192]{1,2,0:T(8,128)(2,1)S(1)} async-done(((bf16[4,128,192]{1,2,0:T(8,128)(2,1)}), bf16[4,128,192]{1,2,0:T(8,128)(2,1)S(1)}, u32[]{:S(2)}, u32[]{:S(2)}) %all-to-all-start.5) | async-done | bytes 196640 | tf_op jit(solution)/shard_map/all_to_all | solution.py:714
  164.4 3.5 %all-to-all-start.6 = ((bf16[16,64,128]{2,1,0:T(8,128)(2,1)}), bf16[16,64,128]{2,1,0:T(8,128)(2,1)S(1)}, u32[]{:S(2)}, u32[]{:S(2)}) async-start(bf16[16,64,128]{2,1,0:T(8,128)(2,1)} %to_col.1), calls=%async_computation.6 | async-start | bytes 524288 | tf_op jit(solution)/shard_map/all_to_all | solution.py:714
  167.9 3.5 %slice_bitcast_fusion = (bf16[3888,128]{1,0:T(8,128)(2,1)}, bf16[3888,128]{1,0:T(8,128)(2,1)}, bf16[3888,128]{1,0:T(8,128)(2,1)}) fusion(bf16[4,3888,128]{2,1,0:T(8,128)(2,1)} %get-tuple-element.69.own_ref), kind=kLoop, calls=%fused_computation.2 | loop fusion | bytes 5971968 | tf_op jit(solution)/shard_map/squeeze | solution.py:806
  176.2 20.6 %attend_back_first.1 = (bf16[16,304,128]{2,1,0:T(8,128)(2,1)}, bf16[1664,80]{1,0:T(8,128)(2,1)}, bf16[128,1664]{1,0:T(8,128)(2,1)}, f32[1664,128]{1,0:T(8,128)}) custom-call(bf16[16,624,128]{2,1,0:T(8,128)(2,1)} %copy-done.1, bf16[16,64,128]{2,1,0:T(8,128)(2,1)} %copy-done.19, bf16[1664,144]{1,0:T(8,128)(2,1)} %get-tuple-element.53.qa_ref, ...), custom_call_target="tpu_custom_call" | custom-call | flops 17999998976 | bytes 36000000 | tf_op jit(solution)/shard_map/attend_back_first/pallas_call | solution.py:294
  196.7 5.3 %all-to-all-start.7 = ((bf16[16,304,128]{2,1,0:T(8,128)(2,1)}), bf16[16,304,128]{2,1,0:T(8,128)(2,1)S(1)}, u32[]{:S(2)}, u32[]{:S(2)}) async-start(bf16[16,304,128]{2,1,0:T(8,128)(2,1)} %get-tuple-element.66), calls=%async_computation.7 | async-start | bytes 2490368 | tf_op jit(solution)/shard_map/all_to_all | solution.py:714
  202.0 19.6 %attend_back_second.1 = bf16[16,320,128]{2,1,0:T(8,128)(2,1)} custom-call(bf16[1664,144]{1,0:T(8,128)(2,1)} %get-tuple-element.53.qa_ref, bf16[1664,80]{1,0:T(8,128)(2,1)} %get-tuple-element.63.doa_ref, bf16[128,1664]{1,0:T(8,128)(2,1)} %get-tuple-element.64.turned_ref, f32[1664,128]{1,0:T(8,128)} %get-tuple-element.65.acc_in, ...), custom_call_target="tpu_custom_call" | custom-call | flops 17999998976 | bytes 36000000 | tf_op jit(solution)/shard_map/attend_back_second/pallas_call | solution.py:327
  222.6 6.5 %weight_grads.1 = (bf16[16,384,128]{2,1,0:T(8,128)(2,1)}, bf16[16,384,128]{2,1,0:T(8,128)(2,1)}) custom-call(s32[1]{0:T(128)} %bitcast.21.core_ref, s32[1]{0:T(128)} %bitcast.13.row_ref, bf16[4,3888,128]{2,1,0:T(8,128)(2,1)} %get-tuple-element.69.own_ref, bf16[3888,128]{1,0:T(8,128)(2,1)} %copy-done.17, bf16[3888,128]{1,0:T(8,128)(2,1)} %collective-permute-done.1.got_2, ...), custom_call_target="tpu_custom_call" | custom-call | flops 1000000000 | bytes 2000000 | tf_op jit(solution)/shard_map/weight_grads/pallas_call | solution.py:630
  229.0 7.2 %collective-permute-start.3 = (bf16[16,384,128]{2,1,0:T(8,128)(2,1)}, bf16[16,384,128]{2,1,0:T(8,128)(2,1)}, u32[]{:S(2)}, u32[]{:S(2)}) collective-permute-start(bf16[16,384,128]{2,1,0:T(8,128)(2,1)} %get-tuple-element.74), channel_id=1, source_target_pairs={{0,64},{64,0},{1,65},{65,1},{2,66},{66,2},{3,67},{67,3},{4,68},{68... | collective-permute-start | bytes 4718600 | tf_op jit(solution)/shard_map/ppermute | solution.py:722
  236.3 6.9 %all-to-all-start.8 = ((bf16[16,320,128]{2,1,0:T(8,128)(2,1)}), bf16[16,320,128]{2,1,0:T(8,128)(2,1)S(1)}, u32[]{:S(2)}, u32[]{:S(2)}) async-start(bf16[16,320,128]{2,1,0:T(8,128)(2,1)} %attend_back_second.1), calls=%async_computation.8 | async-start | bytes 2621440 | tf_op jit(solution)/shard_map/all_to_all | solution.py:714
  243.3 3.5 %add_convert_fusion = bf16[16,384,128]{2,1,0:T(8,128)(2,1)} fusion(bf16[16,384,128]{2,1,0:T(8,128)(2,1)} %collective-permute-done.3, bf16[16,384,128]{2,1,0:T(8,128)(2,1)} %get-tuple-element.73), kind=kLoop, calls=%fused_computation | loop fusion | flops 3145728 | bytes 4718592 | tf_op jit(solution)/shard_map/convert_element_type | solution.py:816
  246.8 18.1 %all-to-all-done.8.second_ref = bf16[16,320,128]{2,1,0:T(8,128)(2,1)S(1)} async-done(((bf16[16,320,128]{2,1,0:T(8,128)(2,1)}), bf16[16,320,128]{2,1,0:T(8,128)(2,1)S(1)}, u32[]{:S(2)}, u32[]{:S(2)}) %all-to-all-start.8) | async-done | bytes 1310752 | tf_op jit(solution)/shard_map/all_to_all | solution.py:714
  266.1 3.6 %project_back.1 = (bf16[4,768,128]{2,1,0:T(8,128)(2,1)}, bf16[16,128,128]{2,1,0:T(8,128)(2,1)S(1)}, bf16[16,128,128]{2,1,0:T(8,128)(2,1)S(1)}) custom-call(s32[1]{0:T(128)} %bitcast.21.core_ref, bf16[16,304,128]{2,1,0:T(8,128)(2,1)S(1)} %all-to-all-done.7.first_ref, bf16[16,320,128]{2,1,0:T(8,128)(2,1)S(1)} %all-to-all-done.8.second_ref, ...), custom_call_target="tpu_custom_call" | custom-call | flops 5000000000 | bytes 10000000 | tf_op jit(solution)/shard_map/project_back/pallas_call | solution.py:681
  271.3 4.0 %all-to-all-start.9 = ((bf16[4,768,128]{2,1,0:T(8,128)(2,1)}), bf16[4,768,128]{2,1,0:T(8,128)(2,1)S(1)}, u32[]{:S(2)}, u32[]{:S(2)}) async-start(bf16[4,768,128]{2,1,0:T(8,128)(2,1)} %get-tuple-element.79), calls=%async_computation.9 | async-start | bytes 1572864 | tf_op jit(solution)/shard_map/all_to_all | solution.py:714
  278.3 8.0 %all-to-all-done.9.din_ref = bf16[4,768,128]{2,1,0:T(8,128)(2,1)S(1)} async-done(((bf16[4,768,128]{2,1,0:T(8,128)(2,1)}), bf16[4,768,128]{2,1,0:T(8,128)(2,1)S(1)}, u32[]{:S(2)}, u32[]{:S(2)}) %all-to-all-start.9) | async-done | bytes 786464 | tf_op jit(solution)/shard_map/all_to_all | solution.py:714
  290.5 2.1 collective-permute-start.6
  293.8 4.3 %all-to-all-start.10 = ((bf16[16,176,128]{2,1,0:T(8,128)(2,1)}), bf16[16,176,128]{2,1,0:T(8,128)(2,1)S(1)}, u32[]{:S(2)}, u32[]{:S(2)}) async-start(bf16[16,176,128]{2,1,0:T(8,128)(2,1)} %last_payload.1), calls=%async_computation.11 | async-start | bytes 1441792 | tf_op jit(solution)/shard_map/all_to_all | solution.py:714
  299.7 8.4 %all-to-all-done.10 = bf16[16,176,128]{2,1,0:T(8,128)(2,1)S(1)} async-done(((bf16[16,176,128]{2,1,0:T(8,128)(2,1)}), bf16[16,176,128]{2,1,0:T(8,128)(2,1)S(1)}, u32[]{:S(2)}, u32[]{:S(2)}) %all-to-all-start.10) | async-done | bytes 720928 | tf_op jit(solution)/shard_map/all_to_all | solution.py:714
  308.2 4.6 %collective-permute-start.8 = (f32[512,128]{1,0:T(8,128)S(1)}, f32[512,128]{1,0:T(8,128)S(1)}, u32[]{:S(2)}, u32[]{:S(2)}) collective-permute-start(f32[512,128]{1,0:T(8,128)S(1)} %pad_maximum_fusion.1), channel_id=1, source_target_pairs={{0,64},{64,0},{1,65},{65,1},{2,66},{66,2},{3,67},{67,3},{4,68},{68... | collective-permute-start | bytes 786440 | tf_op jit(solution)/shard_map/ppermute | solution.py:722
  (155 shorter events, 51.6 us)
Async XLA Ops:
  7.2 15.0 %copy-start.22 = (f32[384]{0:T(512)S(1)}, f32[384]{0:T(512)}, u32[]{:S(2)}) copy-start(f32[384]{0:T(512)} %param.18) | copy-start | bytes 4612
  7.2 128.5 %all-gather.3.cloned.1.call-start = ((), (), s32[]{:S(2)}) async-start(), calls=%async_computation.13 | async-start | bytes 11096064 | tf_op jit(solution)/shard_map/all_gather | solution.py:779
  11.1 15.8 %all-to-all-start = ((bf16[16,48,128]{2,1,0:T(8,128)(2,1)}), bf16[16,48,128]{2,1,0:T(8,128)(2,1)S(1)}, u32[]{:S(2)}, u32[]{:S(2)}) async-start(bf16[16,48,128]{2,1,0:T(8,128)(2,1)} %bitcast_bitcast_fusion.1), calls=%async_computation | async-start | bytes 393216 | tf_op jit(solution)/shard_map/all_to_all | solution.py:714
  22.2 9.7 %copy-start.20 = (bf16[48,2048]{1,0:T(8,128)(2,1)S(1)}, bf16[48,2048]{1,0:T(8,128)(2,1)}, u32[]{:S(2)}) copy-start(bf16[48,2048]{1,0:T(8,128)(2,1)} %param.29) | copy-start | bytes 589828
  27.0 5.0 %copy-start.7 = (bf16[16,48,128]{2,1,0:T(8,128)(2,1)}, bf16[16,48,128]{2,1,0:T(8,128)(2,1)S(1)}, u32[]{:S(2)}) copy-start(bf16[16,48,128]{2,1,0:T(8,128)(2,1)S(1)} %all-to-all-done.x_ref) | copy-start | bytes 589828
  28.0 18.4 %all-to-all-start.1 = ((bf16[16,48,640]{2,1,0:T(8,128)(2,1)}), bf16[16,48,640]{2,1,0:T(8,128)(2,1)S(1)}, u32[]{:S(2)}, u32[]{:S(2)}) async-start(bf16[16,48,640]{2,1,0:T(8,128)(2,1)} %broadcast_in_dim.4), calls=%async_computation.1 | async-start | bytes 1966080 | tf_op jit(solution)/shard_map/all_to_all | solution.py:714
  47.4 1.5 copy-start.3
  48.9 37.6 %all-to-all-start.2 = ((bf16[16,624,128]{2,1,0:T(8,128)(2,1)}), bf16[16,624,128]{2,1,0:T(8,128)(2,1)S(1)}, u32[]{:S(2)}, u32[]{:S(2)}) async-start(bf16[16,624,128]{2,1,0:T(8,128)(2,1)} %copy-done.3), calls=%async_computation.2 | async-start | bytes 5111808 | tf_op jit(solution)/shard_map/all_to_all | solution.py:714
  86.5 1.5 copy-start.1
  88.0 27.9 %copy-start.21 = (f32[768]{0:T(1024)S(1)}, f32[768]{0:T(1024)}, u32[]{:S(2)}) copy-start(f32[768]{0:T(1024)} %param.24) | copy-start | bytes 9220
  108.8 14.6 %all-to-all-start.3 = ((bf16[16,64,128]{2,1,0:T(8,128)(2,1)}), bf16[16,64,128]{2,1,0:T(8,128)(2,1)}, u32[]{:S(2)}, u32[]{:S(2)}) async-start(bf16[16,64,128]{2,1,0:T(8,128)(2,1)} %get-tuple-element.54), calls=%async_computation.3 | async-start | bytes 524288 | tf_op jit(solution)/shard_map/all_to_all | solution.py:714
  116.2 19.6 %copy-start.2 = (bf16[16,624,128]{2,1,0:T(8,128)(2,1)S(1)}, bf16[16,624,128]{2,1,0:T(8,128)(2,1)}, u32[]{:S(2)}) copy-start(bf16[16,624,128]{2,1,0:T(8,128)(2,1)} %copy-done.1) | copy-start | bytes 7667716
  125.3 10.4 %all-to-all-start.4 = ((bf16[4,144,192]{2,1,0:T(8,128)(2,1)}), bf16[4,144,192]{2,1,0:T(8,128)(2,1)}, u32[]{:S(2)}, u32[]{:S(2)}) async-start(bf16[4,144,192]{2,1,0:T(8,128)(2,1)} %to_row.1.att_ref), calls=%async_computation.4 | async-start | bytes 589824 | tf_op jit(solution)/shard_map/all_to_all | solution.py:714
  135.7 1.2 copy-start.5
  154.9 8.5 %all-to-all-start.5 = ((bf16[4,128,192]{1,2,0:T(8,128)(2,1)}), bf16[4,128,192]{1,2,0:T(8,128)(2,1)S(1)}, u32[]{:S(2)}, u32[]{:S(2)}) async-start(bf16[4,128,192]{1,2,0:T(8,128)(2,1)} %copy.68), calls=%async_computation.5 | async-start | bytes 393216 | tf_op jit(solution)/shard_map/all_to_all | solution.py:714
  164.4 11.0 %all-to-all-start.6 = ((bf16[16,64,128]{2,1,0:T(8,128)(2,1)}), bf16[16,64,128]{2,1,0:T(8,128)(2,1)S(1)}, u32[]{:S(2)}, u32[]{:S(2)}) async-start(bf16[16,64,128]{2,1,0:T(8,128)(2,1)} %to_col.1), calls=%async_computation.6 | async-start | bytes 524288 | tf_op jit(solution)/shard_map/all_to_all | solution.py:714
  171.4 50.2 %collective-permute-start = (bf16[3888,128]{1,0:T(8,128)(2,1)}, bf16[3888,128]{1,0:T(8,128)(2,1)S(1)}, u32[]{:S(2)}, u32[]{:S(2)}) collective-permute-start(bf16[3888,128]{1,0:T(8,128)(2,1)} %get-tuple-element.88), channel_id=1, source_target_pairs={{0,16},{16,32},{32,48},{48,0},{1,17},{17,33},{33,49},{49,1},{2,18}... | collective-permute-start | bytes 2985992 | tf_op jit(solution)/shard_map/ppermute | solution.py:718
  171.7 49.9 %collective-permute-start.1 = (bf16[3888,128]{1,0:T(8,128)(2,1)}, bf16[3888,128]{1,0:T(8,128)(2,1)}, u32[]{:S(2)}, u32[]{:S(2)}) collective-permute-start(bf16[3888,128]{1,0:T(8,128)(2,1)} %get-tuple-element.87), channel_id=1, source_target_pairs={{0,32},{16,48},{32,0},{48,16},{1,33},{17,49},{33,1},{49,17},{2,34}... | collective-permute-start | bytes 2985992 | tf_op jit(solution)/shard_map/ppermute | solution.py:718
  173.5 48.1 %collective-permute-start.2 = (bf16[3888,128]{1,0:T(8,128)(2,1)}, bf16[3888,128]{1,0:T(8,128)(2,1)}, u32[]{:S(2)}, u32[]{:S(2)}) collective-permute-start(bf16[3888,128]{1,0:T(8,128)(2,1)} %get-tuple-element.86), channel_id=1, source_target_pairs={{0,48},{16,0},{32,16},{48,32},{1,49},{17,1},{33,17},{49,33},{2,50}... | collective-permute-start | bytes 2985992 | tf_op jit(solution)/shard_map/ppermute | solution.py:718
  196.7 39.6 %all-to-all-start.7 = ((bf16[16,304,128]{2,1,0:T(8,128)(2,1)}), bf16[16,304,128]{2,1,0:T(8,128)(2,1)S(1)}, u32[]{:S(2)}, u32[]{:S(2)}) async-start(bf16[16,304,128]{2,1,0:T(8,128)(2,1)} %get-tuple-element.66), calls=%async_computation.7 | async-start | bytes 2490368 | tf_op jit(solution)/shard_map/all_to_all | solution.py:714
  229.0 14.2 %collective-permute-start.3 = (bf16[16,384,128]{2,1,0:T(8,128)(2,1)}, bf16[16,384,128]{2,1,0:T(8,128)(2,1)}, u32[]{:S(2)}, u32[]{:S(2)}) collective-permute-start(bf16[16,384,128]{2,1,0:T(8,128)(2,1)} %get-tuple-element.74), channel_id=1, source_target_pairs={{0,64},{64,0},{1,65},{65,1},{2,66},{66,2},{3,67},{67,3},{4,68},{68... | collective-permute-start | bytes 4718600 | tf_op jit(solution)/shard_map/ppermute | solution.py:722
  236.3 28.6 %all-to-all-start.8 = ((bf16[16,320,128]{2,1,0:T(8,128)(2,1)}), bf16[16,320,128]{2,1,0:T(8,128)(2,1)S(1)}, u32[]{:S(2)}, u32[]{:S(2)}) async-start(bf16[16,320,128]{2,1,0:T(8,128)(2,1)} %attend_back_second.1), calls=%async_computation.8 | async-start | bytes 2621440 | tf_op jit(solution)/shard_map/all_to_all | solution.py:714
  243.2 46.2 %reduce-scatter.2.cloned.1.call-start = ((), (), s32[]{:S(2)}) async-start(), calls=%async_computation.12 | async-start | bytes 1966080 | tf_op jit(solution)/shard_map/reduce_scatter | solution.py:818
  264.9 1.2 copy-start.6
  271.3 4.0 %copy-start.11 = (bf16[16,128,128]{2,1,0:T(8,128)(2,1)S(1)}, bf16[16,128,128]{2,1,0:T(8,128)(2,1)}, u32[]{:S(2)}) copy-start(bf16[16,128,128]{2,1,0:T(8,128)(2,1)} %copy-done.10) | copy-start | bytes 1572868
  271.3 14.9 %all-to-all-start.9 = ((bf16[4,768,128]{2,1,0:T(8,128)(2,1)}), bf16[4,768,128]{2,1,0:T(8,128)(2,1)S(1)}, u32[]{:S(2)}, u32[]{:S(2)}) async-start(bf16[4,768,128]{2,1,0:T(8,128)(2,1)} %get-tuple-element.79), calls=%async_computation.9 | async-start | bytes 1572864 | tf_op jit(solution)/shard_map/all_to_all | solution.py:714
  275.3 2.9 collective-permute-start.4
  290.4 8.3 %collective-permute-start.5 = (bf16[384,128]{1,0:T(8,128)(2,1)S(1)}, bf16[384,128]{1,0:T(8,128)(2,1)S(1)}, u32[]{:S(2)}, u32[]{:S(2)}) collective-permute-start(bf16[384,128]{1,0:T(8,128)(2,1)S(1)} %get-tuple-element.91), channel_id=1, source_target_pairs={{0,1},{1,2},{2,3},{3,0},{4,5},{5,6},{6,7},{7,4},{8,9},{9,10},{10,1... | collective-permute-start | bytes 294920 | tf_op jit(solution)/shard_map/ppermute | solution.py:718
  290.5 8.2 %collective-permute-start.6 = (bf16[384,128]{1,0:T(8,128)(2,1)S(1)}, bf16[384,128]{1,0:T(8,128)(2,1)S(1)}, u32[]{:S(2)}, u32[]{:S(2)}) collective-permute-start(bf16[384,128]{1,0:T(8,128)(2,1)S(1)} %get-tuple-element.93), channel_id=1, source_target_pairs={{0,2},{1,3},{2,0},{3,1},{4,6},{5,7},{6,4},{7,5},{8,10},{9,11},{10,... | collective-permute-start | bytes 294920 | tf_op jit(solution)/shard_map/ppermute | solution.py:718
  292.6 6.1 %collective-permute-start.7 = (bf16[384,128]{1,0:T(8,128)(2,1)S(1)}, bf16[384,128]{1,0:T(8,128)(2,1)S(1)}, u32[]{:S(2)}, u32[]{:S(2)}) collective-permute-start(bf16[384,128]{1,0:T(8,128)(2,1)S(1)} %get-tuple-element.92), channel_id=1, source_target_pairs={{0,3},{1,0},{2,1},{3,2},{4,7},{5,4},{6,5},{7,6},{8,11},{9,8},{10,9... | collective-permute-start | bytes 294920 | tf_op jit(solution)/shard_map/ppermute | solution.py:718
  293.8 14.3 %all-to-all-start.10 = ((bf16[16,176,128]{2,1,0:T(8,128)(2,1)}), bf16[16,176,128]{2,1,0:T(8,128)(2,1)S(1)}, u32[]{:S(2)}, u32[]{:S(2)}) async-start(bf16[16,176,128]{2,1,0:T(8,128)(2,1)} %last_payload.1), calls=%async_computation.11 | async-start | bytes 1441792 | tf_op jit(solution)/shard_map/all_to_all | solution.py:714
  308.2 5.8 %collective-permute-start.8 = (f32[512,128]{1,0:T(8,128)S(1)}, f32[512,128]{1,0:T(8,128)S(1)}, u32[]{:S(2)}, u32[]{:S(2)}) collective-permute-start(f32[512,128]{1,0:T(8,128)S(1)} %pad_maximum_fusion.1), channel_id=1, source_target_pairs={{0,64},{64,0},{1,65},{65,1},{2,66},{66,2},{3,67},{67,3},{4,68},{68... | collective-permute-start | bytes 786440 | tf_op jit(solution)/shard_map/ppermute | solution.py:722
  (13 other events, 10.9 us)
Sparse Core Ops, SparseCore 0:
  11.5 100.2 all-gather.2
  265.0 22.7 reduce-scatter.1

commit v4 on v3

--- a/solution.py
+++ b/solution.py
@@ -51,8 +51,24 @@
     return lax.dot_general(a, b, (((ca,), (cb,)), ((), ())), preferred_element_type=F32)
 
 
-def params(limit):
-    return pltpu.CompilerParams(vmem_limit_bytes=limit * MIB)
+LIMITS = {
+    "project": 16,
+    "attend": 32,
+    "attend_back_first": 63,
+    "attend_back_second": 63,
+    "to_row": 8,
+    "to_col": 8,
+    "tokenwise": 63,
+    "weight_grads": 63,
+    "project_back": 20,
+    "last_payload": 12,
+    "finish": 12,
+    "joint_gradient": 8,
+}
+
+
+def params(name):
+    return pltpu.CompilerParams(vmem_limit_bytes=LIMITS[name] * MIB)
 
 
 def cost(us):
@@ -89,11 +105,11 @@
 def project(x4, wj, bias, cot):
     return pl.pallas_call(
         project_kernel,
-        out_shape=jax.ShapeDtypeStruct((NCOL, BLOCK, 128), BF),
+        out_shape=pltpu.HBM((NCOL, BLOCK, 128), BF),
         in_specs=[VMEM] * 4,
         out_specs=VMEM,
         scratch_shapes=[pltpu.VMEM((640, 256), F32)],
-        compiler_params=params(40),
+        compiler_params=params("project"),
         cost_estimate=cost(3),
         name="project",
     )(x4, wj, bias, cot)
@@ -198,9 +214,9 @@
         attend_kernel,
         grid=(NCOL // FWD_C,),
         out_shape=(
-            jax.ShapeDtypeStruct((ROWS, AUG), BF),
-            jax.ShapeDtypeStruct((ROWS, HDIM), F32),
-            jax.ShapeDtypeStruct((NCOL, 64, 128), BF),
+            pltpu.HBM((ROWS, AUG), BF),
+            pltpu.HBM((ROWS, HDIM), F32),
+            pltpu.HBM((NCOL, 64, 128), BF),
         ),
         in_specs=[
             Q_BLOCK,
@@ -214,7 +230,7 @@
             pltpu.VMEM((ROWS, 128), F32),
             pltpu.VMEM((ROWS, 128), F32),
         ],
-        compiler_params=params(60),
+        compiler_params=params("attend"),
         cost_estimate=cost(20),
         name="attend",
     )(arrived, arrived, segq, seg)
@@ -295,10 +311,10 @@
         back_first_kernel,
         grid=(BACK_STEPS,),
         out_shape=(
-            jax.ShapeDtypeStruct((NCOL, 304, 128), BF),
-            jax.ShapeDtypeStruct((ROWS, 80), BF),
-            jax.ShapeDtypeStruct((128, ROWS), BF),
-            jax.ShapeDtypeStruct((ROWS, 128), F32),
+            pltpu.HBM((NCOL, 304, 128), BF),
+            pltpu.HBM((ROWS, 80), BF),
+            pltpu.HBM((128, ROWS), BF),
+            pltpu.HBM((ROWS, 128), F32),
         ),
         in_specs=[
             Q_BLOCK,
@@ -316,7 +332,7 @@
             whole((ROWS, 128)),
         ],
         scratch_shapes=[pltpu.VMEM((ROWS, 128), F32)],
-        compiler_params=params(58),
+        compiler_params=params("attend_back_first"),
         cost_estimate=cost(18),
         name="attend_back_first",
     )(arrived, grad, qa, o, fin, arrived, seg)
@@ -327,7 +343,7 @@
     return pl.pallas_call(
         back_second_kernel,
         grid=(BACK_STEPS,),
-        out_shape=jax.ShapeDtypeStruct((NCOL, 320, 128), BF),
+        out_shape=pltpu.HBM((NCOL, 320, 128), BF),
         in_specs=[
             whole((ROWS, AUG)),
             whole((ROWS, 80)),
@@ -338,7 +354,7 @@
         ],
         out_specs=whole((NCOL, 320, 128)),
         scratch_shapes=[pltpu.VMEM((ROWS, 128), F32)],
-        compiler_params=params(58),
+        compiler_params=params("attend_back_second"),
         cost_estimate=cost(18),
         name="attend_back_second",
     )(qa, doa, turned, acc, arrived, seg)
@@ -353,22 +369,36 @@
         scr[SHARE * k + 64 : SHARE * (k + 1), lanes] = block[0:TAIL, 64:128]
 
 
+def heads_of(block):
+    return jnp.concatenate(
+        [
+            jnp.concatenate([block[64 * h : 64 * (h + 1), 64 * k : 64 * (k + 1)] for h in range(3)], axis=1)
+            for k in range(2)
+        ],
+        axis=0,
+    )
+
+
 def to_row_kernel(got_ref, bias_ref, out_ref, scr):
     gather_rows(got_ref, scr)
     for r in range(NROW):
-        out_ref[r, 0:TOK, :] = scr[r * TOK : (r + 1) * TOK, :].astype(BF)
-        out_ref[r, TOK : TOK + 16, :] = bias_ref[...]
+        for h in range(3):
+            lanes = slice(HDIM * h, HDIM * (h + 1))
+            a = scr[r * TOK : r * TOK + 64, lanes]
+            b = scr[r * TOK + 64 : (r + 1) * TOK, lanes]
+            out_ref[r, 64 * h : 64 * (h + 1), :] = jnp.concatenate([a, b], axis=1).astype(BF)
+        out_ref[r, 192:224, :] = bias_ref[...]
 
 
 def to_row(got, bias_rows):
     return pl.pallas_call(
         to_row_kernel,
-        out_shape=jax.ShapeDtypeStruct((NROW, TOK + 16, 192), BF),
+        out_shape=pltpu.HBM((NROW, 224, TOK), BF),
         in_specs=[VMEM] * 2,
         out_specs=VMEM,
         scratch_shapes=[pltpu.VMEM((528, 192), F32)],
         cost_estimate=cost(1),
-        compiler_params=params(16),
+        compiler_params=params("to_row"),
         name="to_row",
     )(got, bias_rows)
 
@@ -376,7 +406,7 @@
 def to_col_kernel(got_ref, out_ref, scr):
     scr[512:640, :] = jnp.zeros((128, 192), F32)
     for r in range(NROW):
-        scr[r * TOK : (r + 1) * TOK, :] = got_ref[r].astype(F32)
+        scr[r * TOK : (r + 1) * TOK, :] = heads_of(got_ref[r].astype(F32))
     for j in range(15):
         h, k = j // PER_HEAD, j % PER_HEAD
         lanes = slice(HDIM * h, HDIM * (h + 1))
@@ -389,12 +419,12 @@
 def to_col(got):
     return pl.pallas_call(
         to_col_kernel,
-        out_shape=jax.ShapeDtypeStruct((NCOL, 64, 128), BF),
+        out_shape=pltpu.HBM((NCOL, 64, 128), BF),
         in_specs=[VMEM],
         out_specs=VMEM,
         scratch_shapes=[pltpu.VMEM((640, 192), F32)],
         cost_estimate=cost(1),
-        compiler_params=params(16),
+        compiler_params=params("to_col"),
         name="to_col",
     )(got)
 
@@ -452,7 +482,7 @@
     wait(0)
     attn = jnp.zeros((TOK, DIM), F32)
     for r in range(NROW):
-        rows = att_ref[r, 0:TOK, :]
+        rows = heads_of(att_ref[r, 0:192, :].astype(F32)).astype(BF)
         for k in range(2):
             piece = jnp.concatenate([rows[:, 96 * k : 96 * (k + 1)], gap], axis=1)
             attn = attn + dot(piece, out_ref[k * NROW + r].reshape(DIM, 128), 1, 1)
@@ -467,9 +497,9 @@
     for r in range(NROW):
         wait(1 + r)
         cols = slice(r * DIM, (r + 1) * DIM)
-        parts = att_ref[r, TOK : TOK + 12, :].astype(F32)
-        parts = parts[0:4] + parts[4:8] + parts[8:12]
-        up_b = jnp.concatenate([parts[i : i + 1] for i in range(4)], axis=1)
+        parts = att_ref[r, 192:224, :].astype(F32)
+        parts = parts[0:6] + parts[6:12] + parts[12:18]
+        up_b = jnp.concatenate([parts[i : i + 1] for i in range(6)], axis=1)
         pre = dot(n1_low, up_ref[:, :, cols].reshape(DIM, DIM), 1, 0) + up_b
         phi = 0.5 * (1.0 + lax.erf(pre * (1.0 / math.sqrt(2.0))))
         act = (pre * phi).astype(BF)
@@ -503,7 +533,11 @@
     d_attn = dh1.astype(BF)
     for r in range(NROW):
         pieces = [dot(d_attn, out_ref[k * NROW + r].reshape(DIM, 128), 1, 0)[:, 0:96] for k in range(2)]
-        datt_ref[r] = jnp.concatenate(pieces, axis=1).astype(BF)
+        piece = jnp.concatenate(pieces, axis=1)
+        for h in range(3):
+            lanes = slice(HDIM * h, HDIM * (h + 1))
+            both = jnp.concatenate([piece[0:64, lanes], piece[64:128, lanes]], axis=1)
+            datt_ref[r, 64 * h : 64 * (h + 1), :] = both.astype(BF)
     turned = dh1.T
     dh1_ref[...] = turned
     shared = [n1.T.astype(BF), dh2.T.astype(BF), turned.astype(BF)]
@@ -528,15 +562,15 @@
     return pl.pallas_call(
         tokenwise_kernel,
         out_shape=(
-            jax.ShapeDtypeStruct((NROW, SENT, TOK), BF),
-            jax.ShapeDtypeStruct((NROW, TOK, 192), BF),
-            jax.ShapeDtypeStruct((NCOL, 48, TOK), BF),
-            jax.ShapeDtypeStruct((DIM, TOK), F32),
+            pltpu.HBM((NROW, SENT, TOK), BF),
+            pltpu.HBM((NROW, 192, TOK), BF),
+            pltpu.HBM((NCOL, 48, TOK), BF),
+            pltpu.HBM((DIM, TOK), F32),
         ),
         grid=(1,),
         in_specs=[
             SMEM,
-            whole((NROW, TOK + 16, 192)),
+            whole((NROW, 224, TOK)),
             whole((NCOL, 48, TOK)),
             pl.BlockSpec((NCOL, 48, TOK), lambda i: (0, C_AT // 48, 0)),
             pl.BlockSpec((NCOL, 48, TOK), lambda i: (0, 0, 1)),
@@ -544,7 +578,7 @@
         ],
         out_specs=[
             whole((NROW, SENT, TOK)),
-            whole((NROW, TOK, 192)),
+            whole((NROW, 192, TOK)),
             whole((NCOL, 48, TOK)),
             whole((DIM, TOK)),
         ],
@@ -555,7 +589,7 @@
             pltpu.VMEM((TOK, FF), F32),
             pltpu.SemaphoreType.DMA((9,)),
         ],
-        compiler_params=params(48),
+        compiler_params=params("tokenwise"),
         cost_estimate=cost(15),
         name="tokenwise",
     )(row, att, x_t, arrived, wj, everything)
@@ -603,7 +637,7 @@
     d_pre = hidden(3 * DIM + 48)
     d_branch = feats(DIM)
     d_attn = feats(2 * DIM)
-    att = jnp.concatenate([att_ref[source[r], 0:TOK, :] for r in range(NROW)], axis=0)
+    att = jnp.concatenate([heads_of(att_ref[source[r], 0:192, :].astype(F32)).astype(BF) for r in range(NROW)], axis=0)
     att = jnp.concatenate([att, jnp.zeros((NROW * TOK, 64), BF)], axis=1)
     pieces = chunks(dot(feats(0), d_pre, 1, 0), 6)
     pieces += chunks(dot(d_branch, hidden(4 * DIM + 48), 1, 0), 6)
@@ -626,25 +660,26 @@
 
 
 def weight_grads(core, row, sent, got, att):
-    kind = jax.ShapeDtypeStruct((NCOL, WROWS // 2, 128), BF)
+    kind = pltpu.HBM((NCOL, WROWS // 2, 128), BF)
     return pl.pallas_call(
         weight_grads_kernel,
         out_shape=(kind, kind),
         grid=(1,),
         in_specs=[SMEM, SMEM, pl.BlockSpec((1, SENT, TOK), lambda i: (0, 0, 0))]
         + [whole((SENT, TOK))] * 3
-        + [whole((NROW, TOK + 16, 192))],
+        + [whole((NROW, 224, TOK))],
         out_specs=[whole(kind.shape)] * 2,
-        compiler_params=params(56),
+        compiler_params=params("weight_grads"),
         cost_estimate=cost(1),
         name="weight_grads",
     )(core, row, sent, *got, att)
 
 
 def project_back_kernel(
-    core_ref, first_ref, second_ref, w_ref, x_ref, din_ref, mine_ref, other_ref, scr
+    core_ref, first_ref, second_ref, w_ref, x_ref, din_ref, mine_ref, other_ref, layer_ref, scr
 ):
     core = core_ref[0]
+    layer_ref[...] = jnp.concatenate([first_ref[c, 256:304, :] for c in range(NCOL)], axis=1)
     scr[...] = jnp.zeros_like(scr)
     gather_rows(second_ref, scr, slice(256, 320))
     dq = scr[0:512, :].T.astype(BF)
@@ -677,14 +712,19 @@
 
 
 def project_back(core, first, second, wj, x4):
-    kind = jax.ShapeDtypeStruct((NCOL, 128, 128), BF)
+    kind = pltpu.HBM((NCOL, 128, 128), BF)
     return pl.pallas_call(
         project_back_kernel,
-        out_shape=(jax.ShapeDtypeStruct((NROW, DIM, TOK), BF), kind, kind),
+        out_shape=(
+            pltpu.HBM((NROW, DIM, TOK), BF),
+            kind,
+            kind,
+            pltpu.HBM((48, NCOL * TOK), BF),
+        ),
         in_specs=[SMEM] + [VMEM] * 4,
-        out_specs=[VMEM] * 3,
+        out_specs=[VMEM] * 4,
         scratch_shapes=[pltpu.VMEM((528, 256), F32)],
-        compiler_params=params(48),
+        compiler_params=params("project_back"),
         cost_estimate=cost(5),
         name="project_back",
     )(core, first, second, wj, x4)
@@ -701,13 +741,79 @@
 def last_payload(mine, theirs, din, dh1):
     return pl.pallas_call(
         last_kernel,
-        out_shape=jax.ShapeDtypeStruct((NCOL, 176, 128), BF),
+        out_shape=pltpu.HBM((NCOL, 176, 128), BF),
         in_specs=[VMEM] * 4,
         out_specs=VMEM,
-        compiler_params=params(24),
+        compiler_params=params("last_payload"),
         cost_estimate=cost(1),
         name="last_payload",
     )(mine, theirs, din, dh1)
+
+
+def join(core_ref, mine, theirs):
+    first = core_ref[0] == 0
+    a, b = mine[...], theirs[...]
+    return jnp.concatenate([jnp.where(first, a, b), jnp.where(first, b, a)], axis=0)
+
+
+def finish_kernel(
+    core_ref, col_ref, wide_ref, other_ref, out_ref, up_ref, up_bias_ref, down_ref, *own_refs
+):
+    wide = join(core_ref, wide_ref, other_ref)
+    for i in range(6):
+        lanes = slice(i * 128, (i + 1) * 128)
+        up_ref[:, lanes] = wide[48 * i : 48 * (i + 1)]
+        down_ref[:, lanes] = wide[288 + 48 * i : 288 + 48 * (i + 1)]
+    out_ref[...] = jnp.concatenate([wide[576:624], wide[624:672, 0:64]], axis=1)
+    vecs = wide[672:720] + wide[720:768]
+    up_bias_ref[...] = vecs[36:42]
+    rows = [
+        jnp.concatenate([vecs[6 * v + i : 6 * v + i + 1] for i in range(6)], axis=1) for v in range(6)
+    ]
+    rows = jnp.concatenate(rows + [jnp.zeros((2, DIM), F32)], axis=0)
+    feature = lax.broadcasted_iota(jnp.int32, (DIM, 48), 0)
+    lane = lax.broadcasted_iota(jnp.int32, (DIM, 48), 1)
+    pick = jnp.where(feature == col_ref[0] * 48 + lane, 1.0, 0.0).astype(BF)
+    own = sum(dot(part, pick, 1, 0) for part in split3(rows))
+    for v, ref in enumerate(own_refs):
+        ref[...] = own[v : v + 1]
+
+
+def finish(core, col, wide, other):
+    shapes = [(48, 192), (48, DIM), (6, 128), (48, DIM)] + [(1, 48)] * 6
+    return pl.pallas_call(
+        finish_kernel,
+        out_shape=[pltpu.HBM(shape, F32) for shape in shapes],
+        in_specs=[SMEM] * 2 + [VMEM] * 2,
+        out_specs=[VMEM] * len(shapes),
+        compiler_params=params("finish"),
+        cost_estimate=cost(1),
+        name="finish",
+    )(core, col, wide, other)
+
+
+def joint_kernel(core_ref, last_ref, other_ref, joint_ref, joint_bias_ref):
+    last = join(core_ref, last_ref, other_ref)
+    chunks = [last[48 * i : 48 * (i + 1)] for i in range(5)]
+    heads = [chunks[0][:, 0:64], chunks[0][:, 64:128], chunks[1][:, 0:64]]
+    joint_ref[...] = jnp.concatenate([v for h in range(3) for v in (heads[h], chunks[2 + h])], axis=1)
+    sums = last[240:248] + last[248:256]
+    heads = [sums[0:1, 0:64], sums[0:1, 64:128], sums[1:2, 0:64]]
+    joint_bias_ref[...] = jnp.concatenate(
+        [jnp.concatenate([heads[h], sums[2 + h : 3 + h, 64:128]], axis=1) for h in range(3)], axis=0
+    )
+
+
+def joint_gradient(core, last, other):
+    return pl.pallas_call(
+        joint_kernel,
+        out_shape=[pltpu.HBM(shape, F32) for shape in ((48, 576), (3, 128))],
+        in_specs=[SMEM] + [VMEM] * 2,
+        out_specs=[VMEM] * 2,
+        compiler_params=params("joint_gradient"),
+        cost_estimate=cost(1),
+        name="joint_gradient",
+    )(core, last, other)
 
 
 def exchange(blocks, axis):
@@ -742,7 +848,7 @@
     core = lax.axis_index("dp")
     col = lax.axis_index(COL)
     row = lax.axis_index("row")
-    my_y = lax.axis_index("y")
+    my_z, my_y = lax.axis_index("z"), lax.axis_index("y")
     core_word = core.reshape(1).astype(jnp.int32)
     row_word = row.reshape(1).astype(jnp.int32)
 
@@ -787,7 +893,7 @@
             jnp.concatenate([jnp.zeros((3, HDIM), F32), bias3[:, 1]], axis=1).reshape(384),
         ]
     ).reshape(1, JW)
-    bias_rows = jnp.pad(jnp.concatenate([v.reshape(4, 192) for v in split3(up_bias)]), ((0, 4), (0, 0)))
+    bias_rows = jnp.pad(jnp.concatenate([v.reshape(6, 128) for v in split3(up_bias)]), ((0, 14), (0, 0)))
     seg_k = jnp.transpose(segments.reshape(NROW, NCOL, TOK), (1, 0, 2))
     seg_rows = jnp.pad(seg_k.reshape(NCOL, 512), ((0, 0), (0, 8)))
     seg_q = lax.dynamic_slice_in_dim(seg_rows, lax.rem(col, PER_HEAD) * SHARE, SHARE, 1)
@@ -807,62 +913,44 @@
     back_a, doa, turned_qd, acc = attend_back_first(arrived, grad_o, qa, o, fin, seg_k)
     back_b = attend_back_second(qa, doa, turned_qd, acc, arrived, seg_k)
     back_a = exchange(back_a, COL)
-    late = lax.optimization_barrier((back_b, got, sent))
-    got, sent = late[1:]
+    back_b, got, sent, back_a = lax.optimization_barrier((back_b, got, sent, back_a))
     mine, other = weight_grads(core_word, row_word, sent, got, att_r)
     theirs = swap_cores(other)
     back_b, back_a = lax.optimization_barrier((back_b, back_a))
     back_b = exchange(back_b, COL)
     wide = (mine.astype(F32) + theirs.astype(F32)).astype(BF).reshape(4, 4, WROWS // 2, 128)
-    wide, back_b = lax.optimization_barrier((wide, back_b))
-    wide = lax.psum_scatter(wide, "z", scatter_dimension=0, tiled=False)
-
-    din, mine_j, other_j = project_back(core_word, back_a, back_b, wj, x4)
+    near = [lax.dynamic_index_in_dim(wide, lax.rem(my_z + d, 4), 0, keepdims=False) for d in range(4)]
+    near = [near[0]] + [around(near[d], "z", d) for d in range(1, 4)]
+    wide = near[0].astype(F32) + near[1].astype(F32) + near[2].astype(F32) + near[3].astype(F32)
+    wide = wide.astype(BF)
+
+    din, mine_j, other_j, layer_output = project_back(core_word, back_a, back_b, wj, x4)
     theirs_j = swap_cores(other_j)
     din = exchange(din, "row")
-    mixed = last_payload(mine_j, theirs_j, din, dh1)
-    mixed, wide = lax.optimization_barrier((mixed, wide))
-    mixed = exchange(mixed, COL)
-    wide = lax.dynamic_index_in_dim(wide, my_y, 0, keepdims=False).astype(F32) + sum(
-        around(lax.dynamic_index_in_dim(wide, lax.rem(my_y + d, 4), 0, keepdims=False), "y", d).astype(F32)
-        for d in range(1, 4)
+    near = [lax.dynamic_index_in_dim(wide, lax.rem(my_y + d, 4), 0, keepdims=False) for d in range(4)]
+    din, near = lax.optimization_barrier((din, near))
+    near = [near[0]] + [around(near[d], "y", d) for d in range(1, 4)]
+    mixed = exchange(last_payload(mine_j, theirs_j, din, dh1), COL)
+    wide = near[0].astype(F32) + near[1].astype(F32) + near[2].astype(F32) + near[3].astype(F32)
+    grad_out, grad_up, grad_up_bias, grad_down, *own = finish(
+        core_word, col.reshape(1).astype(jnp.int32), wide, swap_cores(wide)
     )
-
-    layer_output = jnp.transpose(back_a[:, 256:304], (1, 0, 2)).reshape(48, 2048)
-    mixed, wide = lax.optimization_barrier((mixed, wide))
-    mine = jnp.concatenate([wide, jnp.sum(mixed[:, :128].astype(F32), axis=0)], axis=0)
-    theirs = swap_cores(mine)
-    low = jnp.where(core == 0, mine, theirs)
-    high = jnp.where(core == 0, theirs, mine)
-    wide = jnp.concatenate([low[:384], high[:384]], axis=0)
-    last = jnp.concatenate([low[384:], high[384:]], axis=0)
-    as_cols = lambda v, n: jnp.transpose(v.reshape(n, 48, 128), (1, 0, 2)).reshape(48, n * 128)
-    grad_up = as_cols(wide[0:288], 6)
-    grad_down = as_cols(wide[288:576], 6)
-    grad_out = as_cols(wide[576:672], 2)[:, :192].T
-    vecs = (wide[672:720] + wide[720:768])[:42].reshape(7, DIM)
-    own = lax.dynamic_slice_in_dim(vecs[:6], col * 48, 48, 1)
-    grad_up_bias = vecs[6]
+    last = jnp.sum(mixed[:, :128].astype(F32), axis=0)
     grad_inputs = jnp.transpose(mixed[:, 128:].astype(F32), (1, 0, 2)).reshape(48, 2048)
-    gj = as_cols(last[0:240], 5)
-    gj_q = gj[:, :192].reshape(48, 3, 1, HDIM)
-    gj_kv = gj[:, 256:].reshape(48, 3, 2, HDIM)
-    grad_joint = jnp.concatenate([gj_q, gj_kv], axis=2).reshape(48, 576)
-    bj = (last[240:245] + last[248:253]).reshape(JW)
-    bj = jnp.concatenate([bj[:192].reshape(3, 1, HDIM), bj[256:].reshape(3, 2, HDIM)[:, 1:]], axis=1)
-    grad_joint_bias = bj.reshape(384)
+    grad_joint, grad_joint_bias = joint_gradient(core_word, last, swap_cores(last))
+    own = [v.reshape(48) for v in own]
 
     return (
         layer_output,
         grad_inputs,
         grad_joint,
-        grad_joint_bias,
-        grad_out,
+        grad_joint_bias.reshape(384),
+        grad_out.T,
         own[5],
         own[0],
         own[1],
         grad_up,
-        grad_up_bias,
+        grad_up_bias.reshape(768),
         grad_down,
         own[4],
         own[2],

time: 328 us -> 311 us (0.948)
  local copies, waits for them, and re-layouts: 38.7 us -> 19.5 us
  waiting for transfers between devices: 90.3 us -> 85.3 us
  starting transfers between devices: 75.3 us -> 79.9 us
    all_to_all x11, waiting for transfers between devices: 88.3 us -> 73 us  [exchange(): return lax.all_to_all(blocks, axis, 0, 0, tiled=True)]
    unnamed x52 -> x34, local copies, waits for them, and re-layouts: 16 us -> 4.75 us
    ppermute x6 -> x9, waiting for transfers between devices: 0.02 us -> 11 us  [around(): return lax.ppermute(v, axis, [(i, (i + shift) % 4) for i in range(4)])]
    ppermute x6 -> x9, starting transfers between devices: 6.02 us -> 11.9 us  [around(): return lax.ppermute(v, axis, [(i, (i + shift) % 4) for i in range(4)])]
    reshape x13 -> x0, local copies, waits for them, and re-layouts: 4.15 us -> none  [the longest x3 1.35 us: per_device(): jnp.transpose(v.reshape(n, 48, 128), (1, 0, 2)).reshape(48, n * 128)]
    pallas_call x9 -> x11, Pallas kernels: 82.5 us -> 85.7 us  [the longest x1 20.6 us: attend_back_first(): pl.pallas_call(back_first_kernel, grid=(BACK_STEPS,), out_shape=(pltpu.HB...]
    ppermute x3 -> x4, starting transfers between devices: 13.3 us -> 11.5 us  [swap_cores(): return lax.ppermute(v, 'dp', [(0, 1), (1, 0)])]
  transfers between devices with their start and end apart: 22 -> 25, of which waited for: 12 -> 15; matrix products, arithmetic and copies ran while one was open for 6% -> 6% of each run, Pallas kernels for 23% -> 22%
where the time goes in v4:
time: 311 us; the launch traced here: 309 us
  Pallas kernels  92.1 us (30%)
  waiting for transfers between devices  85.3 us (27%)
  starting transfers between devices  79.9 us (26%)
  local copies, waits for them, and re-layouts  19.5 us (6%)
  between operations  14.4 us (5%)
  blocking collectives  12.3 us (4%)
  other arithmetic  5.59 us (2%)
    all_to_all x11, waiting for transfers between devices, exchange(): return lax.all_to_all(blocks, axis, 0, 0, tiled=True)  73 us
    all_to_all x11, starting transfers between devices, exchange(): return lax.all_to_all(blocks, axis, 0, 0, tiled=True)  56.4 us
    pallas_call x1, Pallas kernels, attend_back_first(): pl.pallas_call(back_first_kernel, grid=(BACK_STEPS,), out_shape=(pltpu.HB...  20.6 us
    pallas_call x1, Pallas kernels, attend_back_second(): pl.pallas_call(back_second_kernel, grid=(BACK_STEPS,), out_shape=pltpu.HB...  19.6 us
    pallas_call x1, Pallas kernels, attend(): pl.pallas_call(attend_kernel, grid=(NCOL // FWD_C,), out_shape=(pltpu.HBM...  19.6 us
    pallas_call x1, Pallas kernels, tokenwise(): pl.pallas_call(tokenwise_kernel, out_shape=(pltpu.HBM((NROW, SENT, TOK),...  13.6 us
    all_gather x1, blocking collectives, per_device(): x4 = lax.all_gather(x_t.reshape(DIM, TOK), 'row', axis=0, tiled=False)  12.3 us
    ppermute x9, starting transfers between devices, around(): return lax.ppermute(v, axis, [(i, (i + shift) % 4) for i in range(4)])  11.9 us
  transfers between devices with their start and end apart: 25, of which 15 were waited for; matrix products, arithmetic and copies ran while one was open for 6% of the time, Pallas kernels for 22%

profile of v4, /device:TPU:1, one launch (start us, length us, event | category | flops | bytes accessed | tf_op | source)
XLA Modules:
  0.0 309.1 jit_solution(15266276401557437447)
XLA Ops:
  11.1 8.6 %all-to-all-start = ((bf16[16,48,128]{2,1,0:T(8,128)(2,1)}), bf16[16,48,128]{2,1,0:T(8,128)(2,1)S(1)}, u32[]{:S(2)}, u32[]{:S(2)}) async-start(bf16[16,48,128]{2,1,0:T(8,128)(2,1)} %bitcast_bitcast_fusion.1), calls=%async_computation | async-start | bytes 393216 | tf_op jit(solution)/shard_map/all_to_all | solution.py:820
  22.3 4.6 %all-to-all-done.x_ref = bf16[16,48,128]{2,1,0:T(8,128)(2,1)S(1)} async-done(((bf16[16,48,128]{2,1,0:T(8,128)(2,1)}), bf16[16,48,128]{2,1,0:T(8,128)(2,1)S(1)}, u32[]{:S(2)}, u32[]{:S(2)}) %all-to-all-start) | async-done | bytes 196640 | tf_op jit(solution)/shard_map/all_to_all | solution.py:820
  28.0 3.6 %all-to-all-start.1 = ((bf16[16,48,640]{2,1,0:T(8,128)(2,1)}), bf16[16,48,640]{2,1,0:T(8,128)(2,1)S(1)}, u32[]{:S(2)}, u32[]{:S(2)}) async-start(bf16[16,48,640]{2,1,0:T(8,128)(2,1)} %broadcast_in_dim.4), calls=%async_computation.1 | async-start | bytes 1966080 | tf_op jit(solution)/shard_map/all_to_all | solution.py:820
  32.0 12.3 %all_gather.9.x_ref = bf16[4,768,128]{2,1,0:T(8,128)(2,1)S(1)} all-gather(bf16[1,768,128]{2,1,0:T(8,128)(2,1)S(1)} %bitcast.100), channel_id=1, replica_groups=mesh['dp'=2,'row'=4,'z'=4,'y'=4] {'row'}, dimensions={0}, use_global_device_ids=true | all-gather | bytes 983040 | tf_op jit(solution)/shard_map/all_gather | solution.py:872
  46.4 2.5 project.1
  48.9 4.7 %all-to-all-start.2 = ((bf16[16,624,128]{2,1,0:T(8,128)(2,1)}), bf16[16,624,128]{2,1,0:T(8,128)(2,1)S(1)}, u32[]{:S(2)}, u32[]{:S(2)}) async-start(bf16[16,624,128]{2,1,0:T(8,128)(2,1)} %project.1), calls=%async_computation.2 | async-start | bytes 5111808 | tf_op jit(solution)/shard_map/all_to_all | solution.py:820
  57.6 28.9 %all-to-all-done.2.q_ref.kv_ref.cot_ref = bf16[16,624,128]{2,1,0:T(8,128)(2,1)S(1)} async-done(((bf16[16,624,128]{2,1,0:T(8,128)(2,1)}), bf16[16,624,128]{2,1,0:T(8,128)(2,1)S(1)}, u32[]{:S(2)}, u32[]{:S(2)}) %all-to-all-start.2) | async-done | bytes 2555936 | tf_op jit(solution)/shard_map/all_to_all | solution.py:820
  89.0 19.6 %attend.1 = (bf16[1664,144]{1,0:T(8,128)(2,1)}, f32[1664,64]{1,0:T(8,128)}, bf16[16,64,128]{2,1,0:T(8,128)(2,1)}) custom-call(bf16[16,624,128]{2,1,0:T(8,128)(2,1)S(1)} %all-to-all-done.2.q_ref.kv_ref.cot_ref, bf16[16,624,128]{2,1,0:T(8,128)(2,1)S(1)} %all-to-all-done.2.q_ref.kv_ref.cot_ref, s32[1664,1]{1,0:T(8,128)S(1)} %copy-done.4, s32[8,8,128]{2,1,0:T(8,128)S(1)} %bitcast.97), custom_call_target="tpu_custom_call" | custom-call | flops 20000000000 | bytes 40000000 | tf_op jit(solution)/shard_map/attend/pallas_call | solution.py:213
  108.6 6.9 %all-to-all-start.3 = ((bf16[16,64,128]{2,1,0:T(8,128)(2,1)}), bf16[16,64,128]{2,1,0:T(8,128)(2,1)S(1)}, u32[]{:S(2)}, u32[]{:S(2)}) async-start(bf16[16,64,128]{2,1,0:T(8,128)(2,1)} %get-tuple-element.68), calls=%async_computation.3 | async-start | bytes 524288 | tf_op jit(solution)/shard_map/all_to_all | solution.py:820
  115.5 7.6 %all-to-all-done.3.got_ref = bf16[16,64,128]{2,1,0:T(8,128)(2,1)S(1)} async-done(((bf16[16,64,128]{2,1,0:T(8,128)(2,1)}), bf16[16,64,128]{2,1,0:T(8,128)(2,1)S(1)}, u32[]{:S(2)}, u32[]{:S(2)}) %all-to-all-start.3) | async-done | bytes 262176 | tf_op jit(solution)/shard_map/all_to_all | solution.py:820
  124.1 4.6 %all-to-all-start.4 = ((bf16[4,224,128]{2,1,0:T(8,128)(2,1)}), bf16[4,224,128]{2,1,0:T(8,128)(2,1)}, u32[]{:S(2)}, u32[]{:S(2)}) async-start(bf16[4,224,128]{2,1,0:T(8,128)(2,1)} %to_row.1.att_ref), calls=%async_computation.4 | async-start | bytes 458752 | tf_op jit(solution)/shard_map/all_to_all | solution.py:820
  128.7 5.5 %all-to-all-done.4.att_ref = bf16[4,224,128]{2,1,0:T(8,128)(2,1)} async-done(((bf16[4,224,128]{2,1,0:T(8,128)(2,1)}), bf16[4,224,128]{2,1,0:T(8,128)(2,1)}, u32[]{:S(2)}, u32[]{:S(2)}) %all-to-all-start.4) | async-done | bytes 229408 | tf_op jit(solution)/shard_map/all_to_all | solution.py:820
  134.2 13.6 %tokenwise.1 = (bf16[4,3888,128]{2,1,0:T(8,128)(2,1)}, bf16[4,192,128]{2,1,0:T(8,128)(2,1)}, bf16[16,48,128]{2,1,0:T(8,128)(2,1)}, f32[768,128]{1,0:T(8,128)}) custom-call(s32[1]{0:T(128)} %bitcast.14.row_ref, bf16[4,224,128]{2,1,0:T(8,128)(2,1)} %all-to-all-done.4.att_ref, bf16[16,48,128]{2,1,0:T(8,128)(2,1)} %copy-done.10, ...), custom_call_target="tpu_custom_call" | custom-call | flops 15000000512 | bytes 30000000 | tf_op jit(solution)/shard_map/tokenwise/pallas_call | solution.py:562
  147.7 3.4 %all-to-all-start.5 = ((bf16[4,192,128]{2,1,0:T(8,128)(2,1)}), bf16[4,192,128]{2,1,0:T(8,128)(2,1)S(1)}, u32[]{:S(2)}, u32[]{:S(2)}) async-start(bf16[4,192,128]{2,1,0:T(8,128)(2,1)} %get-tuple-element.72), calls=%async_computation.5 | async-start | bytes 393216 | tf_op jit(solution)/shard_map/all_to_all | solution.py:820
  152.6 3.7 %all-to-all-done.5.got_ref = bf16[4,192,128]{2,1,0:T(8,128)(2,1)S(1)} async-done(((bf16[4,192,128]{2,1,0:T(8,128)(2,1)}), bf16[4,192,128]{2,1,0:T(8,128)(2,1)S(1)}, u32[]{:S(2)}, u32[]{:S(2)}) %all-to-all-start.5) | async-done | bytes 196640 | tf_op jit(solution)/shard_map/all_to_all | solution.py:820
  157.2 4.2 %all-to-all-start.6 = ((bf16[16,64,128]{2,1,0:T(8,128)(2,1)}), bf16[16,64,128]{2,1,0:T(8,128)(2,1)}, u32[]{:S(2)}, u32[]{:S(2)}) async-start(bf16[16,64,128]{2,1,0:T(8,128)(2,1)} %to_col.1), calls=%async_computation.6 | async-start | bytes 524288 | tf_op jit(solution)/shard_map/all_to_all | solution.py:820
  161.4 3.4 %slice_bitcast_fusion = (bf16[3888,128]{1,0:T(8,128)(2,1)}, bf16[3888,128]{1,0:T(8,128)(2,1)}, bf16[3888,128]{1,0:T(8,128)(2,1)}) fusion(bf16[4,3888,128]{2,1,0:T(8,128)(2,1)} %get-tuple-element.90.own_ref), kind=kLoop, calls=%fused_computation.2 | loop fusion | bytes 5971968 | tf_op jit(solution)/shard_map/squeeze | solution.py:912
  168.9 20.6 %attend_back_first.1 = (bf16[16,304,128]{2,1,0:T(8,128)(2,1)}, bf16[1664,80]{1,0:T(8,128)(2,1)}, bf16[128,1664]{1,0:T(8,128)(2,1)}, f32[1664,128]{1,0:T(8,128)}) custom-call(bf16[16,624,128]{2,1,0:T(8,128)(2,1)} %copy-done.1, bf16[16,64,128]{2,1,0:T(8,128)(2,1)} %all-to-all-done.6.do_ref, bf16[1664,144]{1,0:T(8,128)(2,1)} %get-tuple-element.67.qa_ref, ...), custom_call_target="tpu_custom_call" | custom-call | flops 17999998976 | bytes 36000000 | tf_op jit(solution)/shard_map/attend_back_first/pallas_call | solution.py:310
  189.5 5.2 %all-to-all-start.7 = ((bf16[16,304,128]{2,1,0:T(8,128)(2,1)}), bf16[16,304,128]{2,1,0:T(8,128)(2,1)}, u32[]{:S(2)}, u32[]{:S(2)}) async-start(bf16[16,304,128]{2,1,0:T(8,128)(2,1)} %get-tuple-element.81), calls=%async_computation.7 | async-start | bytes 2490368 | tf_op jit(solution)/shard_map/all_to_all | solution.py:820
  194.7 19.6 %attend_back_second.1 = bf16[16,320,128]{2,1,0:T(8,128)(2,1)} custom-call(bf16[1664,144]{1,0:T(8,128)(2,1)} %get-tuple-element.67.qa_ref, bf16[1664,80]{1,0:T(8,128)(2,1)} %get-tuple-element.77.doa_ref, bf16[128,1664]{1,0:T(8,128)(2,1)} %get-tuple-element.78.turned_ref, f32[1664,128]{1,0:T(8,128)} %get-tuple-element.79.acc_in, ...), custom_call_target="tpu_custom_call" | custom-call | flops 17999998976 | bytes 36000000 | tf_op jit(solution)/shard_map/attend_back_second/pallas_call | solution.py:343
  214.4 6.4 %weight_grads.1 = (bf16[16,384,128]{2,1,0:T(8,128)(2,1)}, bf16[16,384,128]{2,1,0:T(8,128)(2,1)}) custom-call(s32[1]{0:T(128)} %bitcast.core_ref, s32[1]{0:T(128)} %bitcast.14.row_ref, bf16[4,3888,128]{2,1,0:T(8,128)(2,1)} %get-tuple-element.90.own_ref, bf16[3888,128]{1,0:T(8,128)(2,1)} %collective-permute-done.got_1, ...), custom_call_target="tpu_custom_call" | custom-call | flops 1000000000 | bytes 2000000 | tf_op jit(solution)/shard_map/weight_grads/pallas_call | solution.py:664
  220.8 6.5 %collective-permute-start.4 = (bf16[16,384,128]{2,1,0:T(8,128)(2,1)}, bf16[16,384,128]{2,1,0:T(8,128)(2,1)}, u32[]{:S(2)}, u32[]{:S(2)}) collective-permute-start(bf16[16,384,128]{2,1,0:T(8,128)(2,1)} %get-tuple-element.95), channel_id=1, source_target_pairs={{0,64},{64,0},{1,65},{65,1},{2,66},{66,2},{3,67},{67,3},{4,68},{68... | collective-permute-start | bytes 4718600 | tf_op jit(solution)/shard_map/ppermute | solution.py:828
  227.3 6.9 %all-to-all-start.8 = ((bf16[16,320,128]{2,1,0:T(8,128)(2,1)}), bf16[16,320,128]{2,1,0:T(8,128)(2,1)S(1)}, u32[]{:S(2)}, u32[]{:S(2)}) async-start(bf16[16,320,128]{2,1,0:T(8,128)(2,1)} %attend_back_second.1), calls=%async_computation.8 | async-start | bytes 2621440 | tf_op jit(solution)/shard_map/all_to_all | solution.py:820
  239.0 2.4 collective-permute-start.6
  242.5 13.5 %all-to-all-done.8.second_ref = bf16[16,320,128]{2,1,0:T(8,128)(2,1)S(1)} async-done(((bf16[16,320,128]{2,1,0:T(8,128)(2,1)}), bf16[16,320,128]{2,1,0:T(8,128)(2,1)S(1)}, u32[]{:S(2)}, u32[]{:S(2)}) %all-to-all-start.8) | async-done | bytes 1310752 | tf_op jit(solution)/shard_map/all_to_all | solution.py:820
  256.0 5.3 %project_back.1 = (bf16[4,768,128]{2,1,0:T(8,128)(2,1)}, bf16[16,128,128]{2,1,0:T(8,128)(2,1)}, bf16[16,128,128]{2,1,0:T(8,128)(2,1)}, bf16[48,2048]{1,0:T(8,128)(2,1)}) custom-call(s32[1]{0:T(128)} %bitcast.core_ref, bf16[16,304,128]{2,1,0:T(8,128)(2,1)} %all-to-all-done.7.first_ref, bf16[16,320,128]{2,1,0:T(8,128)(2,1)S(1)} %all-to-all-done.8.second_ref, ...), custom_call_target="tpu_custom_call" | custom-call | flops 5000000000 | bytes 10000000 | tf_op jit(solution)/shard_map/project_back/pallas_call | solution.py:716
  261.3 4.0 %all-to-all-start.9 = ((bf16[4,768,128]{2,1,0:T(8,128)(2,1)}), bf16[4,768,128]{2,1,0:T(8,128)(2,1)S(1)}, u32[]{:S(2)}, u32[]{:S(2)}) async-start(bf16[4,768,128]{2,1,0:T(8,128)(2,1)} %get-tuple-element.89), calls=%async_computation.9 | async-start | bytes 1572864 | tf_op jit(solution)/shard_map/all_to_all | solution.py:820
  270.4 5.8 %all-to-all-done.9.din_ref = bf16[4,768,128]{2,1,0:T(8,128)(2,1)S(1)} async-done(((bf16[4,768,128]{2,1,0:T(8,128)(2,1)}), bf16[4,768,128]{2,1,0:T(8,128)(2,1)S(1)}, u32[]{:S(2)}, u32[]{:S(2)}) %all-to-all-start.9) | async-done | bytes 786464 | tf_op jit(solution)/shard_map/all_to_all | solution.py:820
  277.3 4.3 %all-to-all-start.10 = ((bf16[16,176,128]{2,1,0:T(8,128)(2,1)}), bf16[16,176,128]{2,1,0:T(8,128)(2,1)S(1)}, u32[]{:S(2)}, u32[]{:S(2)}) async-start(bf16[16,176,128]{2,1,0:T(8,128)(2,1)} %last_payload.1), calls=%async_computation.10 | async-start | bytes 1441792 | tf_op jit(solution)/shard_map/all_to_all | solution.py:820
  281.6 2.9 collective-permute-start.10
  285.9 7.5 %collective-permute-done.10 = bf16[384,128]{1,0:T(8,128)(2,1)S(1)} collective-permute-done((bf16[384,128]{1,0:T(8,128)(2,1)S(1)}, bf16[384,128]{1,0:T(8,128)(2,1)S(1)}, u32[]{:S(2)}, u32[]{:S(2)}) %collective-permute-start.10) | collective-permute-done | bytes 98336 | tf_op jit(solution)/shard_map/ppermute | solution.py:824
  295.1 3.0 collective-permute-start.12
  (104 shorter events, 43.3 us)
Async XLA Ops:
  7.2 15.0 %copy-start.13 = (f32[384]{0:T(512)S(1)}, f32[384]{0:T(512)}, u32[]{:S(2)}) copy-start(f32[384]{0:T(512)} %param.18) | copy-start | bytes 4612
  7.2 127.0 %all-gather.3.cloned.1.call-start = ((), (), s32[]{:S(2)}) async-start(), calls=%async_computation.11 | async-start | bytes 11096064 | tf_op jit(solution)/shard_map/all_gather | solution.py:885
  11.1 15.8 %all-to-all-start = ((bf16[16,48,128]{2,1,0:T(8,128)(2,1)}), bf16[16,48,128]{2,1,0:T(8,128)(2,1)S(1)}, u32[]{:S(2)}, u32[]{:S(2)}) async-start(bf16[16,48,128]{2,1,0:T(8,128)(2,1)} %bitcast_bitcast_fusion.1), calls=%async_computation | async-start | bytes 393216 | tf_op jit(solution)/shard_map/all_to_all | solution.py:820
  22.2 9.7 %copy-start.11 = (bf16[48,2048]{1,0:T(8,128)(2,1)S(1)}, bf16[48,2048]{1,0:T(8,128)(2,1)}, u32[]{:S(2)}) copy-start(bf16[48,2048]{1,0:T(8,128)(2,1)} %param.29) | copy-start | bytes 589828
  28.0 18.4 %all-to-all-start.1 = ((bf16[16,48,640]{2,1,0:T(8,128)(2,1)}), bf16[16,48,640]{2,1,0:T(8,128)(2,1)S(1)}, u32[]{:S(2)}, u32[]{:S(2)}) async-start(bf16[16,48,640]{2,1,0:T(8,128)(2,1)} %broadcast_in_dim.4), calls=%async_computation.1 | async-start | bytes 1966080 | tf_op jit(solution)/shard_map/all_to_all | solution.py:820
  48.9 37.6 %all-to-all-start.2 = ((bf16[16,624,128]{2,1,0:T(8,128)(2,1)}), bf16[16,624,128]{2,1,0:T(8,128)(2,1)S(1)}, u32[]{:S(2)}, u32[]{:S(2)}) async-start(bf16[16,624,128]{2,1,0:T(8,128)(2,1)} %project.1), calls=%async_computation.2 | async-start | bytes 5111808 | tf_op jit(solution)/shard_map/all_to_all | solution.py:820
  86.5 22.1 %copy-start.1 = (bf16[16,624,128]{2,1,0:T(8,128)(2,1)}, bf16[16,624,128]{2,1,0:T(8,128)(2,1)S(1)}, u32[]{:S(2)}) copy-start(bf16[16,624,128]{2,1,0:T(8,128)(2,1)S(1)} %all-to-all-done.2.q_ref.kv_ref.cot_ref) | copy-start | bytes 7667716
  89.0 26.5 %copy-start.12 = (f32[768]{0:T(1024)S(1)}, f32[768]{0:T(1024)}, u32[]{:S(2)}) copy-start(f32[768]{0:T(1024)} %param.24) | copy-start | bytes 9220
  108.6 14.6 %all-to-all-start.3 = ((bf16[16,64,128]{2,1,0:T(8,128)(2,1)}), bf16[16,64,128]{2,1,0:T(8,128)(2,1)S(1)}, u32[]{:S(2)}, u32[]{:S(2)}) async-start(bf16[16,64,128]{2,1,0:T(8,128)(2,1)} %get-tuple-element.68), calls=%async_computation.3 | async-start | bytes 524288 | tf_op jit(solution)/shard_map/all_to_all | solution.py:820
  124.1 10.1 %all-to-all-start.4 = ((bf16[4,224,128]{2,1,0:T(8,128)(2,1)}), bf16[4,224,128]{2,1,0:T(8,128)(2,1)}, u32[]{:S(2)}, u32[]{:S(2)}) async-start(bf16[4,224,128]{2,1,0:T(8,128)(2,1)} %to_row.1.att_ref), calls=%async_computation.4 | async-start | bytes 458752 | tf_op jit(solution)/shard_map/all_to_all | solution.py:820
  147.7 8.5 %all-to-all-start.5 = ((bf16[4,192,128]{2,1,0:T(8,128)(2,1)}), bf16[4,192,128]{2,1,0:T(8,128)(2,1)S(1)}, u32[]{:S(2)}, u32[]{:S(2)}) async-start(bf16[4,192,128]{2,1,0:T(8,128)(2,1)} %get-tuple-element.72), calls=%async_computation.5 | async-start | bytes 393216 | tf_op jit(solution)/shard_map/all_to_all | solution.py:820
  157.2 11.8 %all-to-all-start.6 = ((bf16[16,64,128]{2,1,0:T(8,128)(2,1)}), bf16[16,64,128]{2,1,0:T(8,128)(2,1)}, u32[]{:S(2)}, u32[]{:S(2)}) async-start(bf16[16,64,128]{2,1,0:T(8,128)(2,1)} %to_col.1), calls=%async_computation.6 | async-start | bytes 524288 | tf_op jit(solution)/shard_map/all_to_all | solution.py:820
  164.8 49.5 %collective-permute-start = (bf16[3888,128]{1,0:T(8,128)(2,1)}, bf16[3888,128]{1,0:T(8,128)(2,1)}, u32[]{:S(2)}, u32[]{:S(2)}) collective-permute-start(bf16[3888,128]{1,0:T(8,128)(2,1)} %get-tuple-element.116), channel_id=1, source_target_pairs={{0,16},{16,32},{32,48},{48,0},{1,17},{17,33},{33,49},{49,1},{2,18}... | collective-permute-start | bytes 2985992 | tf_op jit(solution)/shard_map/ppermute | solution.py:824
  165.1 49.2 %collective-permute-start.1 = (bf16[3888,128]{1,0:T(8,128)(2,1)}, bf16[3888,128]{1,0:T(8,128)(2,1)}, u32[]{:S(2)}, u32[]{:S(2)}) collective-permute-start(bf16[3888,128]{1,0:T(8,128)(2,1)} %get-tuple-element.115), channel_id=1, source_target_pairs={{0,32},{16,48},{32,0},{48,16},{1,33},{17,49},{33,1},{49,17},{2,34}... | collective-permute-start | bytes 2985992 | tf_op jit(solution)/shard_map/ppermute | solution.py:824
  166.9 47.4 %collective-permute-start.2 = (bf16[3888,128]{1,0:T(8,128)(2,1)}, bf16[3888,128]{1,0:T(8,128)(2,1)}, u32[]{:S(2)}, u32[]{:S(2)}) collective-permute-start(bf16[3888,128]{1,0:T(8,128)(2,1)} %get-tuple-element.114), channel_id=1, source_target_pairs={{0,48},{16,0},{32,16},{48,32},{1,49},{17,1},{33,17},{49,33},{2,50}... | collective-permute-start | bytes 2985992 | tf_op jit(solution)/shard_map/ppermute | solution.py:824
  189.5 24.8 %all-to-all-start.7 = ((bf16[16,304,128]{2,1,0:T(8,128)(2,1)}), bf16[16,304,128]{2,1,0:T(8,128)(2,1)}, u32[]{:S(2)}, u32[]{:S(2)}) async-start(bf16[16,304,128]{2,1,0:T(8,128)(2,1)} %get-tuple-element.81), calls=%async_computation.7 | async-start | bytes 2490368 | tf_op jit(solution)/shard_map/all_to_all | solution.py:820
  220.8 13.4 %collective-permute-start.4 = (bf16[16,384,128]{2,1,0:T(8,128)(2,1)}, bf16[16,384,128]{2,1,0:T(8,128)(2,1)}, u32[]{:S(2)}, u32[]{:S(2)}) collective-permute-start(bf16[16,384,128]{2,1,0:T(8,128)(2,1)} %get-tuple-element.95), channel_id=1, source_target_pairs={{0,64},{64,0},{1,65},{65,1},{2,66},{66,2},{3,67},{67,3},{4,68},{68... | collective-permute-start | bytes 4718600 | tf_op jit(solution)/shard_map/ppermute | solution.py:828
  227.3 28.7 %all-to-all-start.8 = ((bf16[16,320,128]{2,1,0:T(8,128)(2,1)}), bf16[16,320,128]{2,1,0:T(8,128)(2,1)S(1)}, u32[]{:S(2)}, u32[]{:S(2)}) async-start(bf16[16,320,128]{2,1,0:T(8,128)(2,1)} %attend_back_second.1), calls=%async_computation.8 | async-start | bytes 2621440 | tf_op jit(solution)/shard_map/all_to_all | solution.py:820
  236.5 19.5 %copy-start.3 = (bf16[16,48,640]{2,1,0:T(8,128)(2,1)S(1)}, bf16[16,48,640]{2,1,0:T(8,128)(2,1)}, u32[]{:S(2)}) copy-start(bf16[16,48,640]{2,1,0:T(8,128)(2,1)} %copy-done.2) | copy-start | bytes 2949124
  237.6 29.3 %collective-permute-start.5 = (bf16[4,384,128]{2,1,0:T(8,128)(2,1)}, bf16[4,384,128]{2,1,0:T(8,128)(2,1)}, u32[]{:S(2)}, u32[]{:S(2)}) collective-permute-start(bf16[4,384,128]{2,1,0:T(8,128)(2,1)} %get-tuple-element.117), channel_id=1, source_target_pairs={{0,4},{4,8},{8,12},{12,0},{1,5},{5,9},{9,13},{13,1},{2,6},{6,10},{... | collective-permute-start | bytes 1179656 | tf_op jit(solution)/shard_map/ppermute | solution.py:824
  239.0 29.8 %collective-permute-start.6 = (bf16[4,384,128]{2,1,0:T(8,128)(2,1)}, bf16[4,384,128]{2,1,0:T(8,128)(2,1)}, u32[]{:S(2)}, u32[]{:S(2)}) collective-permute-start(bf16[4,384,128]{2,1,0:T(8,128)(2,1)} %get-tuple-element.119), channel_id=1, source_target_pairs={{0,8},{4,12},{8,0},{12,4},{1,9},{5,13},{9,1},{13,5},{2,10},{6,14},... | collective-permute-start | bytes 1179656 | tf_op jit(solution)/shard_map/ppermute | solution.py:824
  241.4 27.4 %collective-permute-start.7 = (bf16[4,384,128]{2,1,0:T(8,128)(2,1)}, bf16[4,384,128]{2,1,0:T(8,128)(2,1)}, u32[]{:S(2)}, u32[]{:S(2)}) collective-permute-start(bf16[4,384,128]{2,1,0:T(8,128)(2,1)} %get-tuple-element.118), channel_id=1, source_target_pairs={{0,12},{4,0},{8,4},{12,8},{1,13},{5,1},{9,5},{13,9},{2,14},{6,2},{... | collective-permute-start | bytes 1179656 | tf_op jit(solution)/shard_map/ppermute | solution.py:824
  261.3 14.8 %all-to-all-start.9 = ((bf16[4,768,128]{2,1,0:T(8,128)(2,1)}), bf16[4,768,128]{2,1,0:T(8,128)(2,1)S(1)}, u32[]{:S(2)}, u32[]{:S(2)}) async-start(bf16[4,768,128]{2,1,0:T(8,128)(2,1)} %get-tuple-element.89), calls=%async_computation.9 | async-start | bytes 1572864 | tf_op jit(solution)/shard_map/all_to_all | solution.py:820
  265.3 10.8 %copy-start.7 = (bf16[16,128,128]{2,1,0:T(8,128)(2,1)S(1)}, bf16[16,128,128]{2,1,0:T(8,128)(2,1)}, u32[]{:S(2)}) copy-start(bf16[16,128,128]{2,1,0:T(8,128)(2,1)} %get-tuple-element.87.mine_ref) | copy-start | bytes 1572868
  265.3 10.8 %copy-start.8 = (f32[768,128]{1,0:T(8,128)S(1)}, f32[768,128]{1,0:T(8,128)}, u32[]{:S(2)}) copy-start(f32[768,128]{1,0:T(8,128)} %get-tuple-element.97.dh1_ref) | copy-start | bytes 1179652
  265.3 10.8 %collective-permute-start.3 = (bf16[16,128,128]{2,1,0:T(8,128)(2,1)S(1)}, bf16[16,128,128]{2,1,0:T(8,128)(2,1)S(1)}, u32[]{:S(2)}, u32[]{:S(2)}) collective-permute-start(bf16[16,128,128]{2,1,0:T(8,128)(2,1)S(1)} %copy-done.14), channel_id=1, source_target_pairs={{0,64},{64,0},{1,65},{65,1},{2,66},{66,2},{3,67},{67,3},{4,68},{68... | collective-permute-start | bytes 1572872 | tf_op jit(solution)/shard_map/ppermute | solution.py:828
  277.3 22.8 %all-to-all-start.10 = ((bf16[16,176,128]{2,1,0:T(8,128)(2,1)}), bf16[16,176,128]{2,1,0:T(8,128)(2,1)S(1)}, u32[]{:S(2)}, u32[]{:S(2)}) async-start(bf16[16,176,128]{2,1,0:T(8,128)(2,1)} %last_payload.1), calls=%async_computation.10 | async-start | bytes 1441792 | tf_op jit(solution)/shard_map/all_to_all | solution.py:820
  281.6 11.8 %collective-permute-start.10 = (bf16[384,128]{1,0:T(8,128)(2,1)S(1)}, bf16[384,128]{1,0:T(8,128)(2,1)S(1)}, u32[]{:S(2)}, u32[]{:S(2)}) collective-permute-start(bf16[384,128]{1,0:T(8,128)(2,1)S(1)} %get-tuple-element.102), channel_id=1, source_target_pairs={{0,2},{1,3},{2,0},{3,1},{4,6},{5,7},{6,4},{7,5},{8,10},{9,11},{10,... | collective-permute-start | bytes 294920 | tf_op jit(solution)/shard_map/ppermute | solution.py:824
  284.5 9.6 %collective-permute-start.11 = (bf16[384,128]{1,0:T(8,128)(2,1)S(1)}, bf16[384,128]{1,0:T(8,128)(2,1)S(1)}, u32[]{:S(2)}, u32[]{:S(2)}) collective-permute-start(bf16[384,128]{1,0:T(8,128)(2,1)S(1)} %get-tuple-element.103), channel_id=1, source_target_pairs={{0,3},{1,0},{2,1},{3,2},{4,7},{5,4},{6,5},{7,6},{8,11},{9,8},{10,9... | collective-permute-start | bytes 294920 | tf_op jit(solution)/shard_map/ppermute | solution.py:824
  285.4 9.7 %collective-permute-start.9 = (bf16[384,128]{1,0:T(8,128)(2,1)S(1)}, bf16[384,128]{1,0:T(8,128)(2,1)S(1)}, u32[]{:S(2)}, u32[]{:S(2)}) collective-permute-start(bf16[384,128]{1,0:T(8,128)(2,1)S(1)} %get-tuple-element.101), channel_id=1, source_target_pairs={{0,1},{1,2},{2,3},{3,0},{4,5},{5,6},{6,7},{7,4},{8,9},{9,10},{10,1... | collective-permute-start | bytes 294920 | tf_op jit(solution)/shard_map/ppermute | solution.py:824
  295.1 4.0 %collective-permute-start.12 = (f32[384,128]{1,0:T(8,128)S(1)}, f32[384,128]{1,0:T(8,128)S(1)}, u32[]{:S(2)}, u32[]{:S(2)}) collective-permute-start(f32[384,128]{1,0:T(8,128)S(1)} %convert_add_fusion.1.wide_ref), channel_id=1, source_target_pairs={{0,64},{64,0},{1,65},{65,1},{2,66},{66,2},{3,67},{67,3},{4,68},{68... | collective-permute-start | bytes 589832 | tf_op jit(solution)/shard_map/ppermute | solution.py:828
  300.1 1.4 collective-permute-start.8
  (8 other events, 20.4 us)
Sparse Core Ops, SparseCore 0:
  11.5 100.1 all-gather.2
